TPU v7x, 32 devices: a whole 2x2x4 slice. The times are simulated.
32 devices in a mesh: rep: 4 (over y, x), shard: 8 (over z, core).
Axes of the slice: x: 2, y: 2, z: 4, core: 2. Of those that a mesh axis runs over, the one named last changes fastest.
Arguments:
- hidden: bfloat16 [32, 256, 2048], P(('rep', 'shard')), may hold values from -6 to 6
- segments: int32 [32, 256], P(('rep', 'shard')), may hold values from 0 to 1, as said below
- cotangent: bfloat16 [32, 256, 2048], P(('rep', 'shard')), may hold values from -6 to 6
- in_master: float32 [2048, 8192], P('shard'), may hold values from -0.125 to 0.125
- in_first: float32 [2048, 8192], P('shard'), may hold values from -32 to 32
- in_second: float32 [2048, 8192], P('shard'), may hold values from 155.648 to 622.592
- x_master: float32 [4096, 160], P('shard'), may hold values from -0.09375 to 0.09375
- x_first: float32 [4096, 160], P('shard'), may hold values from -32 to 32
- x_second: float32 [4096, 160], P('shard'), may hold values from 155.648 to 622.592
- dt_master: float32 [4096, 128], P('shard'), may hold values from -0.5 to 0.5
- dt_first: float32 [4096, 128], P('shard'), may hold values from -1.75 to 1.75
- dt_second: float32 [4096, 128], P('shard'), may hold values from 0.0622592 to 0.24576
- out_master: float32 [4096, 2048], P('shard'), may hold values from -0.25 to 0.25
- out_first: float32 [4096, 2048], P('shard'), may hold values from -20 to 20
- out_second: float32 [4096, 2048], P('shard'), may hold values from 56.5248 to 221.184
- chan_master: float32 [4096, 23], P('shard'), may hold values from -7.5 to 2.8, as said below
- chan_first: float32 [4096, 23], P('shard'), may hold values from -16 to 16
- chan_second: float32 [4096, 23], P('shard'), may hold values from 39.3216 to 155.648
- gain_master: float32 [2048], P('shard'), may hold values from 0.5 to 1.5
- gain_first: float32 [2048], P('shard'), may hold values from -64 to 64
- gain_second: float32 [2048], P('shard'), may hold values from 622.592 to 2457.6
Outputs:
- layer_output: bfloat16 [32, 256, 2048], P(('rep', 'shard'))
- input_grad: bfloat16 [32, 256, 2048], P(('rep', 'shard'))
- in_first_new: float32 [2048, 8192], P('shard')
- in_second_new: float32 [2048, 8192], P('shard')
- in_master_new: float32 [2048, 8192], P('shard')
- x_first_new: float32 [4096, 160], P('shard')
- x_second_new: float32 [4096, 160], P('shard')
- x_master_new: float32 [4096, 160], P('shard')
- dt_first_new: float32 [4096, 128], P('shard')
- dt_second_new: float32 [4096, 128], P('shard')
- dt_master_new: float32 [4096, 128], P('shard')
- out_first_new: float32 [4096, 2048], P('shard')
- out_second_new: float32 [4096, 2048], P('shard')
- out_master_new: float32 [4096, 2048], P('shard')
- chan_first_new: float32 [4096, 23], P('shard')
- chan_second_new: float32 [4096, 23], P('shard')
- chan_master_new: float32 [4096, 23], P('shard')
- gain_first_new: float32 [2048], P('shard')
- gain_second_new: float32 [2048], P('shard')
- gain_master_new: float32 [2048], P('shard')
Inputs may be any that keep to these rules, and one draw needn't show every extreme that they name: `segments`: each sequence holds two documents: ids are 0 on its first L tokens and 1 on the rest, with 96 <= L <= 160. `chan_master`: column layout as in the meaning; the logarithms of the rates lie in 0 to 2.8, the step-size biases in -7.5 to -2.5, the skip gains in 0.5 to 1.5.
All inputs are finite; a program needn't handle non-finite values.
Results may differ from a plain program's by a relative error of at most 0.0055.
The roundings to bfloat16 on the way count: a program that leaves them out, or rounds other values in their place, can miss the bound.
Values may be sent and summed in bfloat16 or wider, within the bound.
A program may use at most 384 MiB of HBM per device.

v0:
```python
import jax
import jax.numpy as jnp
from jax import lax
from jax.sharding import PartitionSpec as P

NSTATE = 16
RANK = 128
KCONV = 4
BLOCK = 16
GROUP = 8
ADAM_STEP = 10


norm_eps = 1e-05
beta_first = 0.9
beta_second = 0.95
adam_eps = 1e-08
weight_decay = 0.1
learn_rates = (0.044, 0.03, 0.18, 0.09, 1.0, 0.6)
with_decay = (True, True, True, True, False, False)


def chain_pair(earlier, later):
    return (earlier[0] * later[0], later[0] * earlier[1] + later[1])


def silu_slope(values):
    sigma = jax.nn.sigmoid(values)
    return sigma * (1.0 + values * (1.0 - sigma))


def to_steps(values):
    blocks = values.shape[0] // BLOCK
    return jnp.swapaxes(values.reshape((blocks, BLOCK) + values.shape[1:]), 0, 1)


def from_steps(values):
    swapped = jnp.swapaxes(values, 0, 1)
    return swapped.reshape((-1,) + swapped.shape[2:])


def to_groups(values):
    groups = values.shape[0] // (BLOCK * GROUP)
    return jnp.swapaxes(values.reshape((groups, GROUP, BLOCK) + values.shape[1:]), 1, 2)


def from_groups(values):
    swapped = jnp.swapaxes(values, 1, 2)
    return swapped.reshape((-1,) + swapped.shape[3:])


def decay_of(step_size, carry_mask, rates):
    return jnp.exp(step_size[..., None] * rates) * carry_mask[..., None, None]


def drive_of(step_size, conv_out, state_in):
    return (step_size * conv_out)[..., None] * state_in[..., None, :]


def block_totals(step_size, carry_mask, rates):
    blocks = step_size.shape[0] // BLOCK
    sums = jnp.sum(step_size.reshape(blocks, BLOCK, -1), axis=1)
    kept = jnp.prod(carry_mask.reshape(blocks, BLOCK), axis=1)
    return jnp.exp(sums[:, :, None] * rates) * kept[:, None, None]


def scan_forward(step_size, conv_out, state_in, state_out, carry_mask, rates):
    blocks = step_size.shape[0] // BLOCK
    size_steps = to_steps(step_size)
    conv_steps = to_steps(conv_out)
    in_steps = to_steps(state_in)
    out_steps = to_steps(state_out)
    mask_steps = to_steps(carry_mask)

    def local_step(state, inputs_now):
        size_now, conv_now, in_now, mask_now = inputs_now
        state = decay_of(size_now, mask_now, rates) * state + drive_of(size_now, conv_now, in_now)
        return (state, None)

    zero_state = jnp.zeros((blocks, rates.shape[0], rates.shape[1]), jnp.float32)
    block_ends, _ = lax.scan(local_step, zero_state, (size_steps, conv_steps, in_steps, mask_steps))
    totals = block_totals(step_size, carry_mask, rates)
    _, reached = lax.associative_scan(chain_pair, (totals, block_ends), axis=0)
    starts = jnp.concatenate([jnp.zeros_like(reached[:1]), reached[:-1]], axis=0)

    def full_step(state, inputs_now):
        size_now, conv_now, in_now, out_now, mask_now = inputs_now
        state = decay_of(size_now, mask_now, rates) * state + drive_of(size_now, conv_now, in_now)
        return (state, jnp.sum(state * out_now[:, None, :], axis=2))

    _, outputs = lax.scan(
        full_step, starts, (size_steps, conv_steps, in_steps, out_steps, mask_steps)
    )
    return (from_steps(outputs), starts)


def scan_backward(step_size, conv_out, state_in, state_out, carry_mask, rates, starts, grad_y):
    blocks = step_size.shape[0] // BLOCK
    inner_width, state_width = rates.shape

    def local_back(flow_back, inputs_now):
        size_now, conv_now, in_now, out_now, mask_now, gy_now = inputs_now
        gradient = gy_now[:, :, None] * out_now[:, None, :] + flow_back
        return (decay_of(size_now, mask_now, rates) * gradient, None)

    zero_state = jnp.zeros((blocks, inner_width, state_width), jnp.float32)
    stepped = tuple(
        (to_steps(v) for v in (step_size, conv_out, state_in, state_out, carry_mask, grad_y))
    )
    block_out, _ = lax.scan(local_back, zero_state, stepped, reverse=True)
    totals = block_totals(step_size, carry_mask, rates)
    _, reached = lax.associative_scan(chain_pair, (totals[::-1], block_out[::-1]), axis=0)
    reached = reached[::-1]
    flows = jnp.concatenate([reached[1:], jnp.zeros_like(reached[:1])], axis=0)
    group_count = blocks // GROUP
    start_groups = starts.reshape(group_count, GROUP, inner_width, state_width)
    flow_groups = flows.reshape(group_count, GROUP, inner_width, state_width)
    grouped = tuple(
        (to_groups(v) for v in (step_size, conv_out, state_in, state_out, carry_mask, grad_y))
    )

    def group_back(grad_rates, group_item):
        start, flow_in, size_g, conv_g, in_g, out_g, mask_g, gy_g = group_item

        def forward_step(state, inputs_now):
            size_now, conv_now, in_now, mask_now = inputs_now
            updated = decay_of(size_now, mask_now, rates) * state + drive_of(
                size_now, conv_now, in_now
            )
            return (updated, state)

        _, priors = lax.scan(forward_step, start, (size_g, conv_g, in_g, mask_g))

        def reverse_step(carry, inputs_now):
            flow_back, grad_acc = carry
            size_now, conv_now, in_now, out_now, mask_now, gy_now, prior = inputs_now
            decay = decay_of(size_now, mask_now, rates)
            state = decay * prior + drive_of(size_now, conv_now, in_now)
            gradient = gy_now[:, :, None] * out_now[:, None, :] + flow_back
            through = gradient * prior * decay
            along = jnp.sum(gradient * in_now[:, None, :], axis=2)
            grad_size = jnp.sum(through * rates, axis=2) + conv_now * along
            grad_conv = size_now * along
            grad_in = jnp.sum(gradient * (size_now * conv_now)[:, :, None], axis=1)
            grad_outs = jnp.sum(state * gy_now[:, :, None], axis=1)
            grad_acc = grad_acc + jnp.sum(through * size_now[:, :, None], axis=0)
            return ((decay * gradient, grad_acc), (grad_size, grad_conv, grad_in, grad_outs))

        (_, grad_rates), pieces = lax.scan(
            reverse_step,
            (flow_in, grad_rates),
            (size_g, conv_g, in_g, out_g, mask_g, gy_g, priors),
            reverse=True,
        )
        return (grad_rates, pieces)

    grad_rates, pieces = lax.scan(
        group_back,
        jnp.zeros((inner_width, state_width), jnp.float32),
        (start_groups, flow_groups) + grouped,
    )
    grad_size, grad_conv, grad_in, grad_outs = (from_groups(v) for v in pieces)
    return (grad_size, grad_conv, grad_in, grad_outs, grad_rates)


def doc_masks(doc_ids):
    length = doc_ids.shape[0]
    return [
        jnp.pad(doc_ids, (KCONV - 1 - k, 0), constant_values=-1)[:length] == doc_ids
        for k in range(KCONV)
    ]


def adam_step(master, first, second, gradient, rate, decays):
    first_new = beta_first * first + (1.0 - beta_first) * gradient
    second_new = beta_second * second + (1.0 - beta_second) * gradient * gradient
    update = (
        first_new
        / (1.0 - beta_first**ADAM_STEP)
        / (jnp.sqrt(second_new / (1.0 - beta_second**ADAM_STEP)) + adam_eps)
    )
    if decays:
        update = update + weight_decay * master
    return (first_new, second_new, master - rate * update)


def shards(
    hidden,
    segments,
    cotangent,
    in_master,
    in_first,
    in_second,
    x_master,
    x_first,
    x_second,
    dt_master,
    dt_first,
    dt_second,
    out_master,
    out_first,
    out_second,
    chan_master,
    chan_first,
    chan_second,
    gain_master,
    gain_first,
    gain_second,
):
    in_copy = in_master.astype(jnp.bfloat16)
    x_copy = x_master.astype(jnp.bfloat16)
    dt_copy = dt_master.astype(jnp.bfloat16)
    out_copy = out_master.astype(jnp.bfloat16)
    chan_copy = chan_master.astype(jnp.bfloat16)
    gain_copy = gain_master.astype(jnp.bfloat16)
    w_in, w_x, w_dt, w_out, channel, gain = (
        lax.all_gather(in_copy, "shard", axis=0, tiled=True),
        lax.all_gather(x_copy, "shard", axis=0, tiled=True),
        lax.all_gather(dt_copy, "shard", axis=0, tiled=True),
        lax.all_gather(out_copy, "shard", axis=0, tiled=True),
        lax.all_gather(chan_copy, "shard", axis=0, tiled=True),
        lax.all_gather(gain_copy, "shard", axis=0, tiled=True),
    )
    inner_width = w_out.shape[0]
    residual = hidden[0].astype(jnp.float32)
    doc_ids = segments[0]
    upstream = cotangent[0]
    channel_f = channel.astype(jnp.float32)
    gain_f = gain.astype(jnp.float32)
    taps = channel_f[:, :KCONV]
    a_log = channel_f[:, KCONV : KCONV + NSTATE]
    conv_bias = channel_f[:, KCONV + NSTATE]
    dt_bias = channel_f[:, KCONV + NSTATE + 1]
    skip = channel_f[:, KCONV + NSTATE + 2]
    rates = -jnp.exp(a_log)
    length = residual.shape[0]
    inv_rms = lax.rsqrt(jnp.mean(residual * residual, axis=1, keepdims=True) + norm_eps)
    normed = (residual * inv_rms * gain_f).astype(jnp.bfloat16)
    both = jnp.dot(normed, w_in, preferred_element_type=jnp.float32)
    inner_part = both[:, :inner_width]
    gate_part = both[:, inner_width:]
    masks = doc_masks(doc_ids)
    carry_mask = masks[KCONV - 2].astype(jnp.float32)
    conv_pre = jnp.zeros_like(inner_part) + conv_bias
    moved_list = []
    for k in range(KCONV):
        offset = KCONV - 1 - k
        moved = jnp.where(
            masks[k][:, None], jnp.pad(inner_part, ((offset, 0), (0, 0)))[:length], 0.0
        )
        moved_list.append(moved)
        conv_pre = conv_pre + taps[:, k] * moved
    conv_out = jax.nn.silu(conv_pre).astype(jnp.bfloat16)
    conv_f = conv_out.astype(jnp.float32)
    projected = jnp.dot(conv_out, w_x, preferred_element_type=jnp.float32)
    dt_in = projected[:, :RANK].astype(jnp.bfloat16)
    state_in = projected[:, RANK : RANK + NSTATE]
    state_out = projected[:, RANK + NSTATE :]
    dt_pre = (
        lax.dot_general(dt_in, w_dt, (((1,), (1,)), ((), ())), preferred_element_type=jnp.float32)
        + dt_bias
    )
    step_size = jax.nn.softplus(dt_pre)
    scanned, starts = scan_forward(step_size, conv_f, state_in, state_out, carry_mask, rates)
    mixer_y = scanned + skip * conv_f
    gate_act = jax.nn.silu(gate_part)
    mixed = (mixer_y * gate_act).astype(jnp.bfloat16)
    layer_output = (residual + jnp.dot(mixed, w_out, preferred_element_type=jnp.float32)).astype(
        jnp.bfloat16
    )
    back_in, back_x, back_dt, back_out = (
        lax.all_gather(in_copy, "shard", axis=0, tiled=True),
        lax.all_gather(x_copy, "shard", axis=0, tiled=True),
        lax.all_gather(dt_copy, "shard", axis=0, tiled=True),
        lax.all_gather(out_copy, "shard", axis=0, tiled=True),
    )
    part = mixed
    out_grad = lax.psum_scatter(
        lax.dot_general(
            part, upstream, (((0,), (0,)), ((), ())), preferred_element_type=jnp.float32
        ),
        "shard",
        scatter_dimension=0,
        tiled=True,
    )
    grad_mixed = lax.dot_general(
        upstream, back_out, (((1,), (1,)), ((), ())), preferred_element_type=jnp.float32
    )
    grad_y = grad_mixed * gate_act
    grad_gate = grad_mixed * mixer_y * silu_slope(gate_part)
    grad_skip = jnp.sum(grad_y * conv_f, axis=0)
    grad_size, grad_conv, grad_state_in, grad_state_out, grad_rates = scan_backward(
        step_size, conv_f, state_in, state_out, carry_mask, rates, starts, grad_y
    )
    grad_conv = grad_conv + skip * grad_y
    grad_dtpre = grad_size * jax.nn.sigmoid(dt_pre)
    grad_dtbias = jnp.sum(grad_dtpre, axis=0)
    grad_dtlow = grad_dtpre.astype(jnp.bfloat16)
    grad_dt = lax.dot_general(
        grad_dtlow, dt_in, (((0,), (0,)), ((), ())), preferred_element_type=jnp.float32
    )
    grad_dtin = jnp.dot(grad_dtlow, back_dt, preferred_element_type=jnp.float32)
    grad_proj = jnp.concatenate([grad_dtin, grad_state_in, grad_state_out], axis=1).astype(
        jnp.bfloat16
    )
    grad_x = lax.dot_general(
        conv_out, grad_proj, (((0,), (0,)), ((), ())), preferred_element_type=jnp.float32
    )
    grad_conv = grad_conv + lax.dot_general(
        grad_proj, back_x, (((1,), (1,)), ((), ())), preferred_element_type=jnp.float32
    )
    grad_pre = grad_conv * silu_slope(conv_pre)
    grad_inner = jnp.zeros_like(grad_pre)
    tap_grads = []
    for k in range(KCONV):
        offset = KCONV - 1 - k
        masked = jnp.where(masks[k][:, None], grad_pre, 0.0)
        tap_grads.append(jnp.sum(grad_pre * moved_list[k], axis=0))
        grad_inner = grad_inner + taps[:, k] * jnp.pad(masked, ((0, offset), (0, 0)))[offset:]
    grad_convbias = jnp.sum(grad_pre, axis=0)
    grad_both = jnp.concatenate([grad_inner, grad_gate], axis=1).astype(jnp.bfloat16)
    grad_normed = lax.dot_general(
        grad_both, back_in, (((1,), (1,)), ((), ())), preferred_element_type=jnp.float32
    )
    grad_gain = jnp.sum(grad_normed * residual * inv_rms, axis=0)
    grad_scaled = grad_normed * gain_f
    grad_resid = (
        inv_rms * grad_scaled
        - residual * inv_rms**3 * jnp.mean(grad_scaled * residual, axis=1, keepdims=True)
        + upstream.astype(jnp.float32)
    )
    input_grad = grad_resid.astype(jnp.bfloat16)
    grad_chan = jnp.concatenate(
        [
            jnp.stack(tap_grads, axis=1),
            grad_rates * rates,
            grad_convbias[:, None],
            grad_dtbias[:, None],
            grad_skip[:, None],
        ],
        axis=1,
    )
    x_grad, dt_grad, chan_grad, gain_grad = (
        lax.psum_scatter(grad_x, "shard", scatter_dimension=0, tiled=True),
        lax.psum_scatter(grad_dt, "shard", scatter_dimension=0, tiled=True),
        lax.psum_scatter(grad_chan, "shard", scatter_dimension=0, tiled=True),
        lax.psum_scatter(grad_gain, "shard", scatter_dimension=0, tiled=True),
    )
    part = normed
    in_grad = lax.psum_scatter(
        lax.dot_general(
            part, grad_both, (((0,), (0,)), ((), ())), preferred_element_type=jnp.float32
        ),
        "shard",
        scatter_dimension=0,
        tiled=True,
    )
    summed = lax.psum((in_grad, x_grad, dt_grad, out_grad, chan_grad, gain_grad), "rep")
    in_first_new, in_second_new, in_master_new = adam_step(
        in_master, in_first, in_second, summed[0], learn_rates[0], with_decay[0]
    )
    x_first_new, x_second_new, x_master_new = adam_step(
        x_master, x_first, x_second, summed[1], learn_rates[1], with_decay[1]
    )
    dt_first_new, dt_second_new, dt_master_new = adam_step(
        dt_master, dt_first, dt_second, summed[2], learn_rates[2], with_decay[2]
    )
    out_first_new, out_second_new, out_master_new = adam_step(
        out_master, out_first, out_second, summed[3], learn_rates[3], with_decay[3]
    )
    chan_first_new, chan_second_new, chan_master_new = adam_step(
        chan_master, chan_first, chan_second, summed[4], learn_rates[4], with_decay[4]
    )
    gain_first_new, gain_second_new, gain_master_new = adam_step(
        gain_master, gain_first, gain_second, summed[5], learn_rates[5], with_decay[5]
    )
    return (
        layer_output[None],
        input_grad[None],
        in_first_new,
        in_second_new,
        in_master_new,
        x_first_new,
        x_second_new,
        x_master_new,
        dt_first_new,
        dt_second_new,
        dt_master_new,
        out_first_new,
        out_second_new,
        out_master_new,
        chan_first_new,
        chan_second_new,
        chan_master_new,
        gain_first_new,
        gain_second_new,
        gain_master_new,
    )


def solution(mesh):
    placed = (
        P(("rep", "shard"), None, None),
        P(("rep", "shard"), None),
        P(("rep", "shard"), None, None),
        P("shard", None),
        P("shard", None),
        P("shard", None),
        P("shard", None),
        P("shard", None),
        P("shard", None),
        P("shard", None),
        P("shard", None),
        P("shard", None),
        P("shard", None),
        P("shard", None),
        P("shard", None),
        P("shard", None),
        P("shard", None),
        P("shard", None),
        P("shard"),
        P("shard"),
        P("shard"),
    )
    return jax.shard_map(
        shards,
        mesh=mesh,
        in_specs=placed,
        out_specs=(
            P(("rep", "shard"), None, None),
            P(("rep", "shard"), None, None),
            P("shard", None),
            P("shard", None),
            P("shard", None),
            P("shard", None),
            P("shard", None),
            P("shard", None),
            P("shard", None),
            P("shard", None),
            P("shard", None),
            P("shard", None),
            P("shard", None),
            P("shard", None),
            P("shard", None),
            P("shard", None),
            P("shard", None),
            P("shard"),
            P("shard"),
            P("shard"),
        ),
        check_vma=False,
    )
```

profile of v0, /device:TPU:0, one launch (start us, length us, event | category | flops | bytes accessed | tf_op | source)
XLA Modules:
  0.0 2826.7 jit_solution(7558487480887177387)
XLA Ops:
  18.9 15.9 all_gather.22
  36.8 21.3 all-gather
  60.2 244.9 %all-gather.6.cloned.1.call-done = bf16[2048,8192]{1,0:T(8,128)(2,1)} async-done(((bf16[256,8192]{1,0:T(8,128)(2,1)}), bf16[2048,8192]{1,0:T(8,128)(2,1)}) %all-gather.6.cloned.1.call-update) | async-done | bytes 33554448 | tf_op jit(solution)/shard_map/all_gather | solution.py:217
  305.1 20.3 fusion.58
  330.2 126.3 %all-gather.12.cloned.1.call-done = bf16[4096,2048]{1,0:T(8,128)(2,1)} async-done(((bf16[512,2048]{1,0:T(8,128)(2,1)}), bf16[4096,2048]{1,0:T(8,128)(2,1)}) %all-gather.12.cloned.1.call-update) | async-done | bytes 16777232 | tf_op jit(solution)/shard_map/all_gather | solution.py:220
  456.6 25.7 multiply_reduce_fusion.5
  487.1 17.0 all-gather.10.cloned.1.call-done
  519.6 8.3 copy_bitcast_fusion.4
  527.9 101.8 %while.145 = (s32[]{:T(128)}, f32[16,4096,16]{1,2,0:T(8,128)}, f32[16,16,4096]{2,1,0:T(8,128)}, f32[4096,16]{0,1:T(8,128)S(1)}, f32[16,16]{1,0:T(8,128)S(1)}, /*...) while((s32[]{:T(128)}, f32[16,4096,16]{1,2,0:T(8,128)}, ...), condition=%wide.region_9.10_spmd.clone, body=%wide.region_8.9_spmd.clone.sunk | while | flops 6291460 | bytes 10227015 | solution.py:110
  634.8 118.0 %while.144 = (s32[]{:T(128)}, f32[16,4096,16]{1,2,0:T(8,128)}, f32[16,16,4096]{2,1,0:T(8,128)}, f32[4096,16]{0,1:T(8,128)S(1)}, f32[16,16]{1,0:T(8,128)S(1)}, /*...) while((s32[]{:T(128)}, f32[16,4096,16]{1,2,0:T(8,128)}, ...), condition=%wide.region_2.3_spmd.clone, body=%wide.region_1.2_spmd.clone.sunk | while | flops 6356995 | bytes 10489143 | solution.py:81
  817.0 7.9 pad.239
  871.8 11.6 copy_bitcast_fusion
  883.5 439.9 %while.143 = (s32[]{:T(128)}, f32[4096,16]{0,1:T(8,128)S(1)}, f32[2,16,8,4096]{3,2,1,0:T(8,128)}, f32[2,16,8,4096]{3,2,1,0:T(8,128)}, bf16[2,16,8,16]{3,2,1,0:T(...) while((s32[]{:T(128)}, f32[4096,16]{0,1:T(8,128)S(1)}, ...), condition=%wide.region_20.21_spmd, body=%wide.region_10.20_spmd.sunk | while | flops 13205255 | bytes 86828016 | solution.py:157
  890.5 75.0 %while.146 = (s32[]{:T(128)}, f32[8,4096,16]{1,2,0:T(8,128)S(1)}, f32[16,8,4096,16]{2,3,1,0:T(8,128)}, f32[16,8,4096]{2,1,0:T(8,128)}, f32[4096,16]{0,1:T(8,128)...) while((s32[]{:T(128)}, f32[8,4096,16]{1,2,0:T(8,128)S(1)}, ...), condition=%wide.region_12.12_spmd, body=%wide.region_11.11_spmd.sunk | while | flops 2654210 | bytes 9570509 | solution.py:132
  972.8 126.1 %while.147 = (s32[]{:T(128)}, f32[8,4096,16]{1,2,0:T(8,128)S(1)}, f32[4096,16]{0,1:T(8,128)S(1)}, f32[16,8,4096]{2,1,0:T(8,128)}, f32[16,8,4096]{2,1,0:T(8,128)}...) while((s32[]{:T(128)}, f32[8,4096,16]{1,2,0:T(8,128)S(1)}, ...), condition=%wide.region_19.19_spmd, body=%wide.region_13.18_spmd.sunk | while | flops 10551043 | bytes 9973545 | solution.py:149
  1110.2 75.0 %while.146 = (s32[]{:T(128)}, f32[8,4096,16]{1,2,0:T(8,128)S(1)}, f32[16,8,4096,16]{2,3,1,0:T(8,128)}, f32[16,8,4096]{2,1,0:T(8,128)}, f32[4096,16]{0,1:T(8,128)...) while((s32[]{:T(128)}, f32[8,4096,16]{1,2,0:T(8,128)S(1)}, ...), condition=%wide.region_12.12_spmd, body=%wide.region_11.11_spmd.sunk | while | flops 2654210 | bytes 9570509 | solution.py:132
  1192.6 126.1 %while.147 = (s32[]{:T(128)}, f32[8,4096,16]{1,2,0:T(8,128)S(1)}, f32[4096,16]{0,1:T(8,128)S(1)}, f32[16,8,4096]{2,1,0:T(8,128)}, f32[16,8,4096]{2,1,0:T(8,128)}...) while((s32[]{:T(128)}, f32[8,4096,16]{1,2,0:T(8,128)S(1)}, ...), condition=%wide.region_19.19_spmd, body=%wide.region_13.18_spmd.sunk | while | flops 10551043 | bytes 9973545 | solution.py:149
  1331.4 142.5 %while.140 = (s32[]{:T(128)}, f32[16,4096,16]{1,2,0:T(8,128)}, f32[16,16,4096]{2,1,0:T(8,128)}, f32[16,16,4096]{2,1,0:T(8,128)}, f32[4096,16]{0,1:T(8,128)S(1)},...) while((s32[]{:T(128)}, f32[16,4096,16]{1,2,0:T(8,128)}, ...), condition=%wide.region_7.8_spmd, body=%wide.region_5.7_spmd.sunk | while | flops 7340034 | bytes 11279157 | solution.py:91
  1481.0 6.8 copy.86
  1498.8 15.1 fusion.81
  1513.9 14.9 fusion.46
  1529.6 8.6 fusion.24
  1538.2 26.0 fusion.29
  1570.5 284.4 %reduce-scatter.12.cloned.1.call-done = f32[512,2048]{1,0:T(8,128)} async-done(((f32[4096,2048]{1,0:T(8,128)}), f32[512,2048]{1,0:T(8,128)}) %reduce-scatter.12.cloned.1.call-update) | async-done | bytes 4194320 | tf_op jit(solution)/shard_map/reduce_scatter | solution.py:278
  1854.9 641.0 %reduce-scatter.6.cloned.1.call-done = f32[256,8192]{1,0:T(8,128)} async-done(((f32[2048,8192]{1,0:T(8,128)}), f32[256,8192]{1,0:T(8,128)}) %reduce-scatter.6.cloned.1.call-update) | async-done | bytes 8388624 | tf_op jit(solution)/shard_map/reduce_scatter | solution.py:350
  2497.8 17.2 fusion.42
  2515.1 14.1 all-reduce.27
  2532.8 10.4 fusion.32
  2543.3 19.7 all-reduce.28
  2564.3 219.5 %all-reduce.32.cloned.1.call-done = (f32[256,8192]{1,0:T(8,128)}, f32[512,160]{0,1:T(8,128)}, f32[512,128]{1,0:T(8,128)}, f32[512,2048]{1,0:T(8,128)}) async-done(((f32[256,8192]{1,0:T(8,128)}, f32[512,160]{0,1:T(8,128)}, f32[512,128]{1,0:T(8,128)}, f32[512,2048]{1,0:T(8,128)}), (f32[256,8192]{1,0:T(8,128)}, f32[512,160]{0,1:T(8,128)}, f32[512,128]{1,0:T(8,128)}, ...) | async-done | bytes 13172752 | tf_op jit(solution)/shard_map/psum | solution.py:358
  2783.8 22.2 multiply_subtract_fusion
  2806.1 11.0 multiply_subtract_fusion.1
  (1075 shorter events, 995.6 us)
Async XLA Ops:
  7.2 297.9 %all-gather.6.cloned.1.call-start = ((), (), s32[]{:S(2)}) async-start(), calls=%async_computation.5 | async-start | bytes 37748736 | tf_op jit(solution)/shard_map/all_gather | solution.py:217
  13.3 22.2 copy-start.74
  13.3 22.6 copy-start.16
  13.3 443.3 %all-gather.12.cloned.1.call-start = ((), (), s32[]{:S(2)}) async-start(), calls=%async_computation.8 | async-start | bytes 18874368 | tf_op jit(solution)/shard_map/all_gather | solution.py:220
  17.3 467.6 %all-gather.8.cloned.1.call-start = ((), (), s32[]{:S(2)}) async-start(), calls=%async_computation.6 | async-start | bytes 1474560 | tf_op jit(solution)/shard_map/all_gather | solution.py:218
  18.1 486.0 %all-gather.10.cloned.1.call-start = ((), (), s32[]{:S(2)}) async-start(), calls=%async_computation.7 | async-start | bytes 1179648 | tf_op jit(solution)/shard_map/all_gather | solution.py:219
  18.8 1551.7 %reduce-scatter.10.cloned.1.call-start = ((), (), s32[]{:S(2)}) async-start(), calls=%async_computation.11 | async-start | bytes 2359296 | tf_op jit(solution)/shard_map/reduce_scatter | solution.py:345
  35.4 421.1 %copy-start.60 = (f32[4096,1]{0,1:T(1,128)}, f32[4096,1]{0,1:T(1,128)S(1)}, u32[]{:S(2)}) copy-start(f32[4096,1]{0,1:T(1,128)S(1)} %get-tuple-element.1330) | copy-start | bytes 49156
  35.4 421.1 %copy-start.62 = (f32[4096,1]{0,1:T(1,128)}, f32[4096,1]{0,1:T(1,128)S(1)}, u32[]{:S(2)}) copy-start(f32[4096,1]{0,1:T(1,128)S(1)} %get-tuple-element.1331) | copy-start | bytes 49156
  35.4 421.1 %copy-start.64 = (f32[4096,1]{0,1:T(1,128)}, f32[4096,1]{0,1:T(1,128)S(1)}, u32[]{:S(2)}) copy-start(f32[4096,1]{0,1:T(1,128)S(1)} %get-tuple-element.1332) | copy-start | bytes 49156
  35.4 421.1 %copy-start.66 = (f32[4096,1]{0,1:T(1,128)}, f32[4096,1]{0,1:T(1,128)S(1)}, u32[]{:S(2)}) copy-start(f32[4096,1]{0,1:T(1,128)S(1)} %get-tuple-element.1333) | copy-start | bytes 49156
  35.5 289.9 %copy-start.31 = (f32[4096,23]{0,1:T(8,128)}, f32[4096,23]{0,1:T(8,128)S(1)}, u32[]{:S(2)}) copy-start(f32[4096,23]{0,1:T(8,128)S(1)} %convert_element_type.77) | copy-start | bytes 1130500
  35.6 421.0 %copy-start.81 = (pred[256]{0:T(512)(128)(4,1)}, pred[256]{0:T(512)(128)(4,1)S(1)}, u32[]{:S(2)}) copy-start(pred[256]{0:T(512)(128)(4,1)S(1)} %get-tuple-element.1338) | copy-start | bytes 772
  35.6 421.0 %copy-start.83 = (pred[256]{0:T(512)(128)(4,1)}, pred[256]{0:T(512)(128)(4,1)S(1)}, u32[]{:S(2)}) copy-start(pred[256]{0:T(512)(128)(4,1)S(1)} %get-tuple-element.1339) | copy-start | bytes 772
  35.6 421.0 %copy-start.85 = (pred[256]{0:T(512)(128)(4,1)}, pred[256]{0:T(512)(128)(4,1)S(1)}, u32[]{:S(2)}) copy-start(pred[256]{0:T(512)(128)(4,1)S(1)} %get-tuple-element.1340) | copy-start | bytes 772
  36.8 288.6 %copy-start.57 = (f32[256]{0:T(256)}, f32[256]{0:T(256)S(1)}, u32[]{:S(2)}) copy-start(f32[256]{0:T(256)S(1)} %get-tuple-element.1337) | copy-start | bytes 3076
  58.1 267.3 %copy-start.41 = (f32[8,1,256]{2,1,0:T(1,128)}, f32[8,1,256]{2,1,0:T(1,128)S(1)}, u32[]{:S(2)}) copy-start(f32[8,1,256]{2,1,0:T(1,128)S(1)} %convert_element_type.94) | copy-start | bytes 24580
  325.4 131.2 %copy-start.28 = (bf16[1,256,2048]{2,1,0:T(8,128)(2,1)S(1)}, bf16[1,256,2048]{2,1,0:T(8,128)(2,1)}, u32[]{:S(2)}) copy-start(bf16[1,256,2048]{2,1,0:T(8,128)(2,1)} %param.35) | copy-start | bytes 3145732
  487.1 21.3 copy-start.43
  487.1 147.4 %copy-start.56 = (f32[256,16]{0,1:T(8,128)}, f32[256,16]{0,1:T(8,128)S(1)}, u32[]{:S(2)}) copy-start(f32[256,16]{0,1:T(8,128)S(1)} %get-tuple-element.1335) | copy-start | bytes 49156
  1331.4 239.1 %reduce-scatter.8.cloned.1.call-start = ((), (), s32[]{:S(2)}) async-start(), calls=%async_computation.10 | async-start | bytes 2949120 | tf_op jit(solution)/shard_map/reduce_scatter | solution.py:344
  1490.7 364.2 %reduce-scatter.12.cloned.1.call-start = ((), (), s32[]{:S(2)}) async-start(), calls=%async_computation.12 | async-start | bytes 37748736 | tf_op jit(solution)/shard_map/reduce_scatter | solution.py:278
  1528.9 967.0 %reduce-scatter.6.cloned.1.call-start = ((), (), s32[]{:S(2)}) async-start(), calls=%async_computation.9 | async-start | bytes 75497472 | tf_op jit(solution)/shard_map/reduce_scatter | solution.py:350
  1564.3 978.9 %reduce-scatter.14.cloned.1.call-start = ((), (), s32[]{:S(2)}) async-start(), calls=%async_computation.13 | async-start | bytes 442368 | tf_op jit(solution)/shard_map/reduce_scatter | solution.py:346
  1570.4 1213.4 %all-reduce.32.cloned.1.call-start = ((), (), s32[]{:S(2)}) async-start(), calls=%async_computation.14 | async-start | bytes 26345472 | tf_op jit(solution)/shard_map/psum | solution.py:358
  2497.8 31.4 %copy-start.76 = (f32[256]{0:T(256)S(1)}, f32[256]{0:T(256)}, u32[]{:S(2)}) copy-start(f32[256]{0:T(256)} %get-tuple-element.1336) | copy-start | bytes 3076
  2532.8 30.2 %copy-start.78 = (f32[256]{0:T(256)S(1)}, f32[256]{0:T(256)}, u32[]{:S(2)}) copy-start(f32[256]{0:T(256)} %param.51) | copy-start | bytes 3076
  2532.8 30.2 %copy-start.79 = (f32[256]{0:T(256)S(1)}, f32[256]{0:T(256)}, u32[]{:S(2)}) copy-start(f32[256]{0:T(256)} %param.53) | copy-start | bytes 3076
  2532.8 30.2 %copy-start.80 = (f32[256]{0:T(256)S(1)}, f32[256]{0:T(256)}, u32[]{:S(2)}) copy-start(f32[256]{0:T(256)} %param.52) | copy-start | bytes 3076
  2532.8 30.8 %copy-start.55 = (f32[512,23]{0,1:T(8,128)S(1)}, f32[512,23]{0,1:T(8,128)}, u32[]{:S(2)}) copy-start(f32[512,23]{0,1:T(8,128)} %param.48) | copy-start | bytes 141316
  2532.8 30.8 %copy-start.71 = (f32[512,23]{0,1:T(8,128)S(1)}, f32[512,23]{0,1:T(8,128)}, u32[]{:S(2)}) copy-start(f32[512,23]{0,1:T(8,128)} %param.50) | copy-start | bytes 141316
  2532.8 30.8 %copy-start.72 = (f32[512,23]{0,1:T(8,128)S(1)}, f32[512,23]{0,1:T(8,128)}, u32[]{:S(2)}) copy-start(f32[512,23]{0,1:T(8,128)} %param.49) | copy-start | bytes 141316
  (68 other events, 421.8 us)
Sparse Core Ops, SparseCore 0:
  13.3 291.7 all-gather.5
  307.3 149.2 all-gather.11
  458.8 21.6 all-gather.7
  482.5 21.5 all-gather.9
  1331.5 35.3 reduce-scatter.9
  1490.8 37.0 reduce-scatter.7
  1530.3 324.5 reduce-scatter.11
  1857.4 638.4 reduce-scatter.5
  2498.8 29.0 reduce-scatter.13
  2532.2 251.5 all-reduce.31
where the time goes:
time: 2840 us; the launch traced here: 2830 us
  waiting for transfers between devices  1530 us (54%)
  other arithmetic  690 us (24%)
  local copies, waits for them, and re-layouts  370 us (13%)
  matrix products  141 us (5%)
  blocking collectives  71 us (2%)
    reduce_scatter x1, waiting for transfers between devices, shards(): lax.psum_scatter(lax.dot_general(part, grad_both, (((0,), (0,)), ((), ())...  641 us
    reduce_scatter x1, waiting for transfers between devices, shards(): lax.psum_scatter(lax.dot_general(part, upstream, (((0,), (0,)), ((), ()))...  284 us
    all_gather x1, waiting for transfers between devices, shards(): lax.all_gather(in_copy, 'shard', axis=0, tiled=True)  245 us
    psum x1, waiting for transfers between devices, shards(): lax.psum((in_grad, x_grad, dt_grad, out_grad, chan_grad, gain_grad), 'rep')  220 us
    reduce_sum x32, other arithmetic, reverse_step(): grad_size = jnp.sum(through * rates, axis=2) + conv_now * along  129 us
    all_gather x1, waiting for transfers between devices, shards(): lax.all_gather(out_copy, 'shard', axis=0, tiled=True)  126 us
    add x16, other arithmetic, local_step(): decay_of(size_now, mask_now, rates) * state  84.7 us
    mul x16, other arithmetic, local_back(): return (decay_of(size_now, mask_now, rates) * gradient, None)  84 us
  transfers between devices with their start and end apart: 10, of which 6 were waited for; matrix products, arithmetic and copies ran while one was open for 12% of the time, Pallas kernels for 0%

commit v1 on v0

v1 whole, which is shorter than its diff:
```python
import functools

import jax
import jax.numpy as jnp
from jax import lax
from jax.experimental import pallas as pl
from jax.experimental.pallas import tpu as pltpu
from jax.sharding import PartitionSpec as P

NSTATE = 16
RANK = 128
KCONV = 4
ADAM_STEP = 10
CHUNK = 32
LANES = 128
SUBS = 8
CUT = 1e30
LOG2E = 1.4426950408889634

norm_eps = 1e-05
beta_first = 0.9
beta_second = 0.95
adam_eps = 1e-08
weight_decay = 0.1
learn_rates = (0.044, 0.03, 0.18, 0.09, 1.0, 0.6)
with_decay = (True, True, True, True, False, False)

bf16 = jnp.bfloat16
f32 = jnp.float32


def silu_slope(values):
    sigma = jax.nn.sigmoid(values)
    return sigma * (1.0 + values * (1.0 - sigma))


def dot(a, b, dims):
    return lax.dot_general(a, b, (dims, ((), ())), preferred_element_type=f32)


def expand_inputs(bc_ref, bx, sb):
    def one(n, carry):
        v = bc_ref[0, n, pl.ds(sb * SUBS, SUBS), :]
        for t in range(CHUNK):
            bx[t, n] = jnp.broadcast_to(v[:, t : t + 1], (SUBS, LANES))
        return carry

    lax.fori_loop(0, 2 * NSTATE, one, 0)


def spread(scratch, q, values):
    for g in range(scratch.shape[0]):
        scratch[g, pl.ds(q * CHUNK, CHUNK), :] = values[:, g * LANES : (g + 1) * LANES]


def collect(ref, q, scratch):
    for g in range(scratch.shape[0]):
        ref[q, :, pl.ds(g * LANES, LANES)] = scratch[g, pl.ds(q * CHUNK, CHUNK), :]


def scan_fwd_kernel(step_ref, cut_ref, conv_ref, bc_ref, rate_ref, y_ref, starts_ref, state, bx, stepm, drive, ys):
    seqs, _, width = step_ref.shape

    @pl.when(pl.program_id(0) == 0)
    def _():
        state[...] = jnp.zeros_like(state)

    starts_ref[0] = state[...]
    for q in range(seqs):
        step = step_ref[q]
        spread(stepm, q, step + cut_ref[q])
        spread(drive, q, step * conv_ref[q].astype(f32))
    for sb in range(seqs // SUBS):
        expand_inputs(bc_ref, bx, sb)
        sub = pl.ds(sb * SUBS, SUBS)

        def group(g, carry):
            lanes = pl.ds(pl.multiple_of(g * LANES, LANES), LANES)
            rates = [rate_ref[n, :, lanes] for n in range(NSTATE)]

            def token(t, st):
                rows = pl.ds(sb * SUBS * CHUNK + t, SUBS, stride=CHUNK)
                sm = stepm[g, rows, :]
                dx = drive[g, rows, :]
                y = None
                out = []
                for n in range(NSTATE):
                    dec = jnp.exp2(sm * rates[n])
                    s_n = dec * st[n] + dx * bx[t, n]
                    out.append(s_n)
                    part = s_n * bx[t, NSTATE + n]
                    y = part if y is None else y + part
                ys[g, rows, :] = y
                return tuple(out)

            st = tuple(state[n, sub, lanes] for n in range(NSTATE))
            st = lax.fori_loop(0, CHUNK, token, st)
            for n in range(NSTATE):
                state[n, sub, lanes] = st[n]
            return carry

        lax.fori_loop(0, width // LANES, group, 0)
    for q in range(seqs):
        collect(y_ref, q, ys)


def scan_bwd_kernel(
    step_ref, cut_ref, conv_ref, bc_ref, rate_ref, starts_ref, gy_ref,
    gstep_ref, gconv_ref, gbc_ref, grate_ref,
    flow, bx, stepm, step2, conv2, gy2, gs2, gc2, dec_s, pri_s, acc,
):
    seqs, _, width = step_ref.shape

    @pl.when(pl.program_id(0) == 0)
    def _():
        flow[...] = jnp.zeros_like(flow)
        grate_ref[...] = jnp.zeros_like(grate_ref)

    for q in range(seqs):
        step = step_ref[q]
        spread(step2, q, step)
        spread(stepm, q, step + cut_ref[q])
        spread(conv2, q, conv_ref[q].astype(f32))
        spread(gy2, q, gy_ref[q])
    for sb in range(seqs // SUBS):
        expand_inputs(bc_ref, bx, sb)
        sub = pl.ds(sb * SUBS, SUBS)
        acc[...] = jnp.zeros_like(acc)

        def group(g, carry):
            lanes = pl.ds(pl.multiple_of(g * LANES, LANES), LANES)

            def token_f(t, st):
                rows = pl.ds(sb * SUBS * CHUNK + t, SUBS, stride=CHUNK)
                sm = stepm[g, rows, :]
                dx = step2[g, rows, :] * conv2[g, rows, :]
                out = []
                for n in range(NSTATE):
                    dec = jnp.exp2(sm * (rate_ref[n, :, lanes] * LOG2E))
                    dec_s[t, n] = dec
                    pri_s[t, n] = st[n]
                    out.append(dec * st[n] + dx * bx[t, n])
                return tuple(out)

            st = tuple(starts_ref[0, n, sub, lanes] for n in range(NSTATE))
            st = lax.fori_loop(0, CHUNK, token_f, st)
            for n in range(NSTATE):
                pri_s[CHUNK, n] = st[n]

            def token_b(i, carried):
                t = CHUNK - 1 - i
                fl, ga = carried
                rows = pl.ds(sb * SUBS * CHUNK + t, SUBS, stride=CHUNK)
                size = step2[g, rows, :]
                conv = conv2[g, rows, :]
                gy = gy2[g, rows, :]
                dx = size * conv
                along = None
                gsz = None
                nfl, nga = [], []
                for n in range(NSTATE):
                    grad = gy * bx[t, NSTATE + n] + fl[n]
                    dg = dec_s[t, n] * grad
                    th = dg * pri_s[t, n]
                    a = grad * bx[t, n]
                    b = th * rate_ref[n, :, lanes]
                    along = a if along is None else along + a
                    gsz = b if gsz is None else gsz + b
                    acc[t, n] += grad * dx
                    acc[t, NSTATE + n] += pri_s[t + 1, n] * gy
                    nfl.append(dg)
                    nga.append(ga[n] + th * size)
                gs2[g, rows, :] = gsz + conv * along
                gc2[g, rows, :] = size * along
                return (tuple(nfl), tuple(nga))

            fl = tuple(flow[n, sub, lanes] for n in range(NSTATE))
            ga = tuple(grate_ref[n, :, lanes] for n in range(NSTATE))
            fl, ga = lax.fori_loop(0, CHUNK, token_b, (fl, ga))
            for n in range(NSTATE):
                flow[n, sub, lanes] = fl[n]
                grate_ref[n, :, lanes] = ga[n]
            return carry

        lax.fori_loop(0, width // LANES, group, 0)

        def reduce_n(n, carry):
            column = lax.broadcasted_iota(jnp.int32, (SUBS, CHUNK), 1)
            out = jnp.zeros((SUBS, CHUNK), f32)
            for t in range(CHUNK):
                total = jnp.sum(acc[t, n], axis=1, keepdims=True)
                out = jnp.where(column == t, total, out)
            gbc_ref[0, n, sub, :] = out
            return carry

        lax.fori_loop(0, 2 * NSTATE, reduce_n, 0)
    for q in range(seqs):
        collect(gstep_ref, q, gs2)
        collect(gconv_ref, q, gc2)


def scan_specs(seqs, length, width, chunk_of):
    tokens = pl.BlockSpec((seqs, CHUNK, width), lambda i: (0, chunk_of(i), 0))
    cuts = pl.BlockSpec((seqs, CHUNK, 1), lambda i: (0, chunk_of(i), 0))
    bcs = pl.BlockSpec((1, 2 * NSTATE, seqs, CHUNK), lambda i: (chunk_of(i), 0, 0, 0))
    rates = pl.BlockSpec((NSTATE, SUBS, width), lambda i: (0, 0, 0))
    starts = pl.BlockSpec((1, NSTATE, seqs, width), lambda i: (chunk_of(i), 0, 0, 0))
    return tokens, cuts, bcs, rates, starts


def scan_forward(step, cut, conv, bc, rates):
    seqs, length, width = step.shape
    chunks = length // CHUNK
    tokens, cuts, bcs, rate_spec, starts = scan_specs(seqs, length, width, lambda i: i)
    return pl.pallas_call(
        scan_fwd_kernel,
        grid=(chunks,),
        in_specs=[tokens, cuts, tokens, bcs, rate_spec],
        out_specs=[tokens, starts],
        out_shape=[
            jax.ShapeDtypeStruct(step.shape, f32),
            jax.ShapeDtypeStruct((chunks, NSTATE, seqs, width), f32),
        ],
        scratch_shapes=[
            pltpu.VMEM((NSTATE, seqs, width), f32),
            pltpu.VMEM((CHUNK, 2 * NSTATE, SUBS, LANES), f32),
            pltpu.VMEM((width // LANES, seqs * CHUNK, LANES), f32),
            pltpu.VMEM((width // LANES, seqs * CHUNK, LANES), f32),
            pltpu.VMEM((width // LANES, seqs * CHUNK, LANES), f32),
        ],
        compiler_params=pltpu.CompilerParams(vmem_limit_bytes=50 * 2**20),
        cost_estimate=pl.CostEstimate(
            flops=8 * step.size * NSTATE, bytes_accessed=12 * step.size, transcendentals=step.size * NSTATE
        ),
        name="scan_forward",
    )(step, cut, conv, bc, rates * LOG2E)


def scan_backward(step, cut, conv, bc, rates, starts, grad_y):
    seqs, length, width = step.shape
    chunks = length // CHUNK
    tokens, cuts, bcs, rate_spec, start_spec = scan_specs(seqs, length, width, lambda i: chunks - 1 - i)
    tall = pltpu.VMEM((width // LANES, seqs * CHUNK, LANES), f32)
    return pl.pallas_call(
        scan_bwd_kernel,
        grid=(chunks,),
        in_specs=[tokens, cuts, tokens, bcs, rate_spec, start_spec, tokens],
        out_specs=[tokens, tokens, bcs, rate_spec],
        out_shape=[
            jax.ShapeDtypeStruct(step.shape, f32),
            jax.ShapeDtypeStruct(step.shape, f32),
            jax.ShapeDtypeStruct(bc.shape, f32),
            jax.ShapeDtypeStruct((NSTATE, SUBS, width), f32),
        ],
        scratch_shapes=[
            pltpu.VMEM((NSTATE, seqs, width), f32),
            pltpu.VMEM((CHUNK, 2 * NSTATE, SUBS, LANES), f32),
            tall, tall, tall, tall, tall, tall,
            pltpu.VMEM((CHUNK, NSTATE, SUBS, LANES), f32),
            pltpu.VMEM((CHUNK + 1, NSTATE, SUBS, LANES), f32),
            pltpu.VMEM((CHUNK, 2 * NSTATE, SUBS, LANES), f32),
        ],
        compiler_params=pltpu.CompilerParams(vmem_limit_bytes=56 * 2**20),
        cost_estimate=pl.CostEstimate(
            flops=24 * step.size * NSTATE, bytes_accessed=24 * step.size, transcendentals=step.size * NSTATE
        ),
        name="scan_backward",
    )(step, cut, conv, bc, rates, starts, grad_y)


class Links:
    def __init__(self, reps, shard_size):
        self.reps, self.shard_size = reps, shard_size
        self.planes = shard_size // 2
        self.r = lax.axis_index("rep")
        shard = lax.axis_index("shard")
        self.z, self.c = shard // 2, shard % 2

    def rep(self, value, k):
        return lax.ppermute(value, "rep", [(i, i ^ k) for i in range(self.reps)])

    def core(self, value):
        return lax.ppermute(value, "shard", [(i, i ^ 1) for i in range(self.shard_size)])

    def up(self, value, k):
        n = self.shard_size
        return lax.ppermute(value, "shard", [(i, (i + 2 * k) % n) for i in range(n)])

    def gather_rep(self, value):
        if self.reps != 4:
            return [value] + [self.rep(value, k) for k in range(1, self.reps)]
        half = value.shape[0] // 2
        one, two = self.rep(value, 1), self.rep(value, 2)
        three = jnp.concatenate([self.rep(two[:half], 1), self.rep(one[half:], 2)], axis=0)
        return [value, one, two, three]

    def gather_plane(self, value):
        near = jnp.stack(self.gather_rep(value))
        return jnp.concatenate([near, self.core(near)], axis=0)

    def scatter_plane(self, partial, wire):
        reps = self.reps
        pair = partial[:reps].astype(f32) + self.core(partial[reps:].astype(wire)).astype(f32)
        total = pair[0]
        for k in range(1, reps):
            total = total + self.rep(pair[k].astype(wire), k).astype(f32)
        return total

    def gather_z(self, value):
        rows = value.shape[0]
        out = jnp.zeros((self.planes * rows,) + value.shape[1:], value.dtype)
        start = (0,) * (value.ndim - 1)
        out = lax.dynamic_update_slice(out, value, (self.z * rows,) + start)
        for k in range(1, self.planes):
            at = (self.z + self.planes - k) % self.planes
            out = lax.dynamic_update_slice(out, self.up(value, k), (at * rows,) + start)
        return out

    def scatter_z(self, value, wire):
        rows = value.shape[0] // self.planes
        total = lax.dynamic_slice_in_dim(value, self.z * rows, rows, 0).astype(f32)
        for k in range(1, self.planes):
            to = (self.z + k) % self.planes
            block = lax.dynamic_slice_in_dim(value, to * rows, rows, 0)
            total = total + self.up(block.astype(wire), k).astype(f32)
        return total

    def pair_rows(self, own, other):
        first = jnp.where(self.c == 0, own, other)
        second = jnp.where(self.c == 0, other, own)
        return jnp.stack([first, second])

    def order_reps(self, values):
        bit = 1
        while bit < self.reps:
            swap = (self.r & bit) != 0
            values = [jnp.where(swap, values[i ^ bit], values[i]) for i in range(self.reps)]
            bit *= 2
        return jnp.stack(values)


def adam_step(master, first, second, gradient, rate, decays):
    first_new = beta_first * first + (1.0 - beta_first) * gradient
    second_new = beta_second * second + (1.0 - beta_second) * gradient * gradient
    update = (
        first_new
        / (1.0 - beta_first**ADAM_STEP)
        / (jnp.sqrt(second_new / (1.0 - beta_second**ADAM_STEP)) + adam_eps)
    )
    if decays:
        update = update + weight_decay * master
    return (first_new, second_new, master - rate * update)


def to_chunks(values):
    seqs, length, n = values.shape
    return values.reshape(seqs, length // CHUNK, CHUNK, n).transpose(1, 3, 0, 2)


def from_chunks(values):
    chunks, n, seqs, _ = values.shape
    return values.transpose(2, 0, 3, 1).reshape(seqs, chunks * CHUNK, n)


def shift_down(values, offset):
    return jnp.pad(values, ((0, 0), (offset, 0), (0, 0)))[:, : values.shape[1]]


def shift_up(values, offset):
    return jnp.pad(values, ((0, 0), (0, offset), (0, 0)))[:, offset:]


def shards(
    reps, shard_size,
    hidden, segments, cotangent,
    in_master, in_first, in_second,
    x_master, x_first, x_second,
    dt_master, dt_first, dt_second,
    out_master, out_first, out_second,
    chan_master, chan_first, chan_second,
    gain_master, gain_first, gain_second,
):
    net = Links(reps, shard_size)
    planes, r, z, c = net.planes, net.r, net.z, net.c
    length, model = hidden.shape[1:]
    in_rows = in_master.shape[0]
    own_chan = out_master.shape[0]
    sub = own_chan // reps
    width = planes * sub
    xcols = x_master.shape[1]
    chan_cols = chan_master.shape[1]
    seqs = 2 * reps

    def sub_rows(value):
        return lax.dynamic_slice_in_dim(value, r * sub, sub, 0)

    in_view = in_master.reshape(in_rows, 2, planes, 2, reps, sub)
    in_mine = lax.dynamic_index_in_dim(in_view, r, 4, keepdims=False).astype(bf16)
    in_own = lax.dynamic_index_in_dim(in_mine, c, 3, keepdims=False).reshape(in_rows, 2 * width)
    in_other = lax.dynamic_index_in_dim(in_mine, 1 - c, 3, keepdims=False).reshape(in_rows, 2 * width)
    gain_pair = net.pair_rows(gain_master.astype(bf16), net.core(gain_master.astype(bf16)))
    small = jnp.concatenate(
        [
            sub_rows(x_master).astype(bf16),
            sub_rows(dt_master).astype(bf16),
            sub_rows(chan_master).astype(bf16),
            gain_pair.reshape(sub, reps),
        ],
        axis=1,
    )
    small_all = net.gather_z(small)
    w_x = small_all[:, :xcols]
    w_dt = small_all[:, xcols : xcols + RANK]
    channel = small_all[:, xcols + RANK : xcols + RANK + chan_cols].astype(f32)
    gain = small_all[:, xcols + RANK + chan_cols :].reshape(model).astype(f32)
    in_pair = net.pair_rows(in_own, net.core(in_other)).reshape(2 * in_rows, 2 * width)
    w_inner = net.gather_z(in_pair[:, :width])
    w_gate = net.gather_z(in_pair[:, width:])
    w_out = net.gather_z(sub_rows(out_master).astype(bf16))

    taps = channel[:, :KCONV]
    a_log = channel[:, KCONV : KCONV + NSTATE]
    conv_bias = channel[:, KCONV + NSTATE]
    dt_bias = channel[:, KCONV + NSTATE + 1]
    skip = channel[:, KCONV + NSTATE + 2]
    rates = -jnp.exp(a_log)
    rate_tiles = jnp.broadcast_to(rates.T[:, None, :], (NSTATE, SUBS, width))

    hidden_all = net.gather_plane(hidden[0])
    ids = net.gather_plane(segments.astype(f32)).reshape(seqs, length)
    upstream = net.gather_plane(cotangent[0])
    masks = [
        (jnp.pad(ids, ((0, 0), (KCONV - 1 - k, 0)), constant_values=-1)[:, :length] == ids)[:, :, None]
        for k in range(KCONV)
    ]
    cut = jnp.where(masks[KCONV - 2], 0.0, CUT)

    residual = hidden_all.astype(f32)
    inv_rms = lax.rsqrt(jnp.mean(residual * residual, axis=2, keepdims=True) + norm_eps)
    normed = (residual * inv_rms * gain).astype(bf16)
    inner_part = dot(normed, w_inner, ((2,), (0,)))
    conv_pre = jnp.zeros_like(inner_part) + conv_bias
    moved_list = []
    for k in range(KCONV):
        moved = jnp.where(masks[k], shift_down(inner_part, KCONV - 1 - k), 0.0)
        moved_list.append(moved)
        conv_pre = conv_pre + taps[:, k] * moved
    conv_out = jax.nn.silu(conv_pre).astype(bf16)
    conv_f = conv_out.astype(f32)
    projected = net.scatter_plane(dot(conv_out, w_x, ((2,), (0,))), f32)
    projected = net.gather_plane(projected)
    dt_in = projected[:, :, :RANK].astype(bf16)
    bc = to_chunks(projected[:, :, RANK:])
    dt_pre = dot(dt_in, w_dt, ((2,), (1,))) + dt_bias
    step_size = jax.nn.softplus(dt_pre)
    scanned, starts = scan_forward(step_size, cut, conv_out, bc, rate_tiles)

    gate_part = dot(normed, w_gate, ((2,), (0,)))
    mixer_y = scanned + skip * conv_f
    gate_act = jax.nn.silu(gate_part)
    mixed = (mixer_y * gate_act).astype(bf16)
    out_part = dot(mixed, w_out, ((2,), (0,)))
    layer_output = (hidden[0].astype(f32) + net.scatter_plane(out_part, bf16)).astype(bf16)

    grad_out = dot(mixed.reshape(-1, width), upstream.reshape(-1, model), ((0,), (0,)))
    grad_mixed = dot(upstream, w_out, ((2,), (1,)))
    grad_y = grad_mixed * gate_act
    grad_gate = (grad_mixed * mixer_y * silu_slope(gate_part)).astype(bf16)
    grad_skip = jnp.sum(grad_y * conv_f, axis=(0, 1))
    flat_normed = normed.reshape(-1, model)
    gin_gate = dot(flat_normed, grad_gate.reshape(-1, width), ((0,), (0,)))

    grad_step, grad_conv, grad_bc, grad_rates = scan_backward(
        step_size, cut, conv_out, bc, rate_tiles, starts, grad_y
    )
    grad_rates = jnp.sum(grad_rates, axis=1).T
    grad_conv = grad_conv + skip * grad_y
    grad_dtpre = grad_step * jax.nn.sigmoid(dt_pre)
    grad_dtbias = jnp.sum(grad_dtpre, axis=(0, 1))
    grad_dtlow = grad_dtpre.astype(bf16)
    grad_dt = dot(grad_dtlow.reshape(-1, width), dt_in.reshape(-1, RANK), ((0,), (0,)))
    grad_dtin = dot(grad_dtlow, w_dt, ((2,), (0,)))
    proj_part = jnp.concatenate([grad_dtin, from_chunks(grad_bc)], axis=2)
    grad_proj = net.gather_plane(net.scatter_plane(proj_part, f32).astype(bf16))
    grad_x = dot(conv_out.reshape(-1, width), grad_proj.reshape(-1, xcols), ((0,), (0,)))
    grad_conv = grad_conv + dot(grad_proj, w_x, ((2,), (1,)))
    grad_pre = grad_conv * silu_slope(conv_pre)
    grad_inner = jnp.zeros_like(grad_pre)
    tap_grads = []
    for k in range(KCONV):
        tap_grads.append(jnp.sum(grad_pre * moved_list[k], axis=(0, 1)))
        masked = jnp.where(masks[k], grad_pre, 0.0)
        grad_inner = grad_inner + taps[:, k] * shift_up(masked, KCONV - 1 - k)
    grad_convbias = jnp.sum(grad_pre, axis=(0, 1))
    grad_inner = grad_inner.astype(bf16)
    gin_inner = dot(flat_normed, grad_inner.reshape(-1, width), ((0,), (0,)))
    normed_part = dot(grad_inner, w_inner, ((2,), (1,))) + dot(grad_gate, w_gate, ((2,), (1,)))
    grad_gain = jnp.sum(normed_part * residual * inv_rms, axis=(0, 1))
    grad_normed = net.scatter_plane(normed_part, bf16)
    own_res, own_inv = residual[0], inv_rms[0]
    grad_scaled = grad_normed * gain
    input_grad = (
        own_inv * grad_scaled
        - own_res * own_inv**3 * jnp.mean(grad_scaled * own_res, axis=1, keepdims=True)
        + cotangent[0].astype(f32)
    ).astype(bf16)

    def full_in(gin):
        rows = net.scatter_z(gin, bf16).astype(bf16).reshape(2, in_rows, width)
        own = lax.dynamic_index_in_dim(rows, c, 0, keepdims=False)
        other = net.core(lax.dynamic_index_in_dim(rows, 1 - c, 0, keepdims=False))
        cols = net.pair_rows(own, other).reshape(2, in_rows, planes, sub)
        every = net.order_reps(net.gather_rep(cols.transpose(1, 2, 0, 3)))
        return every.transpose(1, 2, 3, 0, 4).reshape(in_rows, 2 * width * reps)

    out_sum = net.order_reps(net.gather_rep(net.scatter_z(grad_out, bf16).astype(bf16)))
    out_sum = out_sum.reshape(own_chan, model).astype(f32)
    in_sum = jnp.concatenate([full_in(gin_inner), full_in(gin_gate)], axis=1).astype(f32)
    grad_small = jnp.concatenate(
        [
            grad_x,
            grad_dt,
            jnp.stack(tap_grads, axis=1),
            grad_rates * rates,
            grad_convbias[:, None],
            grad_dtbias[:, None],
            grad_skip[:, None],
            grad_gain.reshape(width, reps),
        ],
        axis=1,
    )
    small_sum = net.order_reps(net.gather_rep(net.scatter_z(grad_small, f32)))
    gain_two = jnp.sum(small_sum[:, :, xcols + RANK + chan_cols :], axis=0).reshape(2, in_rows)
    gain_own = lax.dynamic_index_in_dim(gain_two, c, 0, keepdims=False)
    gain_sum = gain_own + net.core(lax.dynamic_index_in_dim(gain_two, 1 - c, 0, keepdims=False))
    small_sum = small_sum.reshape(own_chan, -1)
    x_sum = small_sum[:, :xcols]
    dt_sum = small_sum[:, xcols : xcols + RANK]
    chan_sum = small_sum[:, xcols + RANK : xcols + RANK + chan_cols]

    moments = (
        (in_master, in_first, in_second, in_sum),
        (x_master, x_first, x_second, x_sum),
        (dt_master, dt_first, dt_second, dt_sum),
        (out_master, out_first, out_second, out_sum),
        (chan_master, chan_first, chan_second, chan_sum),
        (gain_master, gain_first, gain_second, gain_sum),
    )
    updated = []
    for position, (master, first, second, gradient) in enumerate(moments):
        updated += adam_step(master, first, second, gradient, learn_rates[position], with_decay[position])
    return (layer_output[None], input_grad[None], *updated)


def solution(mesh):
    token = P(("rep", "shard"), None, None)
    rows = P("shard", None)
    placed = (token, P(("rep", "shard"), None), token) + (rows,) * 15 + (P("shard"),) * 3
    return jax.shard_map(
        functools.partial(shards, mesh.shape["rep"], mesh.shape["shard"]),
        mesh=mesh,
        in_specs=placed,
        out_specs=(token, token) + (rows,) * 15 + (P("shard"),) * 3,
        check_vma=False,
    )
```

time: 2840 us -> 1010 us (0.36)
  waiting for transfers between devices: 1530 us -> 237 us
  other arithmetic: 690 us -> 130 us
  Pallas kernels: 0 us -> 236 us
  local copies, waits for them, and re-layouts: 370 us -> 140 us
  starting transfers between devices: 0.41 us -> 137 us
  blocking collectives: 71 us -> 0 us
  matrix products: 141 us -> 106 us
    reduce_scatter x5 -> x0, waiting for transfers between devices: 925 us -> none  [the longest x1 641 us: shards(): lax.psum_scatter(lax.dot_general(part, grad_both, (((0,), (0,)), ((), ())...]
    all_gather x4 -> x0, waiting for transfers between devices: 388 us -> none  [the longest x1 245 us: shards(): lax.all_gather(in_copy, 'shard', axis=0, tiled=True)]
    ppermute x0 -> x85, waiting for transfers between devices: none -> 237 us  [the longest x24 142 us: up(): lax.ppermute(value, 'shard', [(i, (i + 2 * k) % n) for i in range(n)])]
    pallas_call x0 -> x2, Pallas kernels: none -> 236 us  [the longest x1 161 us: scan_backward(): pl.pallas_call(scan_bwd_kernel, grid=(chunks,), in_specs=[tokens, cuts, t...]
    psum x1 -> x0, waiting for transfers between devices: 220 us -> none  [shards(): lax.psum((in_grad, x_grad, dt_grad, out_grad, chan_grad, gain_grad), 'rep')]
    reduce_sum x50 -> x6, other arithmetic: 206 us -> 20 us  [the longest x1 9.35 us: shards(): tap_grads.append(jnp.sum(grad_pre * moved_list[k], axis=(0, 1)))]
    mul x116 -> x1, other arithmetic: 183 us -> 0.01 us  [scan_forward(): rates * LOG2E]
    add x92 -> x3, other arithmetic: 158 us -> 1.3 us  [the longest x2 1.26 us: scatter_plane(): partial[:reps].astype(f32)]
  transfers between devices with their start and end apart: 10 -> 85, of which waited for: 6 -> 33; matrix products, arithmetic and copies ran while one was open for 12% -> 29% of each run, Pallas kernels for 0% -> 0%
where the time goes in v1:
time: 1010 us; the launch traced here: 990 us
  waiting for transfers between devices  237 us (23%)
  Pallas kernels  236 us (23%)
  local copies, waits for them, and re-layouts  140 us (14%)
  starting transfers between devices  137 us (14%)
  other arithmetic  130 us (13%)
  matrix products  106 us (10%)
    pallas_call x1, Pallas kernels, scan_backward(): pl.pallas_call(scan_bwd_kernel, grid=(chunks,), in_specs=[tokens, cuts, t...  161 us
    ppermute x24, waiting for transfers between devices, up(): lax.ppermute(value, 'shard', [(i, (i + 2 * k) % n) for i in range(n)])  142 us
    dot_general x15, matrix products, dot(): return lax.dot_general(a, b, (dims, ((), ())), preferred_element_type=f32)  106 us
    ppermute x47, waiting for transfers between devices, rep(): return lax.ppermute(value, 'rep', [(i, i ^ k) for i in range(self.reps)])  90 us
    ppermute x24, starting transfers between devices, up(): lax.ppermute(value, 'shard', [(i, (i + 2 * k) % n) for i in range(n)])  84.2 us
    unnamed x217, local copies, waits for them, and re-layouts  76.8 us
    pallas_call x1, Pallas kernels, scan_forward(): pl.pallas_call(scan_fwd_kernel, grid=(chunks,), in_specs=[tokens, cuts, t...  75.2 us
    ppermute x47, starting transfers between devices, rep(): return lax.ppermute(value, 'rep', [(i, i ^ k) for i in range(self.reps)])  50.8 us
  transfers between devices with their start and end apart: 85, of which 33 were waited for; matrix products, arithmetic and copies ran while one was open for 29% of the time, Pallas kernels for 0%

profile of v1, /device:TPU:0, one launch (start us, length us, event | category | flops | bytes accessed | tf_op | source)
XLA Modules:
  0.0 989.6 jit_solution(2456987301303717826)
XLA Ops:
  9.4 9.1 copy.126
  39.4 18.7 %collective-permute-done.1 = bf16[128,315]{0,1:T(8,128)(2,1)S(1)} collective-permute-done((bf16[128,315]{0,1:T(8,128)(2,1)S(1)}, bf16[128,315]{0,1:T(8,128)(2,1)S(1)}, u32[]{:S(2)}, u32[]{:S(2)}) %collective-permute-start.1) | collective-permute-done | bytes 80672 | tf_op jit(solution)/shard_map/ppermute | solution.py:287
  58.1 11.9 %collective-permute-start.2 = (bf16[128,315]{0,1:T(8,128)(2,1)S(1)}, bf16[128,315]{0,1:T(8,128)(2,1)S(1)}, u32[]{:S(2)}, u32[]{:S(2)}) collective-permute-start(bf16[128,315]{0,1:T(8,128)(2,1)S(1)} %get-tuple-element.215), channel_id=1, source_target_pairs={{0,4},{1,5},{2,6},{3,7},{4,0},{5,1},{6,2},{7,3},{8,12},{9,13},{10,... | collective-permute-start | bytes 241928 | tf_op jit(solution)/shard_map/ppermute | solution.py:287
  93.5 29.0 %collective-permute-done.10 = bf16[128,2048]{1,0:T(8,128)(2,1)S(1)} collective-permute-done((bf16[128,2048]{1,0:T(8,128)(2,1)S(1)}, bf16[128,2048]{1,0:T(8,128)(2,1)S(1)}, u32[]{:S(2)}, u32[]{:S(2)}) %collective-permute-start.10) | collective-permute-done | bytes 524320 | tf_op jit(solution)/shard_map/ppermute | solution.py:280
  131.3 9.5 collective-permute-done.14
  140.8 11.2 %collective-permute-done.26 = bf16[512,512]{1,0:T(8,128)(2,1)S(1)} collective-permute-done((bf16[512,512]{1,0:T(8,128)(2,1)S(1)}, bf16[512,512]{1,0:T(8,128)(2,1)S(1)}, u32[]{:S(2)}, u32[]{:S(2)}) %collective-permute-start.26) | collective-permute-done | bytes 524320 | tf_op jit(solution)/shard_map/ppermute | solution.py:287
  152.2 20.0 %collective-permute-done.15 = bf16[512,512]{1,0:T(8,128)(2,1)S(1)} collective-permute-done((bf16[512,512]{1,0:T(8,128)(2,1)S(1)}, bf16[512,512]{1,0:T(8,128)(2,1)S(1)}, u32[]{:S(2)}, u32[]{:S(2)}) %collective-permute-start.15) | collective-permute-done | bytes 524320 | tf_op jit(solution)/shard_map/ppermute | solution.py:287
  172.6 21.2 %collective-permute-start.28 = (bf16[512,512]{1,0:T(8,128)(2,1)S(1)}, bf16[512,512]{1,0:T(8,128)(2,1)S(1)}, u32[]{:S(2)}, u32[]{:S(2)}) collective-permute-start(bf16[512,512]{1,0:T(8,128)(2,1)S(1)} %get-tuple-element.190), channel_id=1, source_target_pairs={{0,6},{1,7},{2,0},{3,1},{4,2},{5,3},{6,4},{7,5},{8,14},{9,15},{10,... | collective-permute-start | bytes 1572872 | tf_op jit(solution)/shard_map/ppermute | solution.py:287
  196.5 11.1 %collective-permute-done.27 = bf16[512,512]{1,0:T(8,128)(2,1)S(1)} collective-permute-done((bf16[512,512]{1,0:T(8,128)(2,1)S(1)}, bf16[512,512]{1,0:T(8,128)(2,1)S(1)}, u32[]{:S(2)}, u32[]{:S(2)}) %collective-permute-start.27) | collective-permute-done | bytes 524320 | tf_op jit(solution)/shard_map/ppermute | solution.py:287
  240.2 20.5 %fusion.13 = (f32[512]{0:T(512)}, f32[8,256,512]{2,1,0:T(8,128)}, bf16[8,256,512]{2,1,0:T(8,128)(2,1)S(1)}, f32[8,256,512]{2,1,0:T(8,128)}, f32[8,256,512]{2,1,0:T(8,128)}) fusion(f32[8,256,512]{2,1,0:T(8,128)} %fusion.17, f32[8,256,512]{2,1,0:T(8,128)} %fusion.18, pred[8,256]{1,0:T(8,128)(4,1)S(1)} %copy-done.68, f32[512]{0:T(512)S(1)} %bitcast.379, ...), kind=kOutput, calls=%fused_computation.36 | convolution fusion | flops 4321181184 | bytes 33574912 | tf_op jit(solution)/shard_map/dot_general | solution.py:38
  270.8 9.0 copy.134
  279.8 9.5 copy.145
  303.7 11.3 %convert_element_type.227 = f32[8,256,2048]{2,1,0:T(8,128)} convert(bf16[8,256,2048]{2,1,0:T(8,128)(2,1)} %copy-done.2) | non-fusion elementwise | flops 4194304 | bytes 25165824 | tf_op jit(solution)/shard_map/convert_element_type | solution.py:438
  323.0 75.2 %scan_forward.1 = (f32[8,256,512]{2,1,0:T(8,128)}, f32[8,16,8,512]{3,2,1,0:T(8,128)}) custom-call(f32[8,256,512]{2,1,0:T(8,128)} %get-tuple-element.233.step_ref, f32[8,256,1]{2,1,0:T(8,128)S(1)} %copy.131.cut_ref, bf16[8,256,512]{2,1,0:T(8,128)(2,1)} %copy-done.3, f32[8,32,8,32]{3,2,1,0:T(8,128)S(1)} %bitcast.318, f32[16,8,512]{2,1,0:T(8,128)S(1)} %broadcast_in_dim.99.rate_ref), custom_call_target="tpu_custom_call" | custom-call | flops 134217728 | bytes 12582912 | tf_op jit(solution)/shard_map/scan_forward/pallas_call | solution.py:215
  423.7 9.7 fusion.30
  434.2 161.1 %scan_backward.1 = (f32[8,256,512]{2,1,0:T(8,128)}, f32[8,256,512]{2,1,0:T(8,128)}, f32[8,32,8,32]{3,2,1,0:T(8,128)}, f32[16,8,512]{2,1,0:T(8,128)}) custom-call(f32[8,256,512]{2,1,0:T(8,128)} %get-tuple-element.233.step_ref, f32[8,256,1]{2,1,0:T(8,128)} %copy-done, bf16[8,256,512]{2,1,0:T(8,128)(2,1)} %copy-done.3, f32[8,32,8,32]{3,2,1,0:T(8,128)} %bitcast.319, ...), custom_call_target="tpu_custom_call" | custom-call | flops 402653184 | bytes 25165824 | tf_op jit(solution)/shard_map/scan_backward/pallas_call | solution.py:244
  607.8 11.0 %collective-permute-start.77 = (bf16[128,2048]{1,0:T(8,128)(2,1)}, bf16[128,2048]{1,0:T(8,128)(2,1)}, u32[]{:S(2)}, u32[]{:S(2)}) collective-permute-start(bf16[128,2048]{1,0:T(8,128)(2,1)} %get-tuple-element.158), channel_id=1, source_target_pairs={{0,2},{1,3},{2,4},{3,5},{4,6},{5,7},{6,0},{7,1},{8,10},{9,11},{10,... | collective-permute-start | bytes 1572872 | tf_op jit(solution)/shard_map/ppermute | solution.py:287
  636.8 20.4 %collective-permute-done.78 = bf16[128,2048]{1,0:T(8,128)(2,1)} collective-permute-done((bf16[128,2048]{1,0:T(8,128)(2,1)}, bf16[128,2048]{1,0:T(8,128)(2,1)}, u32[]{:S(2)}, u32[]{:S(2)}) %collective-permute-start.78) | collective-permute-done | bytes 524320 | tf_op jit(solution)/shard_map/ppermute | solution.py:287
  657.2 11.2 %collective-permute-start.64 = (bf16[512,512]{1,0:T(8,128)(2,1)}, bf16[512,512]{1,0:T(8,128)(2,1)S(1)}, u32[]{:S(2)}, u32[]{:S(2)}) collective-permute-start(bf16[512,512]{1,0:T(8,128)(2,1)} %get-tuple-element.165), channel_id=1, source_target_pairs={{0,6},{1,7},{2,0},{3,1},{4,2},{5,3},{6,4},{7,5},{8,14},{9,15},{10,... | collective-permute-start | bytes 1572872 | tf_op jit(solution)/shard_map/ppermute | solution.py:287
  675.0 26.4 %collective-permute-done.63 = bf16[512,512]{1,0:T(8,128)(2,1)S(1)} collective-permute-done((bf16[512,512]{1,0:T(8,128)(2,1)}, bf16[512,512]{1,0:T(8,128)(2,1)S(1)}, u32[]{:S(2)}, u32[]{:S(2)}) %collective-permute-start.63) | collective-permute-done | bytes 524320 | tf_op jit(solution)/shard_map/ppermute | solution.py:287
  730.8 10.6 %broadcast_select_fusion = (f32[8,256,512]{2,1,0:T(8,128)S(1)}, f32[8,256,512]{2,1,0:T(8,128)}, f32[8,256,512]{2,1,0:T(8,128)}, f32[8,256,512]{2,1,0:T(8,128)}) fusion(pred[8,256]{1,0:T(8,128)(4,1)S(1)} %copy-done.67, pred[8,256]{1,0:T(8,128)(4,1)S(1)} %copy-done.74, pred[8,256]{1,0:T(8,128)(4,1)S(1)} %copy-done.71, f32[8,256,512]{2,1,0:T(8,128)} %get-tuple-element.137, ...), kind=kOutput, calls=%fused_computation.87 | convolution fusion | flops 350224384 | bytes 30187520 | tf_op jit(solution)/shard_map/dot_general | solution.py:38
  741.5 9.3 multiply_reduce_fusion.2
  757.5 14.3 %multiply_reduce_fusion = (f32[2048]{0:T(1024)S(1)}, f32[8,256,2048]{2,1,0:T(8,128)}) fusion(bf16[8,256,2048]{2,1,0:T(8,128)(2,1)} %copy-done.2, f32[8,256]{1,0:T(8,128)S(1)} %copy-done.50, f32[8,256,2048]{2,1,0:T(8,128)} %fusion.32, bf16[8,256,512]{2,1,0:T(8,128)(2,1)S(1)} %get-tuple-element.157, bf16[2048,512]{1,0:T(8,128)(2,1)S(1)} %copy-done.11), kind=kOutput, calls=%fused_computation | convolution fusion | flops 4315936768 | bytes 46153728 | tf_op jit(solution)/shard_map/dot_general | solution.py:38
  772.6 9.1 collective-permute-start.70
  815.3 16.3 %collective-permute-done.55 = bf16[512,512]{1,0:T(8,128)(2,1)S(1)} collective-permute-done((bf16[512,512]{1,0:T(8,128)(2,1)S(1)}, bf16[512,512]{1,0:T(8,128)(2,1)S(1)}, u32[]{:S(2)}, u32[]{:S(2)}) %collective-permute-start.55) | collective-permute-done | bytes 524320 | tf_op jit(solution)/shard_map/ppermute | solution.py:287
  880.1 10.1 %fusion.76 = (bf16[4,256,2048]{2,1,0:T(8,128)(2,1)S(1)}, f32[4,256,2048]{2,1,0:T(8,128)}) fusion(bf16[4,256,2048]{2,1,0:T(8,128)(2,1)} %collective-permute-done.32, f32[8,256,2048]{2,1,0:T(8,128)} %fusion.30), kind=kLoop, calls=%fused_computation.297 | loop fusion | flops 6291456 | bytes 25165824 | tf_op jit(solution)/shard_map/convert.8
  895.5 10.3 %fusion.74 = (bf16[4,256,2048]{2,1,0:T(8,128)(2,1)S(1)}, f32[4,256,2048]{2,1,0:T(8,128)}) fusion(bf16[4,256,2048]{2,1,0:T(8,128)(2,1)} %collective-permute-done.50, f32[8,256,2048]{2,1,0:T(8,128)} %get-tuple-element.237), kind=kLoop, calls=%fused_computation.296 | loop fusion | flops 6291456 | bytes 25165824 | tf_op jit(solution)/shard_map/convert.4
  909.3 9.1 collective-permute-done.33
  919.6 23.4 %multiply_subtract_fusion = (f32[256,8192]{0,1:T(8,128)}, f32[256,8192]{0,1:T(8,128)}, f32[256,8192]{0,1:T(8,128)}) fusion(f32[256,8192]{0,1:T(8,128)} %copy.126, bf16[256,4096]{0,1:T(8,128)(2,1)} %bitcast.332, bf16[256,4096]{0,1:T(8,128)(2,1)S(1)} %bitcast.331, f32[256,8192]{0,1:T(8,128)} %copy.145, f32[256,8192]{0,1:T(8,128)} %copy.134), kind=kLoop, calls=%fused_computation.12 | loop fusion | flops 39845888 | bytes 54525952 | tf_op jit(solution)/shard_map/sub | solution.py:352
  943.0 8.9 copy.156
  951.9 8.9 copy.157
  960.8 9.0 copy.158
  (537 shorter events, 340.5 us)
Async XLA Ops:
  0.7 89.7 %collective-permute-start.8 = (bf16[256,2048]{1,0:T(8,128)(2,1)}, bf16[256,2048]{1,0:T(8,128)(2,1)}, u32[]{:S(2)}, u32[]{:S(2)}) collective-permute-start(bf16[256,2048]{1,0:T(8,128)(2,1)} %bitcast.327), channel_id=1, source_target_pairs={{0,8},{8,0},{16,24},{24,16},{1,9},{9,1},{17,25},{25,17},{2,10},{10... | collective-permute-start | bytes 3145736 | tf_op jit(solution)/shard_map/ppermute | solution.py:280
  3.7 86.1 %collective-permute-start.9 = (bf16[256,2048]{1,0:T(8,128)(2,1)}, bf16[256,2048]{1,0:T(8,128)(2,1)S(1)}, u32[]{:S(2)}, u32[]{:S(2)}) collective-permute-start(bf16[256,2048]{1,0:T(8,128)(2,1)} %bitcast.328), channel_id=1, source_target_pairs={{0,16},{8,24},{16,0},{24,8},{1,17},{9,25},{17,1},{25,9},{2,18},{10... | collective-permute-start | bytes 3145736 | tf_op jit(solution)/shard_map/ppermute | solution.py:280
  28.1 58.2 %collective-permute-start.29 = (bf16[128,2048]{1,0:T(8,128)(2,1)}, bf16[128,2048]{1,0:T(8,128)(2,1)}, u32[]{:S(2)}, u32[]{:S(2)}) collective-permute-start(bf16[128,2048]{1,0:T(8,128)(2,1)} %get-tuple-element.150), channel_id=1, source_target_pairs={{0,2},{1,3},{2,4},{3,5},{4,6},{5,7},{6,0},{7,1},{8,10},{9,11},{10,... | collective-permute-start | bytes 1572872 | tf_op jit(solution)/shard_map/ppermute | solution.py:287
  32.0 94.1 %collective-permute-start.30 = (bf16[128,2048]{1,0:T(8,128)(2,1)}, bf16[128,2048]{1,0:T(8,128)(2,1)}, u32[]{:S(2)}, u32[]{:S(2)}) collective-permute-start(bf16[128,2048]{1,0:T(8,128)(2,1)} %get-tuple-element.150), channel_id=1, source_target_pairs={{0,4},{1,5},{2,6},{3,7},{4,0},{5,1},{6,2},{7,3},{8,12},{9,13},{10,... | collective-permute-start | bytes 1572872 | tf_op jit(solution)/shard_map/ppermute | solution.py:287
  80.8 47.3 %collective-permute-start.31 = (bf16[128,2048]{1,0:T(8,128)(2,1)}, bf16[128,2048]{1,0:T(8,128)(2,1)}, u32[]{:S(2)}, u32[]{:S(2)}) collective-permute-start(bf16[128,2048]{1,0:T(8,128)(2,1)} %get-tuple-element.150), channel_id=1, source_target_pairs={{0,6},{1,7},{2,0},{3,1},{4,2},{5,3},{6,4},{7,5},{8,14},{9,15},{10,... | collective-permute-start | bytes 1572872 | tf_op jit(solution)/shard_map/ppermute | solution.py:287
  86.3 107.5 %collective-permute-start.36 = (bf16[256,2048]{1,0:T(8,128)(2,1)S(1)}, bf16[256,2048]{1,0:T(8,128)(2,1)S(1)}, u32[]{:S(2)}, u32[]{:S(2)}) collective-permute-start(bf16[256,2048]{1,0:T(8,128)(2,1)S(1)} %bitcast.329), channel_id=1, source_target_pairs={{0,8},{8,0},{16,24},{24,16},{1,9},{9,1},{17,25},{25,17},{2,10},{10... | collective-permute-start | bytes 3145736 | tf_op jit(solution)/shard_map/ppermute | solution.py:280
  89.8 32.7 %collective-permute-start.10 = (bf16[128,2048]{1,0:T(8,128)(2,1)S(1)}, bf16[128,2048]{1,0:T(8,128)(2,1)S(1)}, u32[]{:S(2)}, u32[]{:S(2)}) collective-permute-start(bf16[128,2048]{1,0:T(8,128)(2,1)S(1)} %slice.306), channel_id=1, source_target_pairs={{0,8},{8,0},{16,24},{24,16},{1,9},{9,1},{17,25},{25,17},{2,10},{10... | collective-permute-start | bytes 1572872 | tf_op jit(solution)/shard_map/ppermute | solution.py:280
  91.4 32.6 %collective-permute-start.11 = (bf16[128,2048]{1,0:T(8,128)(2,1)S(1)}, bf16[128,2048]{1,0:T(8,128)(2,1)S(1)}, u32[]{:S(2)}, u32[]{:S(2)}) collective-permute-start(bf16[128,2048]{1,0:T(8,128)(2,1)S(1)} %slice.307), channel_id=1, source_target_pairs={{0,16},{8,24},{16,0},{24,8},{1,17},{9,25},{17,1},{25,9},{2,18},{10... | collective-permute-start | bytes 1572872 | tf_op jit(solution)/shard_map/ppermute | solution.py:280
  122.5 50.1 %collective-permute-start.37 = (bf16[256,2048]{1,0:T(8,128)(2,1)S(1)}, bf16[256,2048]{1,0:T(8,128)(2,1)S(1)}, u32[]{:S(2)}, u32[]{:S(2)}) collective-permute-start(bf16[256,2048]{1,0:T(8,128)(2,1)S(1)} %bitcast.330), channel_id=1, source_target_pairs={{0,16},{8,24},{16,0},{24,8},{1,17},{9,25},{17,1},{25,9},{2,18},{10... | collective-permute-start | bytes 3145736 | tf_op jit(solution)/shard_map/ppermute | solution.py:280
  126.1 94.8 %collective-permute-start.12 = (bf16[4,256,2048]{2,1,0:T(8,128)(2,1)S(1)}, bf16[4,256,2048]{2,1,0:T(8,128)(2,1)S(1)}, u32[]{:S(2)}, u32[]{:S(2)}) collective-permute-start(bf16[4,256,2048]{2,1,0:T(8,128)(2,1)S(1)} %pad_maximum_fusion), channel_id=1, source_target_pairs={{0,1},{1,0},{2,3},{3,2},{4,5},{5,4},{6,7},{7,6},{8,9},{9,8},{10,11... | collective-permute-start | bytes 12582920 | tf_op jit(solution)/shard_map/ppermute | solution.py:283
  152.0 67.4 %collective-permute-start.16 = (bf16[512,512]{1,0:T(8,128)(2,1)S(1)}, bf16[512,512]{1,0:T(8,128)(2,1)S(1)}, u32[]{:S(2)}, u32[]{:S(2)}) collective-permute-start(bf16[512,512]{1,0:T(8,128)(2,1)S(1)} %get-tuple-element.188), channel_id=1, source_target_pairs={{0,6},{1,7},{2,0},{3,1},{4,2},{5,3},{6,4},{7,5},{8,14},{9,15},{10,... | collective-permute-start | bytes 1572872 | tf_op jit(solution)/shard_map/ppermute | solution.py:287
  172.2 35.4 %collective-permute-start.27 = (bf16[512,512]{1,0:T(8,128)(2,1)S(1)}, bf16[512,512]{1,0:T(8,128)(2,1)S(1)}, u32[]{:S(2)}, u32[]{:S(2)}) collective-permute-start(bf16[512,512]{1,0:T(8,128)(2,1)S(1)} %get-tuple-element.190), channel_id=1, source_target_pairs={{0,4},{1,5},{2,6},{3,7},{4,0},{5,1},{6,2},{7,3},{8,12},{9,13},{10,... | collective-permute-start | bytes 1572872 | tf_op jit(solution)/shard_map/ppermute | solution.py:287
  172.6 46.9 %collective-permute-start.28 = (bf16[512,512]{1,0:T(8,128)(2,1)S(1)}, bf16[512,512]{1,0:T(8,128)(2,1)S(1)}, u32[]{:S(2)}, u32[]{:S(2)}) collective-permute-start(bf16[512,512]{1,0:T(8,128)(2,1)S(1)} %get-tuple-element.190), channel_id=1, source_target_pairs={{0,6},{1,7},{2,0},{3,1},{4,2},{5,3},{6,4},{7,5},{8,14},{9,15},{10,... | collective-permute-start | bytes 1572872 | tf_op jit(solution)/shard_map/ppermute | solution.py:287
  604.2 67.5 %collective-permute-start.41 = (f32[4,256,160]{1,2,0:T(8,128)}, f32[4,256,160]{1,2,0:T(8,128)}, u32[]{:S(2)}, u32[]{:S(2)}) collective-permute-start(f32[4,256,160]{1,2,0:T(8,128)} %pad_maximum_fusion.5), channel_id=1, source_target_pairs={{0,1},{1,0},{2,3},{3,2},{4,5},{5,4},{6,7},{7,6},{8,9},{9,8},{10,11... | collective-permute-start | bytes 1966088 | tf_op jit(solution)/shard_map/ppermute | solution.py:283
  618.8 38.5 %collective-permute-start.78 = (bf16[128,2048]{1,0:T(8,128)(2,1)}, bf16[128,2048]{1,0:T(8,128)(2,1)}, u32[]{:S(2)}, u32[]{:S(2)}) collective-permute-start(bf16[128,2048]{1,0:T(8,128)(2,1)} %get-tuple-element.160), channel_id=1, source_target_pairs={{0,4},{1,5},{2,6},{3,7},{4,0},{5,1},{6,2},{7,3},{8,12},{9,13},{10,... | collective-permute-start | bytes 1572872 | tf_op jit(solution)/shard_map/ppermute | solution.py:287
  622.1 46.3 %collective-permute-start.79 = (bf16[128,2048]{1,0:T(8,128)(2,1)}, bf16[128,2048]{1,0:T(8,128)(2,1)}, u32[]{:S(2)}, u32[]{:S(2)}) collective-permute-start(bf16[128,2048]{1,0:T(8,128)(2,1)} %get-tuple-element.159), channel_id=1, source_target_pairs={{0,6},{1,7},{2,0},{3,1},{4,2},{5,3},{6,4},{7,5},{8,14},{9,15},{10,... | collective-permute-start | bytes 1572872 | tf_op jit(solution)/shard_map/ppermute | solution.py:287
  625.2 48.9 %collective-permute-start.62 = (bf16[512,512]{1,0:T(8,128)(2,1)}, bf16[512,512]{1,0:T(8,128)(2,1)}, u32[]{:S(2)}, u32[]{:S(2)}) collective-permute-start(bf16[512,512]{1,0:T(8,128)(2,1)} %get-tuple-element.164), channel_id=1, source_target_pairs={{0,2},{1,3},{2,4},{3,5},{4,6},{5,7},{6,0},{7,1},{8,10},{9,11},{10,... | collective-permute-start | bytes 1572872 | tf_op jit(solution)/shard_map/ppermute | solution.py:287
  636.7 64.7 %collective-permute-start.63 = (bf16[512,512]{1,0:T(8,128)(2,1)}, bf16[512,512]{1,0:T(8,128)(2,1)S(1)}, u32[]{:S(2)}, u32[]{:S(2)}) collective-permute-start(bf16[512,512]{1,0:T(8,128)(2,1)} %get-tuple-element.166), channel_id=1, source_target_pairs={{0,4},{1,5},{2,6},{3,7},{4,0},{5,1},{6,2},{7,3},{8,12},{9,13},{10,... | collective-permute-start | bytes 1572872 | tf_op jit(solution)/shard_map/ppermute | solution.py:287
  657.2 44.7 %collective-permute-start.64 = (bf16[512,512]{1,0:T(8,128)(2,1)}, bf16[512,512]{1,0:T(8,128)(2,1)S(1)}, u32[]{:S(2)}, u32[]{:S(2)}) collective-permute-start(bf16[512,512]{1,0:T(8,128)(2,1)} %get-tuple-element.165), channel_id=1, source_target_pairs={{0,6},{1,7},{2,0},{3,1},{4,2},{5,3},{6,4},{7,5},{8,14},{9,15},{10,... | collective-permute-start | bytes 1572872 | tf_op jit(solution)/shard_map/ppermute | solution.py:287
  671.2 51.0 %collective-permute-start.80 = (bf16[128,2048]{1,0:T(8,128)(2,1)}, bf16[128,2048]{1,0:T(8,128)(2,1)}, u32[]{:S(2)}, u32[]{:S(2)}) collective-permute-start(bf16[128,2048]{1,0:T(8,128)(2,1)} %add_convert_fusion.1), channel_id=1, source_target_pairs={{0,16},{8,24},{16,0},{24,8},{1,17},{9,25},{17,1},{25,9},{2,18},{10... | collective-permute-start | bytes 1572872 | tf_op jit(solution)/shard_map/ppermute | solution.py:280
  671.7 54.1 %collective-permute-start.82 = (bf16[128,2048]{1,0:T(8,128)(2,1)}, bf16[128,2048]{1,0:T(8,128)(2,1)}, u32[]{:S(2)}, u32[]{:S(2)}) collective-permute-start(bf16[128,2048]{1,0:T(8,128)(2,1)} %add_convert_fusion.1), channel_id=1, source_target_pairs={{0,8},{8,0},{16,24},{24,16},{1,9},{9,1},{17,25},{25,17},{2,10},{10... | collective-permute-start | bytes 1572872 | tf_op jit(solution)/shard_map/ppermute | solution.py:280
  724.2 68.2 %collective-permute-start.81 = (bf16[64,2048]{1,0:T(8,128)(2,1)}, bf16[64,2048]{1,0:T(8,128)(2,1)}, u32[]{:S(2)}, u32[]{:S(2)}) collective-permute-start(bf16[64,2048]{1,0:T(8,128)(2,1)} %slice.361), channel_id=1, source_target_pairs={{0,8},{8,0},{16,24},{24,16},{1,9},{9,1},{17,25},{25,17},{2,10},{10... | collective-permute-start | bytes 786440 | tf_op jit(solution)/shard_map/ppermute | solution.py:280
  727.5 67.3 %collective-permute-start.83 = (bf16[64,2048]{1,0:T(8,128)(2,1)}, bf16[64,2048]{1,0:T(8,128)(2,1)}, u32[]{:S(2)}, u32[]{:S(2)}) collective-permute-start(bf16[64,2048]{1,0:T(8,128)(2,1)} %slice.362), channel_id=1, source_target_pairs={{0,16},{8,24},{16,0},{24,8},{1,17},{9,25},{17,1},{25,9},{2,18},{10... | collective-permute-start | bytes 786440 | tf_op jit(solution)/shard_map/ppermute | solution.py:280
  794.8 36.8 %collective-permute-start.55 = (bf16[512,512]{1,0:T(8,128)(2,1)S(1)}, bf16[512,512]{1,0:T(8,128)(2,1)S(1)}, u32[]{:S(2)}, u32[]{:S(2)}) collective-permute-start(bf16[512,512]{1,0:T(8,128)(2,1)S(1)} %get-tuple-element.163), channel_id=1, source_target_pairs={{0,4},{1,5},{2,6},{3,7},{4,0},{5,1},{6,2},{7,3},{8,12},{9,13},{10,... | collective-permute-start | bytes 1572872 | tf_op jit(solution)/shard_map/ppermute | solution.py:287
  798.7 32.9 %collective-permute-start.56 = (bf16[512,512]{1,0:T(8,128)(2,1)S(1)}, bf16[512,512]{1,0:T(8,128)(2,1)S(1)}, u32[]{:S(2)}, u32[]{:S(2)}) collective-permute-start(bf16[512,512]{1,0:T(8,128)(2,1)S(1)} %get-tuple-element.162), channel_id=1, source_target_pairs={{0,6},{1,7},{2,0},{3,1},{4,2},{5,3},{6,4},{7,5},{8,14},{9,15},{10,... | collective-permute-start | bytes 1572872 | tf_op jit(solution)/shard_map/ppermute | solution.py:287
  814.5 65.6 %collective-permute-start.32 = (bf16[4,256,2048]{2,1,0:T(8,128)(2,1)}, bf16[4,256,2048]{2,1,0:T(8,128)(2,1)}, u32[]{:S(2)}, u32[]{:S(2)}) collective-permute-start(bf16[4,256,2048]{2,1,0:T(8,128)(2,1)} %slice.522), channel_id=1, source_target_pairs={{0,1},{1,0},{2,3},{3,2},{4,5},{5,4},{6,7},{7,6},{8,9},{9,8},{10,11... | collective-permute-start | bytes 12582920 | tf_op jit(solution)/shard_map/ppermute | solution.py:283
  815.2 80.3 %collective-permute-start.50 = (bf16[4,256,2048]{2,1,0:T(8,128)(2,1)}, bf16[4,256,2048]{2,1,0:T(8,128)(2,1)}, u32[]{:S(2)}, u32[]{:S(2)}) collective-permute-start(bf16[4,256,2048]{2,1,0:T(8,128)(2,1)} %slice.521), channel_id=1, source_target_pairs={{0,1},{1,0},{2,3},{3,2},{4,5},{5,4},{6,7},{7,6},{8,9},{9,8},{10,11... | collective-permute-start | bytes 12582920 | tf_op jit(solution)/shard_map/ppermute | solution.py:283
  893.1 76.7 %collective-permute-start.34 = (bf16[256,2048]{1,0:T(8,128)(2,1)}, bf16[256,2048]{1,0:T(8,128)(2,1)}, u32[]{:S(2)}, u32[]{:S(2)}) collective-permute-start(bf16[256,2048]{1,0:T(8,128)(2,1)} %get-tuple-element.175), channel_id=1, source_target_pairs={{0,16},{8,24},{16,0},{24,8},{1,17},{9,25},{17,1},{25,9},{2,18},{10... | collective-permute-start | bytes 3145736 | tf_op jit(solution)/shard_map/ppermute | solution.py:280
  893.8 76.0 %collective-permute-start.35 = (bf16[256,2048]{1,0:T(8,128)(2,1)}, bf16[256,2048]{1,0:T(8,128)(2,1)}, u32[]{:S(2)}, u32[]{:S(2)}) collective-permute-start(bf16[256,2048]{1,0:T(8,128)(2,1)} %get-tuple-element.174), channel_id=1, source_target_pairs={{0,24},{8,16},{16,8},{24,0},{1,25},{9,17},{17,9},{25,1},{2,26},{10... | collective-permute-start | bytes 3145736 | tf_op jit(solution)/shard_map/ppermute | solution.py:280
  907.5 66.6 %collective-permute-start.51 = (bf16[256,2048]{1,0:T(8,128)(2,1)}, bf16[256,2048]{1,0:T(8,128)(2,1)}, u32[]{:S(2)}, u32[]{:S(2)}) collective-permute-start(bf16[256,2048]{1,0:T(8,128)(2,1)} %get-tuple-element.167), channel_id=1, source_target_pairs={{0,8},{8,0},{16,24},{24,16},{1,9},{9,1},{17,25},{25,17},{2,10},{10... | collective-permute-start | bytes 3145736 | tf_op jit(solution)/shard_map/ppermute | solution.py:280
  908.6 70.9 %collective-permute-start.52 = (bf16[256,2048]{1,0:T(8,128)(2,1)}, bf16[256,2048]{1,0:T(8,128)(2,1)}, u32[]{:S(2)}, u32[]{:S(2)}) collective-permute-start(bf16[256,2048]{1,0:T(8,128)(2,1)} %get-tuple-element.169), channel_id=1, source_target_pairs={{0,16},{8,24},{16,0},{24,8},{1,17},{9,25},{17,1},{25,9},{2,18},{10... | collective-permute-start | bytes 3145736 | tf_op jit(solution)/shard_map/ppermute | solution.py:280
  918.4 61.8 %collective-permute-start.53 = (bf16[256,2048]{1,0:T(8,128)(2,1)}, bf16[256,2048]{1,0:T(8,128)(2,1)}, u32[]{:S(2)}, u32[]{:S(2)}) collective-permute-start(bf16[256,2048]{1,0:T(8,128)(2,1)} %get-tuple-element.168), channel_id=1, source_target_pairs={{0,24},{8,16},{16,8},{24,0},{1,25},{9,17},{17,9},{25,1},{2,26},{10... | collective-permute-start | bytes 3145736 | tf_op jit(solution)/shard_map/ppermute | solution.py:280
  (148 other events, 3703.0 us)

commit v2 on v1

v2 whole, which is shorter than its diff:
```python
import functools

import jax
import jax.numpy as jnp
from jax import lax
from jax.experimental import pallas as pl
from jax.experimental.pallas import tpu as pltpu
from jax.sharding import PartitionSpec as P

NSTATE = 16
RANK = 128
KCONV = 4
ADAM_STEP = 10
CHUNK = 32
LANES = 128
SUBS = 8
CUT = 1e30
MASKS = 8
FWD_UNROLL = 8
BWD_UNROLL = 4
LOG2E = 1.4426950408889634

norm_eps = 1e-05
beta_first = 0.9
beta_second = 0.95
adam_eps = 1e-08
weight_decay = 0.1
learn_rates = (0.044, 0.03, 0.18, 0.09, 1.0, 0.6)
with_decay = (True, True, True, True, False, False)

bf16 = jnp.bfloat16
f32 = jnp.float32
PARTS = bf16


def silu_slope(values):
    sigma = jax.nn.sigmoid(values)
    return sigma * (1.0 + values * (1.0 - sigma))


def dot(a, b, dims):
    return lax.dot_general(a, b, (dims, ((), ())), preferred_element_type=f32)


def expand_inputs(bc_ref, bx, sb):
    rows = 2 * NSTATE * SUBS
    v = bc_ref[0, :, pl.ds(sb * SUBS, SUBS), :].reshape(rows, CHUNK)
    high = v.astype(bf16)
    rest = v - high.astype(f32)
    middle = rest.astype(bf16)
    low = (rest - middle.astype(f32)).astype(bf16)
    pieces = jnp.concatenate([high, middle, low], axis=1)
    token = lax.broadcasted_iota(jnp.int32, (3 * CHUNK, LANES), 0) % CHUNK
    for t in range(CHUNK):
        bx[t] = dot(pieces, (token == t).astype(bf16), ((1,), (0,))).reshape(2 * NSTATE, SUBS, LANES)


def lane_sums(acc, gbc_ref, sb):
    rows = 2 * NSTATE * SUBS
    ones = jnp.ones((SUBS, 2 * LANES), bf16)
    for t in range(CHUNK):
        v = acc[t].reshape(rows, LANES)
        high = v.astype(bf16)
        low = (v - high.astype(f32)).astype(bf16)
        sums = dot(ones, jnp.concatenate([high, low], axis=1), ((1,), (1,)))
        gbc_ref[sb, pl.ds(t, 1), :] = sums[:1]


def spread(scratch, q, values):
    for g in range(scratch.shape[0]):
        scratch[g, pl.ds(q * CHUNK, CHUNK), :] = values[:, g * LANES : (g + 1) * LANES]


def collect(ref, q, scratch):
    for g in range(scratch.shape[0]):
        ref[q, :, pl.ds(g * LANES, LANES)] = scratch[g, pl.ds(q * CHUNK, CHUNK), :]


def tree(values):
    while len(values) > 1:
        values = [a + b for a, b in zip(values[::2], values[1::2])]
    return values[0]


def softplus(v):
    return jnp.maximum(v, 0.0) + jnp.log1p(jnp.exp(-jnp.abs(v)))


def dt_products(dt_ref, wdt_ref, chan_ref, q):
    return dot(dt_ref[q], wdt_ref[...], ((1,), (1,))) + chan_ref[pl.ds(KCONV + NSTATE + 1, 1), :]


def scan_fwd_kernel(
    dt_ref, mask_ref, conv_ref, bc_ref, rate_ref, wdt_ref, chan_ref, y_ref, starts_ref, state, bx, stepm, drive, ys
):
    seqs = dt_ref.shape[0]
    width = conv_ref.shape[2]

    @pl.when(pl.program_id(0) == 0)
    def _():
        state[...] = jnp.zeros_like(state)

    starts_ref[0] = state[...]
    for q in range(seqs):
        step = softplus(dt_products(dt_ref, wdt_ref, chan_ref, q))
        spread(stepm, q, step + mask_ref[q, :, pl.ds(KCONV - 1, 1)])
        spread(drive, q, step * conv_ref[q].astype(f32))
    for sb in range(seqs // SUBS):
        expand_inputs(bc_ref, bx, sb)
        sub = pl.ds(sb * SUBS, SUBS)

        def group(g, carry):
            lanes = pl.ds(pl.multiple_of(g * LANES, LANES), LANES)
            rates = [rate_ref[n, :, lanes] * LOG2E for n in range(NSTATE)]

            def token(t, st):
                rows = pl.ds(sb * SUBS * CHUNK + t, SUBS, stride=CHUNK)
                sm = stepm[g, rows, :]
                dx = drive[g, rows, :]
                parts = []
                out = []
                for n in range(NSTATE):
                    dec = jnp.exp2(sm * rates[n])
                    s_n = dec * st[n] + dx * bx[t, n]
                    out.append(s_n)
                    parts.append(s_n * bx[t, NSTATE + n])
                ys[g, rows, :] = tree(parts)
                return tuple(out)

            st = tuple(state[n, sub, lanes] for n in range(NSTATE))
            st = lax.fori_loop(0, CHUNK, token, st, unroll=FWD_UNROLL)
            for n in range(NSTATE):
                state[n, sub, lanes] = st[n]
            return carry

        lax.fori_loop(0, width // LANES, group, 0)
    for q in range(seqs):
        collect(y_ref, q, ys)


def scan_bwd_kernel(
    dt_ref, mask_ref, conv_ref, bc_ref, rate_ref, wdt_ref, chan_ref, starts_ref, gy_ref,
    gconv_ref, glow_ref, gdtin_ref, gbc_ref, grate_ref, gbias_ref,
    flow, bx, stepm, step2, conv2, gy2, gs2, gc2, dec_s, pri_s, acc,
):
    seqs = dt_ref.shape[0]
    width = conv_ref.shape[2]

    @pl.when(pl.program_id(0) == 0)
    def _():
        flow[...] = jnp.zeros_like(flow)
        grate_ref[...] = jnp.zeros_like(grate_ref)
        gbias_ref[...] = jnp.zeros_like(gbias_ref)

    for q in range(seqs):
        step = softplus(dt_products(dt_ref, wdt_ref, chan_ref, q))
        spread(step2, q, step)
        spread(stepm, q, step + mask_ref[q, :, pl.ds(KCONV - 1, 1)])
        spread(conv2, q, conv_ref[q].astype(f32))
        spread(gy2, q, gy_ref[q])
    for sb in range(seqs // SUBS):
        expand_inputs(bc_ref, bx, sb)
        sub = pl.ds(sb * SUBS, SUBS)
        acc[...] = jnp.zeros_like(acc)

        def group(g, carry):
            lanes = pl.ds(pl.multiple_of(g * LANES, LANES), LANES)

            def token_f(t, st):
                rows = pl.ds(sb * SUBS * CHUNK + t, SUBS, stride=CHUNK)
                sm = stepm[g, rows, :]
                dx = step2[g, rows, :] * conv2[g, rows, :]
                out = []
                for n in range(NSTATE):
                    dec = jnp.exp2(sm * (rate_ref[n, :, lanes] * LOG2E))
                    dec_s[t, n] = dec
                    pri_s[t, n] = st[n]
                    out.append(dec * st[n] + dx * bx[t, n])
                return tuple(out)

            st = tuple(starts_ref[0, n, sub, lanes] for n in range(NSTATE))
            st = lax.fori_loop(0, CHUNK, token_f, st, unroll=FWD_UNROLL)
            for n in range(NSTATE):
                pri_s[CHUNK, n] = st[n]

            def token_b(i, carried):
                t = CHUNK - 1 - i
                fl, ga = carried
                rows = pl.ds(sb * SUBS * CHUNK + t, SUBS, stride=CHUNK)
                size = step2[g, rows, :]
                conv = conv2[g, rows, :]
                gy = gy2[g, rows, :]
                dx = size * conv
                along, gsz = [], []
                nfl, nga = [], []
                for n in range(NSTATE):
                    grad = gy * bx[t, NSTATE + n] + fl[n]
                    dg = dec_s[t, n] * grad
                    th = dg * pri_s[t, n]
                    along.append(grad * bx[t, n])
                    gsz.append(th * rate_ref[n, :, lanes])
                    acc[t, n] += grad * dx
                    acc[t, NSTATE + n] += pri_s[t + 1, n] * gy
                    nfl.append(dg)
                    nga.append(ga[n] + th * size)
                along = tree(along)
                gs2[g, rows, :] = tree(gsz) + conv * along
                gc2[g, rows, :] = size * along
                return (tuple(nfl), tuple(nga))

            fl = tuple(flow[n, sub, lanes] for n in range(NSTATE))
            ga = tuple(grate_ref[n, :, lanes] for n in range(NSTATE))
            fl, ga = lax.fori_loop(0, CHUNK, token_b, (fl, ga), unroll=BWD_UNROLL)
            for n in range(NSTATE):
                flow[n, sub, lanes] = fl[n]
                grate_ref[n, :, lanes] = ga[n]
            return carry

        lax.fori_loop(0, width // LANES, group, 0)
        lane_sums(acc, gbc_ref, sb)
    skip = chan_ref[pl.ds(KCONV + NSTATE + 2, 1), :]
    for q in range(seqs):
        collect(gconv_ref, q, gc2)
        gconv_ref[q] += skip * gy_ref[q]
        gstep = jnp.concatenate([gs2[g, pl.ds(q * CHUNK, CHUNK), :] for g in range(width // LANES)], axis=1)
        grad = gstep * jax.nn.sigmoid(dt_products(dt_ref, wdt_ref, chan_ref, q))
        gbias_ref[...] += jnp.sum(grad.reshape(CHUNK // SUBS, SUBS, width), axis=0)
        low = grad.astype(bf16)
        glow_ref[q] = low
        gdtin_ref[q] = dot(low, wdt_ref[...], ((1,), (0,)))


def whole(shape):
    return pl.BlockSpec(shape, lambda i, *_: (0,) * len(shape))


def scan_specs(seqs, width, chan_cols, chunk_of):
    def tokens(columns):
        return pl.BlockSpec((seqs, CHUNK, columns), lambda i: (0, chunk_of(i), 0))

    bcs = pl.BlockSpec((1, 2 * NSTATE, seqs, CHUNK), lambda i: (chunk_of(i), 0, 0, 0))
    starts = pl.BlockSpec((1, NSTATE, seqs, width), lambda i: (chunk_of(i), 0, 0, 0))
    sums = pl.BlockSpec((seqs // SUBS, CHUNK, 2 * NSTATE * SUBS), lambda i: (0, chunk_of(i), 0))
    ins = [
        tokens(RANK), tokens(MASKS), tokens(width), bcs,
        whole((NSTATE, SUBS, width)), whole((width, RANK)), whole((chan_cols, width)),
    ]
    return tokens, starts, sums, ins


def scan_forward(dt_in, masks, conv, bc, rates, w_dt, chan):
    seqs, length, width = conv.shape
    chunks = length // CHUNK
    tokens, starts, _, ins = scan_specs(seqs, width, chan.shape[0], lambda i: i)
    tall = pltpu.VMEM((width // LANES, seqs * CHUNK, LANES), f32)
    return pl.pallas_call(
        scan_fwd_kernel,
        grid=(chunks,),
        in_specs=ins,
        out_specs=[tokens(width), starts],
        out_shape=[
            jax.ShapeDtypeStruct(conv.shape, f32),
            jax.ShapeDtypeStruct((chunks, NSTATE, seqs, width), f32),
        ],
        scratch_shapes=[
            pltpu.VMEM((NSTATE, seqs, width), f32),
            pltpu.VMEM((CHUNK, 2 * NSTATE, SUBS, LANES), f32),
            tall, tall, tall,
        ],
        compiler_params=pltpu.CompilerParams(vmem_limit_bytes=50 * 2**20),
        cost_estimate=pl.CostEstimate(
            flops=8 * conv.size * NSTATE, bytes_accessed=100 * 10**6, transcendentals=conv.size * NSTATE
        ),
        name="scan_forward",
    )(dt_in, masks, conv, bc, rates, w_dt, chan)


def scan_backward(dt_in, masks, conv, bc, rates, w_dt, chan, starts, grad_y):
    seqs, length, width = conv.shape
    chunks = length // CHUNK
    tokens, start_spec, sums, ins = scan_specs(seqs, width, chan.shape[0], lambda i: chunks - 1 - i)
    tall = pltpu.VMEM((width // LANES, seqs * CHUNK, LANES), f32)
    return pl.pallas_call(
        scan_bwd_kernel,
        grid=(chunks,),
        in_specs=ins + [start_spec, tokens(width)],
        out_specs=[
            tokens(width), tokens(width), tokens(RANK), sums,
            whole((NSTATE, SUBS, width)), whole((SUBS, width)),
        ],
        out_shape=[
            jax.ShapeDtypeStruct(conv.shape, f32),
            jax.ShapeDtypeStruct(conv.shape, bf16),
            jax.ShapeDtypeStruct((seqs, length, RANK), f32),
            jax.ShapeDtypeStruct((seqs // SUBS, length, 2 * NSTATE * SUBS), f32),
            jax.ShapeDtypeStruct((NSTATE, SUBS, width), f32),
            jax.ShapeDtypeStruct((SUBS, width), f32),
        ],
        scratch_shapes=[
            pltpu.VMEM((NSTATE, seqs, width), f32),
            pltpu.VMEM((CHUNK, 2 * NSTATE, SUBS, LANES), f32),
            tall, tall, tall, tall, tall, tall,
            pltpu.VMEM((CHUNK, NSTATE, SUBS, LANES), f32),
            pltpu.VMEM((CHUNK + 1, NSTATE, SUBS, LANES), f32),
            pltpu.VMEM((CHUNK, 2 * NSTATE, SUBS, LANES), f32),
        ],
        compiler_params=pltpu.CompilerParams(vmem_limit_bytes=56 * 2**20),
        cost_estimate=pl.CostEstimate(
            flops=24 * conv.size * NSTATE, bytes_accessed=300 * 10**6, transcendentals=conv.size * NSTATE
        ),
        name="scan_backward",
    )(dt_in, masks, conv, bc, rates, w_dt, chan, starts, grad_y)


def put_blocks(place_ref, blocks, out):
    @pl.when(pl.program_id(0) == 0)
    def _():
        for k, block in enumerate(blocks):
            rows = block.shape[0]
            out[pl.ds(pl.multiple_of((place_ref[2] ^ k) * rows, rows), rows), :] = block[...]


def normalised(hid):
    residual = hid.astype(f32)
    return residual * lax.rsqrt(jnp.mean(residual * residual, axis=1, keepdims=True) + norm_eps)


def earlier_rows(inner, masks):
    terms = []
    for k in range(KCONV - 1):
        terms.append(pltpu.roll(inner, KCONV - 1 - k, 0) * masks[:, k : k + 1])
    return terms + [inner]


def conv_sum(terms, chan_ref):
    total = chan_ref[pl.ds(KCONV + NSTATE, 1), :]
    for k, term in enumerate(terms):
        total = total + chan_ref[pl.ds(k, 1), :] * term
    return total


def put_columns(ref, start, values):
    count = values.shape[0]
    for i in range(values.shape[1] // LANES):
        ref[0, pl.ds(start + i * count, count), :] = values[:, i * LANES : (i + 1) * LANES]


def front_kernel(planes, place_ref, hid_ref, gain_ref, mask_ref, chan_ref, wx_ref, wbc_ref, *refs):
    blocks = refs[:planes]
    normed_ref, inner_ref, conv_ref, proj_ref, weights = refs[planes:]
    put_blocks(place_ref, blocks, weights)
    normed = (normalised(hid_ref[0]) * gain_ref[...]).astype(bf16)
    normed_ref[0] = normed
    inner = dot(normed, weights[...], ((1,), (0,)))
    inner_ref[0] = inner
    pre = conv_sum(earlier_rows(inner, mask_ref[0]), chan_ref)
    conv = jax.nn.silu(pre).astype(bf16)
    conv_ref[0] = conv
    length = conv.shape[0]
    proj_ref[0, pl.ds(0, length), :] = dot(conv, wx_ref[...], ((1,), (1,)))
    put_columns(proj_ref, length, dot(wbc_ref[...], conv, ((1,), (1,))))


def per_sequence(kernel, place, stacked, fixed, outs, scratch, flops, name):
    seqs = stacked[0].shape[0]

    def block(shape):
        return pl.BlockSpec((1,) + tuple(shape[1:]), lambda i, p: (i, 0, 0))

    return pl.pallas_call(
        kernel,
        grid_spec=pltpu.PrefetchScalarGridSpec(
            num_scalar_prefetch=1,
            grid=(seqs,),
            in_specs=[block(v.shape) for v in stacked] + [whole(v.shape) for v in fixed],
            out_specs=[block(shape) if per else whole(shape) for shape, _, per in outs],
            scratch_shapes=scratch,
        ),
        out_shape=[jax.ShapeDtypeStruct(shape, kind) for shape, kind, _ in outs],
        compiler_params=pltpu.CompilerParams(vmem_limit_bytes=56 * 2**20),
        cost_estimate=pl.CostEstimate(flops=flops, bytes_accessed=40 * 10**6, transcendentals=0),
        name=name,
    )(place, *stacked, *fixed)


def front(place, hidden_all, gain, masks, chan, w_xdt, w_xbc, inner_blocks):
    seqs, length, model = hidden_all.shape
    width = w_xbc.shape[1]
    packed = length + 2 * NSTATE * length // LANES

    def kernel(place_ref, hid, mask, gain_ref, chan_ref, wx, wbc, *refs):
        front_kernel(len(inner_blocks), place_ref, hid, gain_ref, mask, chan_ref, wx, wbc, *refs)

    return per_sequence(
        kernel,
        place,
        [hidden_all, masks],
        [gain, chan, w_xdt, w_xbc, *inner_blocks],
        [
            ((seqs, length, model), bf16, True),
            ((seqs, length, width), f32, True),
            ((seqs, length, width), bf16, True),
            ((seqs, packed, RANK), f32, True),
        ],
        [pltpu.VMEM((model, width), bf16)],
        2 * seqs * length * model * width,
        "front",
    )


def middle(place, normed, upstream, scanned, conv_out, chan, gate_blocks, out_blocks):
    seqs, length, model = normed.shape
    width = conv_out.shape[2]
    planes = len(gate_blocks)

    def kernel(place_ref, normed_ref, up_ref, y_ref, conv_ref, chan_ref, *refs):
        gates, outs = refs[:planes], refs[planes : 2 * planes]
        part_ref, mixed_ref, gy_ref, ggate_ref, gskip_ref, w_gate, w_out = refs[2 * planes :]
        put_blocks(place_ref, gates, w_gate)
        put_blocks(place_ref, outs, w_out)

        @pl.when(pl.program_id(0) == 0)
        def _():
            gskip_ref[...] = jnp.zeros_like(gskip_ref)

        gate = dot(normed_ref[0], w_gate[...], ((1,), (0,)))
        conv = conv_ref[0].astype(f32)
        sigma = jax.nn.sigmoid(gate)
        act = gate * sigma
        mixer = y_ref[0] + chan_ref[pl.ds(KCONV + NSTATE + 2, 1), :] * conv
        mixed = (mixer * act).astype(bf16)
        mixed_ref[0] = mixed
        part_ref[0] = dot(mixed, w_out[...], ((1,), (0,))).astype(part_ref.dtype)
        grad_mixed = dot(up_ref[0], w_out[...], ((1,), (1,)))
        gy = grad_mixed * act
        gy_ref[0] = gy
        ggate_ref[0] = (grad_mixed * mixer * (sigma * (1.0 + gate * (1.0 - sigma)))).astype(bf16)
        gskip_ref[...] += jnp.sum((gy * conv).reshape(length // SUBS, SUBS, width), axis=0)

    return per_sequence(
        kernel,
        place,
        [normed, upstream, scanned, conv_out],
        [chan, *gate_blocks, *out_blocks],
        [
            ((seqs, length, model), PARTS, True),
            ((seqs, length, width), bf16, True),
            ((seqs, length, width), f32, True),
            ((seqs, length, width), bf16, True),
            ((SUBS, width), f32, False),
        ],
        [pltpu.VMEM((model, width), bf16), pltpu.VMEM((width, model), bf16)],
        6 * seqs * length * model * width,
        "middle",
    )


def back_conv(place, grad_conv, gp_dt, gp_bc, inner, masks, chan, w_xdt, w_xbc):
    seqs, length, width = grad_conv.shape

    def kernel(place_ref, gconv_ref, gdt_ref, gbc_ref, inner_ref, mask_ref, chan_ref, wx_ref, wbc_ref, ginner_ref, sums_ref):
        @pl.when(pl.program_id(0) == 0)
        def _():
            sums_ref[...] = jnp.zeros_like(sums_ref)

        masks_now = mask_ref[0]
        terms = earlier_rows(inner_ref[0], masks_now)
        pre = conv_sum(terms, chan_ref)
        total = gconv_ref[0] + dot(gdt_ref[0], wx_ref[...], ((1,), (0,)))
        total = total + dot(gbc_ref[0], wbc_ref[...], ((0,), (0,)))
        grad = total * silu_slope(pre)
        for k in range(KCONV):
            sums_ref[k] += jnp.sum((grad * terms[k]).reshape(length // SUBS, SUBS, width), axis=0)
        sums_ref[KCONV] += jnp.sum(grad.reshape(length // SUBS, SUBS, width), axis=0)
        ginner = chan_ref[pl.ds(KCONV - 1, 1), :] * grad
        for k in range(KCONV - 1):
            moved = pltpu.roll(grad * masks_now[:, k : k + 1], length - (KCONV - 1 - k), 0)
            ginner = ginner + chan_ref[pl.ds(k, 1), :] * moved
        ginner_ref[0] = ginner.astype(bf16)

    return per_sequence(
        kernel,
        place,
        [grad_conv, gp_dt, gp_bc, inner, masks],
        [chan, w_xdt, w_xbc],
        [((seqs, length, width), bf16, True), ((KCONV + 1, SUBS, width), f32, False)],
        [],
        2 * seqs * length * width * RANK,
        "back_conv",
    )


def back_normed(place, grad_inner, grad_gate, hidden_all, inner_blocks, gate_blocks):
    seqs, length, width = grad_inner.shape
    model = hidden_all.shape[2]
    planes = len(gate_blocks)

    def kernel(place_ref, ginner_ref, ggate_ref, hid_ref, *refs):
        inners, gates = refs[:planes], refs[planes : 2 * planes]
        part_ref, ggain_ref, w_inner, w_gate = refs[2 * planes :]
        put_blocks(place_ref, inners, w_inner)
        put_blocks(place_ref, gates, w_gate)

        @pl.when(pl.program_id(0) == 0)
        def _():
            ggain_ref[...] = jnp.zeros_like(ggain_ref)

        part = dot(ginner_ref[0], w_inner[...], ((1,), (1,))) + dot(ggate_ref[0], w_gate[...], ((1,), (1,)))
        part_ref[0] = part.astype(part_ref.dtype)
        ggain_ref[...] += jnp.sum((part * normalised(hid_ref[0])).reshape(length // SUBS, SUBS, model), axis=0)

    return per_sequence(
        kernel,
        place,
        [grad_inner, grad_gate, hidden_all],
        [*inner_blocks, *gate_blocks],
        [((seqs, length, model), PARTS, True), ((SUBS, model), f32, False)],
        [pltpu.VMEM((model, width), bf16), pltpu.VMEM((model, width), bf16)],
        4 * seqs * length * model * width,
        "back_normed",
    )


MESH = pl.DeviceIdType.MESH


class Peers:
    def __init__(self):
        self.r = lax.axis_index("rep")
        shard = lax.axis_index("shard")
        self.z, self.c = shard // 2, shard % 2

    @staticmethod
    def flip(i, k):
        return (i, i + 1 - 2 * (i % 2), (i + 2) % 4, 3 - i)[k]

    def rep(self, k):
        return {"rep": self.flip(self.r, k)}

    def plane(self, k):
        return {"shard": 2 * self.flip(self.z, k) + self.c}

    def core(self):
        return {"shard": 2 * self.z + 1 - self.c}

    def greet(self, planes):
        devices = [self.core()] + [self.rep(k) for k in (1, 2, 3)]
        if planes:
            devices += [self.plane(k) for k in (1, 2, 3)]
        barrier = pltpu.get_barrier_semaphore()
        for device in devices:
            pl.semaphore_signal(barrier, inc=1, device_id=device, device_id_type=MESH)
        pl.semaphore_wait(barrier, len(devices))


class Sends:
    def __init__(self, send_sems, recv_sems):
        self.send_sems, self.recv_sems = send_sems, recv_sems
        self.made = {}

    def make(self, slot, source, target, device):
        copy = pltpu.make_async_remote_copy(
            src_ref=source,
            dst_ref=target,
            send_sem=self.send_sems.at[slot],
            recv_sem=self.recv_sems.at[slot],
            device_id=device,
            device_id_type=MESH,
        )
        self.made[slot] = copy
        return copy

    def start(self, slot, source, target, device):
        self.make(slot, source, target, device).start()

    def arrived(self, *slots):
        for slot in slots:
            self.made[slot].wait_recv()

    def sent(self, *slots):
        for slot in slots:
            self.made[slot].wait_send()


def gather_first_kernel(
    hid, in_own, in_other, small, gain, ids, hid_all, weights, small_all, gain_all, ids_all, send_sems, recv_sems, local_sems
):
    me = Peers()
    net = Sends(send_sems, recv_sems)
    rows = in_own.shape[0]
    half = hid.shape[0] // 2
    low, high = pl.ds(0, half), pl.ds(half, half)
    inside = (me.z == 1) | (me.z == 2)
    outside = (me.z == 0) | (me.z == 3)
    mine = pl.ds(pl.multiple_of(me.c * rows, rows), rows)
    local = [
        pltpu.make_async_copy(source, target, local_sems.at[i])
        for i, (source, target) in enumerate(
            [
                (in_own, weights.at[0, mine]),
                (hid, hid_all.at[0]),
                (small, small_all.at[0]),
                (gain, gain_all.at[0]),
                (ids, ids_all.at[0]),
            ]
        )
    ]
    for copy in local:
        copy.start()
    me.greet(True)
    net.start(0, in_other, weights.at[0, mine], me.core())
    for k in (1, 2, 3):
        net.start(k, ids, ids_all.at[k], me.rep(k))
        net.start(3 + k, gain, gain_all.at[k], me.plane(k))
        net.start(6 + k, small, small_all.at[k], me.plane(k))
    net.start(10, hid.at[high], hid_all.at[1, high], me.rep(1))
    net.start(11, hid.at[low], hid_all.at[2, low], me.rep(2))
    net.start(12, hid.at[low], hid_all.at[1, low], me.rep(1))
    net.start(13, hid.at[high], hid_all.at[2, high], me.rep(2))
    net.start(14, hid, hid_all.at[4], me.core())
    local[0].wait()
    net.arrived(0)
    own = weights.at[0]
    net.start(15, own, weights.at[2], me.plane(2))
    net.start(16, own, weights.at[1], me.plane(1))
    across = net.make(17, own, weights.at[3], me.plane(3))
    local[3].wait()
    local[4].wait()
    net.arrived(1, 2, 3, 4, 5, 6)
    net.start(18, ids_all.at[pl.ds(0, 4)], ids_all.at[pl.ds(4, 4)], me.core())
    net.start(19, gain_all.at[pl.ds(0, 4)], gain_all.at[pl.ds(4, 4)], me.core())
    net.arrived(10, 11)
    net.start(20, hid_all.at[1, high], hid_all.at[3, high], me.rep(2))
    net.start(21, hid_all.at[2, low], hid_all.at[3, low], me.rep(1))
    net.arrived(12)
    net.start(22, hid_all.at[1], hid_all.at[5], me.core())
    net.arrived(13)
    net.start(23, hid_all.at[2], hid_all.at[6], me.core())
    net.arrived(15)
    onward = net.make(24, weights.at[2], weights.at[3], me.plane(1))

    @pl.when(inside)
    def _():
        across.start()
        onward.start()

    net.arrived(20, 21)
    net.start(25, hid_all.at[3], hid_all.at[7], me.core())
    net.arrived(16)

    @pl.when(inside)
    def _():
        across.wait_recv()

    @pl.when(outside)
    def _():
        onward.wait_recv()

    net.arrived(7, 8, 9, 14, 18, 19, 22, 23, 25)
    local[1].wait()
    local[2].wait()
    net.sent(*[slot for slot in net.made if slot not in (17, 24)])

    @pl.when(inside)
    def _():
        across.wait_send()
        onward.wait_send()


def gather_first(hid, in_own, in_other, small, gain, ids):
    length, model = hid.shape
    anywhere = pl.BlockSpec(memory_space=pl.ANY)
    return pl.pallas_call(
        gather_first_kernel,
        in_specs=[anywhere] * 6,
        out_specs=[anywhere] * 5,
        out_shape=[
            jax.ShapeDtypeStruct((8, length, model), bf16),
            jax.ShapeDtypeStruct((4, 2 * in_own.shape[0], in_own.shape[1]), bf16),
            jax.ShapeDtypeStruct((4,) + small.shape, bf16),
            jax.ShapeDtypeStruct((8,) + gain.shape, f32),
            jax.ShapeDtypeStruct((8,) + ids.shape, f32),
        ],
        scratch_shapes=[
            pltpu.SemaphoreType.DMA((26,)),
            pltpu.SemaphoreType.DMA((26,)),
            pltpu.SemaphoreType.DMA((5,)),
        ],
        compiler_params=pltpu.CompilerParams(collective_id=1, has_side_effects=True),
        cost_estimate=pl.CostEstimate(flops=0, bytes_accessed=100 * 10**6, transcendentals=0),
        name="gather_first",
    )(hid, in_own, in_other, small, gain, ids)


def reduce_plane_kernel(part, dt_all, bc_all, near, pair, far, send_sems, recv_sems):
    me = Peers()
    net = Sends(send_sems, recv_sems)
    tokens = dt_all.shape[1]
    me.greet(False)
    for k in (1, 2, 3, 0):
        net.start(k, part.at[4 + k], near.at[k], me.core())
    for k in (1, 2, 3):
        net.arrived(k)
        pair[k - 1] = part[k] + near[k]
        net.start(3 + k, pair.at[k - 1], far.at[k - 1], me.rep(k))
    net.arrived(0)
    total = part[0] + near[0]
    for k in (1, 2, 3):
        net.arrived(3 + k)
        total = total + far[k - 1]
    dt_all[0] = total[:tokens].astype(bf16)
    bc_all[0] = total[tokens:]
    for k in (1, 2, 3):
        net.start(6 + k, dt_all.at[0], dt_all.at[k], me.rep(k))
        net.start(9 + k, bc_all.at[0], bc_all.at[k], me.rep(k))
    net.start(13, dt_all.at[0], dt_all.at[4], me.core())
    net.start(14, bc_all.at[0], bc_all.at[4], me.core())
    for k in (1, 2, 3):
        net.arrived(6 + k, 9 + k)
        net.start(14 + k, dt_all.at[k], dt_all.at[4 + k], me.core())
        net.start(17 + k, bc_all.at[k], bc_all.at[4 + k], me.core())
    net.arrived(13, 14, 15, 16, 17, 18, 19, 20)
    net.sent(*net.made)


def reduce_plane(part, collective):
    seqs, rows, _ = part.shape
    tokens = rows - 2 * 2 * NSTATE
    vmem = pl.BlockSpec(memory_space=pltpu.VMEM)
    return pl.pallas_call(
        reduce_plane_kernel,
        in_specs=[vmem],
        out_specs=[vmem, vmem],
        out_shape=[
            jax.ShapeDtypeStruct((seqs, tokens, RANK), bf16),
            jax.ShapeDtypeStruct((seqs, rows - tokens, RANK), f32),
        ],
        scratch_shapes=[
            pltpu.VMEM((4, rows, RANK), f32),
            pltpu.VMEM((3, rows, RANK), f32),
            pltpu.VMEM((3, rows, RANK), f32),
            pltpu.SemaphoreType.DMA((21,)),
            pltpu.SemaphoreType.DMA((21,)),
        ],
        compiler_params=pltpu.CompilerParams(
            collective_id=collective, has_side_effects=True, vmem_limit_bytes=16 * 2**20
        ),
        cost_estimate=pl.CostEstimate(flops=0, bytes_accessed=50 * 10**6, transcendentals=0),
        name="reduce_plane",
    )(part)


def finish_kernel(
    part, gin, small, grad_normed, pieces, small_all,
    own_part, core_part, pair, far_one, far_two, from_one, from_two,
    blocks, ends, middle_block, block_one, block_two, two_out, total, small_own, small_in, small_total,
    send_sems, recv_sems, local_sems,
):
    me = Peers()
    net = Sends(send_sems, recv_sems)
    half = part.shape[1] // 2
    low, high = pl.ds(0, half), pl.ds(half, half)
    rows = gin.shape[0] // 4
    small_rows = small.shape[0] // 4
    own_rows = rows // 2
    inside = (me.z == 1) | (me.z == 2)
    outside = (me.z == 0) | (me.z == 3)

    def block(ref, k, size):
        return ref.at[pl.ds(pl.multiple_of(me.flip(me.z, k) * size, size), size)]

    local = [
        pltpu.make_async_copy(part.at[pl.ds(0, 4)], own_part, local_sems.at[0]),
        pltpu.make_async_copy(block(gin, 0, rows), blocks.at[0], local_sems.at[1]),
        pltpu.make_async_copy(block(gin, 2, rows), blocks.at[1], local_sems.at[2]),
        pltpu.make_async_copy(block(small, 0, small_rows), small_own, local_sems.at[3]),
    ]
    for copy in local:
        copy.start()
    me.greet(True)
    for i, k in enumerate((3, 1, 2, 0)):
        net.start(i, part.at[4 + k], core_part.at[k], me.core())
    for k in (1, 2, 3):
        net.start(3 + k, block(small, k, small_rows), small_in.at[k - 1], me.plane(k))
    to_ends = net.make(7, block(gin, 3, rows), ends, me.plane(1))
    to_middle = net.make(8, block(gin, 3, rows), middle_block, me.plane(3))

    @pl.when(outside)
    def _():
        to_ends.start()

    @pl.when(inside)
    def _():
        to_middle.start()

    two = net.make(9, two_out, block_two, me.plane(2))
    local[2].wait()

    @pl.when(outside)
    def _():
        two_out[...] = blocks[1]
        two.start()

    net.start(10, block(gin, 1, rows), block_one, me.plane(1))
    local[0].wait()
    for i, k in enumerate((3, 1, 2)):
        net.arrived(i)
        pair[k - 1] = (own_part[k].astype(f32) + core_part[k].astype(f32)).astype(bf16)
        if k == 3:
            net.start(11, pair.at[2, low], far_one, me.rep(1))
            net.start(12, pair.at[2, high], far_two, me.rep(2))
        elif k == 1:
            net.start(13, pair.at[0, low], from_one.at[low], me.rep(1))
        else:
            net.start(14, pair.at[1, high], from_two.at[high], me.rep(2))

    @pl.when(inside)
    def _():
        to_ends.wait_recv()
        two_out[...] = (blocks[1].astype(f32) + ends[...].astype(f32)).astype(bf16)
        two.start()

    net.arrived(11)
    pair[1, low] = (pair[1, low].astype(f32) + far_one[...].astype(f32)).astype(bf16)
    net.start(15, pair.at[1, low], from_two.at[low], me.rep(2))
    net.arrived(12)
    pair[0, high] = (pair[0, high].astype(f32) + far_two[...].astype(f32)).astype(bf16)
    net.start(16, pair.at[0, high], from_one.at[high], me.rep(1))
    local[3].wait()
    net.arrived(4, 5, 6)
    small_total[...] = small_own[...] + small_in[0] + small_in[1] + small_in[2]
    kept_small = pltpu.make_async_copy(small_total, small_all.at[0], local_sems.at[4])
    kept_small.start()
    for k in (1, 2, 3):
        net.start(16 + k, small_total, small_all.at[k], me.rep(k))
    local[1].wait()
    net.arrived(10, 9)
    summed = blocks[0].astype(f32) + block_one[...].astype(f32) + block_two[...].astype(f32)

    @pl.when(inside)
    def _():
        to_middle.wait_recv()
        total[...] = (summed + middle_block[...].astype(f32)).astype(bf16)

    @pl.when(outside)
    def _():
        total[...] = summed.astype(bf16)

    mine = total.at[pl.ds(pl.multiple_of(me.c * own_rows, own_rows), own_rows)]
    other = total.at[pl.ds(pl.multiple_of((1 - me.c) * own_rows, own_rows), own_rows)]
    net.start(20, other, pieces.at[1, 0], me.core())
    kept = pltpu.make_async_copy(mine, pieces.at[0, 0], local_sems.at[5])
    kept.start()
    for k in (1, 2, 3):
        net.start(20 + k, mine, pieces.at[0, k], me.rep(k))
    net.arrived(20)
    for k in (1, 2, 3):
        net.start(23 + k, pieces.at[1, 0], pieces.at[1, k], me.rep(k))
    net.arrived(3)
    net.arrived(13, 14, 15, 16)
    grad_normed[...] = (
        own_part[0].astype(f32) + core_part[0].astype(f32) + from_one[...].astype(f32) + from_two[...].astype(f32)
    )
    net.arrived(17, 18, 19, 21, 22, 23, 24, 25, 26)
    kept.wait()
    kept_small.wait()
    net.sent(*[slot for slot in net.made if slot not in (7, 8)])

    @pl.when(outside)
    def _():
        to_ends.wait_send()

    @pl.when(inside)
    def _():
        to_middle.wait_send()


def finish(part, gin, small):
    _, length, model = part.shape
    rows, width = gin.shape[0] // 4, gin.shape[1]
    small_rows, cols = small.shape[0] // 4, small.shape[1]
    anywhere = pl.BlockSpec(memory_space=pl.ANY)
    big = (length, model)
    return pl.pallas_call(
        finish_kernel,
        in_specs=[anywhere] * 3,
        out_specs=[pl.BlockSpec(memory_space=pltpu.VMEM), anywhere, anywhere],
        out_shape=[
            jax.ShapeDtypeStruct(big, f32),
            jax.ShapeDtypeStruct((2, 4, rows // 2, width), bf16),
            jax.ShapeDtypeStruct((4, small_rows, cols), f32),
        ],
        scratch_shapes=[
            pltpu.VMEM((4,) + big, bf16),
            pltpu.VMEM((4,) + big, bf16),
            pltpu.VMEM((3,) + big, bf16),
            pltpu.VMEM((length // 2, model), bf16),
            pltpu.VMEM((length // 2, model), bf16),
            pltpu.VMEM(big, bf16),
            pltpu.VMEM(big, bf16),
            pltpu.VMEM((2, rows, width), bf16),
            pltpu.VMEM((rows, width), bf16),
            pltpu.VMEM((rows, width), bf16),
            pltpu.VMEM((rows, width), bf16),
            pltpu.VMEM((rows, width), bf16),
            pltpu.VMEM((rows, width), bf16),
            pltpu.VMEM((rows, width), bf16),
            pltpu.VMEM((small_rows, cols), f32),
            pltpu.VMEM((3, small_rows, cols), f32),
            pltpu.VMEM((small_rows, cols), f32),
            pltpu.SemaphoreType.DMA((27,)),
            pltpu.SemaphoreType.DMA((27,)),
            pltpu.SemaphoreType.DMA((6,)),
        ],
        compiler_params=pltpu.CompilerParams(
            collective_id=4, has_side_effects=True, vmem_limit_bytes=40 * 2**20
        ),
        cost_estimate=pl.CostEstimate(flops=0, bytes_accessed=150 * 10**6, transcendentals=0),
        name="finish",
    )(part, gin, small)


class Links:
    def __init__(self, reps, shard_size):
        self.reps, self.shard_size = reps, shard_size
        self.planes = shard_size // 2
        self.r = lax.axis_index("rep")
        shard = lax.axis_index("shard")
        self.plane, self.c = shard // 2, shard % 2

    def rep(self, value, k):
        return lax.ppermute(value, "rep", [(i, i ^ k) for i in range(self.reps)])

    def core(self, value):
        return lax.ppermute(value, "shard", [(i, i ^ 1) for i in range(self.shard_size)])

    def planes_pairs(self, pairs):
        return [(2 * a + core, 2 * b + core) for a, b in pairs for core in range(2)]

    def z(self, value, pairs):
        return lax.ppermute(value, "shard", self.planes_pairs(pairs))

    def z_xor(self, value, k):
        return self.z(value, [(i, i ^ k) for i in range(self.planes)])

    def gather_rep(self, value):
        if self.reps != 4:
            return [value] + [self.rep(value, k) for k in range(1, self.reps)]
        half = value.shape[0] // 2
        one, two = self.rep(value, 1), self.rep(value, 2)
        return [value, one, two, self.across(one, two, half)]

    def gather_near(self, value):
        return [value] + [self.rep(value, k) for k in ((1, 2) if self.reps == 4 else range(1, self.reps))]

    def gather_far(self, near):
        return [self.across(near[1], near[2], near[0].shape[0] // 2)] if self.reps == 4 else []

    def across(self, one, two, half):
        return jnp.concatenate([self.rep(two[:half], 1), self.rep(one[half:], 2)], axis=0)

    def gather_plane(self, value):
        near = jnp.stack([value] + [self.rep(value, k) for k in range(1, self.reps)])
        return jnp.concatenate([near, self.core(near)], axis=0)

    def scatter_plane(self, partial, wire):
        reps = self.reps
        pair = partial[:reps].astype(f32) + self.core(partial[reps:].astype(wire)).astype(f32)
        total = pair[0]
        for k in range(1, reps):
            total = total + self.rep(pair[k].astype(wire), k).astype(f32)
        return total

    def place_z(self, values):
        rows = values[0].shape[0]
        out = jnp.zeros((self.planes * rows,) + values[0].shape[1:], values[0].dtype)
        start = (0,) * (values[0].ndim - 1)
        for k, value in enumerate(values):
            out = lax.dynamic_update_slice(out, value, ((self.plane ^ k) * rows,) + start)
        return out

    def gather_z_list(self, value):
        return [value] + [self.z_xor(value, k) for k in range(1, self.planes)]

    def gather_z(self, value):
        return self.place_z(self.gather_z_list(value))

    def block_z(self, value, k):
        rows = value.shape[0] // self.planes
        return lax.dynamic_slice_in_dim(value, (self.plane ^ k) * rows, rows, 0)

    def send_z(self, value):
        return [self.z_xor(self.block_z(value, k), k) for k in range(1, self.planes)]

    def sum_z(self, value, moved):
        total = self.block_z(value, 0).astype(f32)
        for other in moved:
            total = total + other.astype(f32)
        return total.astype(value.dtype)

    def add_pair(self, part, far):
        return (part[: self.reps].astype(f32) + far.astype(f32)).astype(bf16)

    def pair_rows(self, own, other):
        first = jnp.where(self.c == 0, own, other)
        second = jnp.where(self.c == 0, other, own)
        return jnp.stack([first, second])

    def order_reps(self, values):
        return order(values, self.r)

    def sum_plane(self, part, length, collective):
        if self.reps == 4 and self.planes == 4:
            return reduce_plane(part, collective)
        total = self.gather_plane(self.scatter_plane(part, f32))
        return total[:, :length].astype(bf16), total[:, length:]


def adam_step(master, first, second, gradient, rate, decays):
    first_new = beta_first * first + (1.0 - beta_first) * gradient
    second_new = beta_second * second + (1.0 - beta_second) * gradient * gradient
    update = (
        first_new
        / (1.0 - beta_first**ADAM_STEP)
        / (jnp.sqrt(second_new / (1.0 - beta_second**ADAM_STEP)) + adam_eps)
    )
    if decays:
        update = update + weight_decay * master
    return (first_new, second_new, master - rate * update)


def adam_in_kernel(place_ref, *refs):
    reps = (len(refs) - 9) // 2
    pieces = refs[: 2 * reps]
    master_ref, first_ref, second_ref = refs[2 * reps : 2 * reps + 3]
    first_out, second_out, master_out = refs[-3:]
    r, c = place_ref[0], place_ref[1]
    sub = pieces[0].shape[1]
    for e in range(2):
        for k in range(reps):
            at = ((c ^ e) * reps + (r ^ k)) * sub
            lanes = pl.ds(pl.multiple_of(at, sub), sub)
            gradient = pieces[e * reps + k][...].astype(f32)
            first, second, master = adam_step(
                master_ref[:, lanes], first_ref[:, lanes], second_ref[:, lanes], gradient,
                learn_rates[0], with_decay[0],
            )
            first_out[:, lanes] = first
            second_out[:, lanes] = second
            master_out[:, lanes] = master


def adam_in(place, half, pieces, master, first, second, earlier):
    rows, columns = master.shape
    reps = len(pieces) // 2
    sub = LANES
    block = 2 * reps * sub
    steps = columns // 2 // block
    wide = pl.BlockSpec((rows, block), lambda i, place_ref: (0, half * steps + i))
    thin = pl.BlockSpec((rows, sub), lambda i, place_ref: (0, i))
    anywhere = pl.BlockSpec(memory_space=pl.ANY)
    if earlier is None:
        earlier = (master, first, second)
        aliases = {}
    else:
        aliases = {1 + 2 * reps + 3 + i: i for i in range(3)}
    return pl.pallas_call(
        adam_in_kernel,
        grid_spec=pltpu.PrefetchScalarGridSpec(
            num_scalar_prefetch=1,
            grid=(steps,),
            in_specs=[thin] * (2 * reps) + [wide] * 3 + [anywhere] * 3,
            out_specs=[wide] * 3,
        ),
        out_shape=[jax.ShapeDtypeStruct(master.shape, f32)] * 3,
        input_output_aliases=aliases,
        compiler_params=pltpu.CompilerParams(vmem_limit_bytes=32 * 2**20),
        cost_estimate=pl.CostEstimate(flops=10 * master.size, bytes_accessed=13 * master.size, transcendentals=master.size),
        name="adam_in",
    )(place, *pieces, master, first, second, *earlier)


def adam_out_kernel(place_ref, *refs):
    reps = len(refs) - 6
    master_ref, first_ref, second_ref, first_out, second_out, master_out = refs[reps:]
    for k in range(reps):

        @pl.when(pl.program_id(0) == k)
        def _():
            first_out[...], second_out[...], master_out[...] = adam_step(
                master_ref[...], first_ref[...], second_ref[...], refs[k][...].astype(f32),
                learn_rates[3], with_decay[3],
            )


def adam_out(place, pieces, master, first, second):
    rows, columns = master.shape
    reps = len(pieces)
    sub = rows // reps
    wide = columns // 2
    mine = pl.BlockSpec((sub, wide), lambda k, j, p: (p[0] ^ k, j))
    piece = pl.BlockSpec((sub, wide), lambda k, j, p: (0, j))
    return pl.pallas_call(
        adam_out_kernel,
        grid_spec=pltpu.PrefetchScalarGridSpec(
            num_scalar_prefetch=1,
            grid=(reps, 2),
            in_specs=[piece] * reps + [mine] * 3,
            out_specs=[mine] * 3,
        ),
        out_shape=[jax.ShapeDtypeStruct(master.shape, f32)] * 3,
        compiler_params=pltpu.CompilerParams(vmem_limit_bytes=32 * 2**20),
        cost_estimate=pl.CostEstimate(flops=10 * master.size, bytes_accessed=26 * master.size, transcendentals=master.size),
        name="adam_out",
    )(place, *pieces, master, first, second)


def slice_in_kernel(place_ref, own_ref, other_ref, out_ref):
    out_ref[0] = own_ref[...].astype(bf16)
    out_ref[1] = other_ref[...].astype(bf16)


def slice_in(place, master, reps):
    rows, columns = master.shape
    blocks = columns // (2 * reps * LANES)

    def of_core(e):
        return pl.BlockSpec((rows, LANES), lambda b, p: (0, (2 * b + (p[1] ^ e)) * reps + p[0]))

    return pl.pallas_call(
        slice_in_kernel,
        grid_spec=pltpu.PrefetchScalarGridSpec(
            num_scalar_prefetch=1,
            grid=(blocks,),
            in_specs=[of_core(0), of_core(1)],
            out_specs=pl.BlockSpec((2, rows, LANES), lambda b, p: (0, 0, b)),
        ),
        out_shape=jax.ShapeDtypeStruct((2, rows, blocks * LANES), bf16),
        name="slice_in",
    )(place, master, master)


def after(value, *earlier):
    return lax.optimization_barrier((value, *earlier))[0]


def after_all(values, *earlier):
    return list(lax.optimization_barrier((*values, *earlier))[: len(values)])


def unpack(values):
    seqs, rows, _ = values.shape
    parts = values.reshape(seqs, rows // (2 * NSTATE), 2 * NSTATE, LANES)
    return parts.transpose(0, 2, 1, 3).reshape(seqs, 2 * NSTATE, -1)


def pack(values):
    seqs, count, length = values.shape
    return values.reshape(seqs, count, length // LANES, LANES).transpose(0, 2, 1, 3).reshape(seqs, -1, LANES)


def to_chunks(values):
    seqs, count, length = values.shape
    return values.reshape(seqs, count, length // CHUNK, CHUNK).transpose(2, 1, 0, 3)


def from_sums(values):
    groups, length, _ = values.shape
    parts = values.reshape(groups, length, 2 * NSTATE, SUBS).transpose(0, 3, 2, 1)
    return parts.reshape(groups * SUBS, 2 * NSTATE, length)


def order(values, index):
    bit = 1
    while bit < len(values):
        swap = (index & bit) != 0
        values = [jnp.where(swap, values[i ^ bit], values[i]) for i in range(len(values))]
        bit *= 2
    return jnp.stack(values)


def shards(
    reps, shard_size,
    hidden, segments, cotangent,
    in_master, in_first, in_second,
    x_master, x_first, x_second,
    dt_master, dt_first, dt_second,
    out_master, out_first, out_second,
    chan_master, chan_first, chan_second,
    gain_master, gain_first, gain_second,
):
    net = Links(reps, shard_size)
    planes, r, c = net.planes, net.r, net.c
    length, model = hidden.shape[1:]
    in_rows = in_master.shape[0]
    own_chan = out_master.shape[0]
    sub = own_chan // reps
    width = planes * sub
    xcols = x_master.shape[1]
    chan_cols = chan_master.shape[1]
    seqs = 2 * reps

    def sub_rows(value):
        return lax.dynamic_slice_in_dim(value, r * sub, sub, 0)

    place = jnp.stack([r, c, net.plane]).astype(jnp.int32)
    own_hidden = hidden[0]
    tiled = sub % LANES == 0
    fast = tiled and reps == 4 and planes == 4
    if tiled:
        in_own, in_other = slice_in(place, in_master, reps)
    else:
        in_view = in_master.reshape(in_rows, 2, planes, 2, reps, sub)
        in_mine = lax.dynamic_index_in_dim(in_view, r, 4, keepdims=False).astype(bf16)
        in_own = lax.dynamic_index_in_dim(in_mine, c, 3, keepdims=False).reshape(in_rows, 2 * width)
        in_other = lax.dynamic_index_in_dim(in_mine, 1 - c, 3, keepdims=False).reshape(in_rows, 2 * width)
    small = jnp.concatenate(
        [sub_rows(x_master).astype(bf16), sub_rows(dt_master).astype(bf16), sub_rows(chan_master).astype(bf16)], axis=1
    )
    own_gain = lax.reduce_precision(gain_master, 8, 7)[None]
    own_ids = segments.astype(f32)
    if fast:
        small = jnp.pad(small, ((0, 0), (0, -small.shape[1] % LANES)))
        hidden_all, inner_blocks, small_parts, gain_parts, ids = gather_first(
            own_hidden, in_own[:, :width], in_other[:, :width], small, own_gain, own_ids
        )
        inner_blocks = [inner_blocks[k] for k in range(planes)]
        small_all = order(list(small_parts), net.plane).reshape(width, -1)
        two = [order([gain_parts[e * planes + k] for k in range(planes)], net.plane) for e in range(2)]
        gain = jnp.stack(order(two, c), axis=1).reshape(model)
        ids = ids.reshape(seqs, length)
        own_up = after(cotangent[0], hidden_all)
        gate_pair = net.pair_rows(in_own[:, width:], net.core(in_other[:, width:])).reshape(2 * in_rows, width)
        gate_blocks = net.gather_z_list(after(gate_pair, hidden_all))
        out_blocks = net.gather_z_list(after(sub_rows(out_master).astype(bf16), hidden_all))
    else:
        ids = net.gather_plane(own_ids).reshape(seqs, length)
        gain_pair = net.pair_rows(own_gain[0], net.core(own_gain[0])).reshape(2 * in_rows)
        gain = net.gather_z(gain_pair)
        small_all = net.gather_z(small)
        in_pair = net.pair_rows(in_own, net.core(in_other)).reshape(2 * in_rows, 2 * width)
        inner_blocks = net.gather_z_list(in_pair[:, :width])
        hidden_all = net.gather_plane(own_hidden)
        own_up = after(cotangent[0], hidden_all)
        gate_blocks = net.gather_z_list(in_pair[:, width:])
        out_blocks = net.gather_z_list(sub_rows(out_master).astype(bf16))
    up_near = net.gather_near(own_up)
    w_xdt = small_all[:, :RANK]
    w_xdt_t = w_xdt.T
    w_xbc = small_all[:, RANK:xcols].T
    w_dt = small_all[:, xcols : xcols + RANK]
    channel = small_all[:, xcols + RANK : xcols + RANK + chan_cols].astype(f32)
    a_log = channel[:, KCONV : KCONV + NSTATE]
    rates = -jnp.exp(a_log)
    rate_tiles = jnp.broadcast_to(rates.T[:, None, :], (NSTATE, SUBS, width))
    chan = channel.T
    same = [
        (jnp.pad(ids, ((0, 0), (KCONV - 1 - k, 0)), constant_values=-1)[:, :length] == ids).astype(f32)
        for k in range(KCONV - 1)
    ]
    cut = jnp.where(same[-1] > 0, 0.0, CUT)
    masks = jnp.stack(same + [cut] + [jnp.zeros_like(cut)] * (MASKS - KCONV), axis=2)

    normed, inner, conv_out, proj_part = front(
        place, hidden_all, gain[None], masks, chan, w_xdt_t, w_xbc, inner_blocks
    )
    dt_in, bc = net.sum_plane(proj_part, length, 2)
    up_all = jnp.stack(up_near + net.gather_far(after_all(up_near, dt_in)))
    upstream = jnp.concatenate([up_all, net.core(up_all)])
    bc = to_chunks(unpack(bc))
    scanned, starts = scan_forward(dt_in, masks, conv_out, bc, rate_tiles, w_dt, chan)
    out_part, mixed, grad_y, grad_gate, grad_skip = middle(
        place, normed, upstream, scanned, conv_out, chan, gate_blocks, out_blocks
    )
    out_far = net.core(out_part[reps:])
    grad_out = dot(mixed.reshape(-1, width), upstream.reshape(-1, model), ((0,), (0,))).astype(bf16)
    flat_normed = normed.reshape(-1, model)
    gin_gate = dot(flat_normed, grad_gate.reshape(-1, width), ((0,), (0,))).astype(bf16)
    pair, grad_y = lax.optimization_barrier((net.add_pair(out_part, out_far), grad_y))
    out_moved = [net.rep(pair[k], k) for k in range(1, reps)]
    grad_out_moved = net.send_z(grad_out)
    gin_gate_moved = net.send_z(gin_gate)
    grad_y = after(grad_y, grad_out, gin_gate)

    grad_conv, grad_dtlow, grad_dtin, grad_bc, grad_rates, grad_dtbias = scan_backward(
        dt_in, masks, conv_out, bc, rate_tiles, w_dt, chan, starts, grad_y
    )
    grad_rates = jnp.sum(grad_rates, axis=1).T
    grad_dt = dot(grad_dtlow.reshape(-1, width), dt_in.reshape(-1, RANK), ((0,), (0,)))
    out_sum = pair[0].astype(f32)
    for moved in after_all(out_moved, grad_dtin):
        out_sum = out_sum + moved.astype(f32)
    layer_output = (hidden[0].astype(f32) + out_sum).astype(bf16)
    grad_out_own = net.sum_z(grad_out, after_all(grad_out_moved, grad_dtin))
    gin_gate_rows = net.sum_z(gin_gate, after_all(gin_gate_moved, grad_dtin))
    proj_back = jnp.concatenate([grad_dtin, pack(from_sums(grad_bc))], axis=1)
    gp_dt, gp_bc = net.sum_plane(proj_back, length, 3)
    gp_bc = unpack(gp_bc).astype(bf16)
    flat_conv = conv_out.reshape(-1, width)
    grad_xdt = dot(flat_conv, gp_dt.reshape(-1, RANK), ((0,), (0,)))
    grad_xbc = lax.dot_general(
        conv_out, gp_bc, (((1,), (2,)), ((0,), (0,))), preferred_element_type=f32
    ).sum(axis=0)
    grad_x = jnp.concatenate([grad_xdt, grad_xbc], axis=1)
    grad_inner, conv_sums = back_conv(place, grad_conv, gp_dt, gp_bc, inner, masks, chan, w_xdt_t, w_xbc)
    gin_inner = dot(flat_normed, grad_inner.reshape(-1, width), ((0,), (0,))).astype(bf16)
    normed_part, grad_gain = back_normed(place, grad_inner, grad_gate, hidden_all, inner_blocks, gate_blocks)
    def pieces_in(rows):
        rows = rows.reshape(2, in_rows, width)
        own = lax.dynamic_index_in_dim(rows, c, 0, keepdims=False)
        other = net.core(lax.dynamic_index_in_dim(rows, 1 - c, 0, keepdims=False))
        return net.gather_rep(own) + net.gather_rep(other)

    def full_in(pieces):
        own = net.order_reps(pieces[:reps])
        other = net.order_reps(pieces[reps:])
        every = net.pair_rows(own, other).reshape(2, reps, in_rows, planes, sub)
        return every.transpose(2, 3, 0, 1, 4).reshape(in_rows, width * seqs).astype(f32)

    out_new = adam_out(
        place, net.gather_rep(grad_out_own), out_master, out_first, out_second
    )
    grad_small = jnp.concatenate(
        [
            grad_x,
            grad_dt,
            jnp.sum(conv_sums[:KCONV], axis=1).T,
            grad_rates * rates,
            jnp.sum(conv_sums[KCONV], axis=0)[:, None],
            jnp.sum(grad_dtbias, axis=0)[:, None],
            jnp.sum(grad_skip, axis=0)[:, None],
            jnp.sum(grad_gain, axis=0).reshape(width, reps),
        ],
        axis=1,
    )
    if fast:
        grad_small = jnp.pad(grad_small, ((0, 0), (0, -grad_small.shape[1] % LANES)))
        grad_normed, inner_pieces, small_sum = finish(normed_part, gin_inner, grad_small)
        inner_pieces = [inner_pieces[e, k] for e in range(2) for k in range(reps)]
        small_sum = net.order_reps(list(small_sum))
    else:
        grad_normed = net.scatter_plane(normed_part, bf16)
        inner_pieces = pieces_in(net.sum_z(gin_inner, net.send_z(gin_inner)))
        small_sum = net.order_reps(net.gather_rep(net.sum_z(grad_small, net.send_z(grad_small))))
    own_res = hidden[0].astype(f32)
    own_inv = lax.rsqrt(jnp.mean(own_res * own_res, axis=1, keepdims=True) + norm_eps)
    grad_scaled = grad_normed * gain
    input_grad = (
        own_inv * grad_scaled
        - own_res * own_inv**3 * jnp.mean(grad_scaled * own_res, axis=1, keepdims=True)
        + cotangent[0].astype(f32)
    ).astype(bf16)

    if tiled:
        in_new = adam_in(place, 1, pieces_in(gin_gate_rows), in_master, in_first, in_second, None)
        in_new = adam_in(place, 0, inner_pieces, in_master, in_first, in_second, in_new)
    else:
        in_sum = jnp.concatenate([full_in(inner_pieces), full_in(pieces_in(gin_gate_rows))], axis=1)
        in_new = adam_step(in_master, in_first, in_second, in_sum, learn_rates[0], with_decay[0])
    gain_cols = slice(xcols + RANK + chan_cols, xcols + RANK + chan_cols + reps)
    gain_two = jnp.sum(small_sum[:, :, gain_cols], axis=0).reshape(2, in_rows)
    gain_own = lax.dynamic_index_in_dim(gain_two, c, 0, keepdims=False)
    gain_sum = gain_own + net.core(lax.dynamic_index_in_dim(gain_two, 1 - c, 0, keepdims=False))
    small_sum = small_sum.reshape(own_chan, -1)
    x_sum = small_sum[:, :xcols]
    dt_sum = small_sum[:, xcols : xcols + RANK]
    chan_sum = small_sum[:, xcols + RANK : xcols + RANK + chan_cols]

    def update(position, master, first, second, gradient):
        return adam_step(master, first, second, gradient, learn_rates[position], with_decay[position])

    updated = (
        *in_new,
        *update(1, x_master, x_first, x_second, x_sum),
        *update(2, dt_master, dt_first, dt_second, dt_sum),
        *out_new,
        *update(4, chan_master, chan_first, chan_second, chan_sum),
        *update(5, gain_master, gain_first, gain_second, gain_sum),
    )
    return (layer_output[None], input_grad[None], *updated)


def solution(mesh):
    token = P(("rep", "shard"), None, None)
    rows = P("shard", None)
    placed = (token, P(("rep", "shard"), None), token) + (rows,) * 15 + (P("shard"),) * 3
    return jax.shard_map(
        functools.partial(shards, mesh.shape["rep"], mesh.shape["shard"]),
        mesh=mesh,
        in_specs=placed,
        out_specs=(token, token) + (rows,) * 15 + (P("shard"),) * 3,
        check_vma=False,
    )
```

time: 1010 us -> 754 us (0.75)
  Pallas kernels: 236 us -> 439 us
  waiting for transfers between devices: 237 us -> 98.3 us
  other arithmetic: 130 us -> 40.1 us
  starting transfers between devices: 137 us -> 49.1 us
  matrix products: 106 us -> 30 us
  local copies, waits for them, and re-layouts: 140 us -> 83.9 us
    pallas_call x2 -> x14, Pallas kernels: 236 us -> 439 us  [the longest x1 120 us: scan_backward(): pl.pallas_call(scan_bwd_kernel, grid=(chunks,), in_specs=ins + [start_spe...]
    ppermute x24 -> x12, waiting for transfers between devices: 142 us -> 31.2 us  [z(): return lax.ppermute(value, 'shard', self.planes_pairs(pairs))]
    dot_general x15 -> x5, matrix products: 106 us -> 28.6 us  [dot(): return lax.dot_general(a, b, (dims, ((), ())), preferred_element_type=f32)]
    ppermute x24 -> x12, starting transfers between devices: 84.2 us -> 27.2 us  [z(): return lax.ppermute(value, 'shard', self.planes_pairs(pairs))]
    unnamed x217 -> x147, local copies, waits for them, and re-layouts: 76.8 us -> 25.1 us
    ppermute x47 -> x19, starting transfers between devices: 50.8 us -> 21.2 us  [rep(): return lax.ppermute(value, 'rep', [(i, i ^ k) for i in range(self.reps)])]
    sub x6 -> x4, other arithmetic: 35.4 us -> 6.44 us  [adam_step(): return (first_new, second_new, master - rate * update)]
    another operation x18 -> x10, other arithmetic: 28.8 us -> 5.79 us  [the longest x2 3.44 us: shards(): up_all = jnp.stack(up_near + net.gather_far(after_all(up_near, dt_in)))]
  transfers between devices with their start and end apart: 85 -> 36, of which waited for: 33 -> 6; matrix products, arithmetic and copies ran while one was open for 29% -> 15% of each run, Pallas kernels for 0% -> 47%
where the time goes in v2:
time: 754 us; the launch traced here: 742 us
  Pallas kernels  439 us (58%)
  waiting for transfers between devices  98.3 us (13%)
  local copies, waits for them, and re-layouts  83.9 us (11%)
  starting transfers between devices  49.1 us (7%)
  other arithmetic  40.1 us (5%)
  matrix products  30 us (4%)
    pallas_call x1, Pallas kernels, scan_backward(): pl.pallas_call(scan_bwd_kernel, grid=(chunks,), in_specs=ins + [start_spe...  120 us
    pallas_call x1, Pallas kernels, finish(): pl.pallas_call(finish_kernel, in_specs=[anywhere] * 3, out_specs=[pl.Bloc...  78.7 us
    ppermute x19, waiting for transfers between devices, rep(): return lax.ppermute(value, 'rep', [(i, i ^ k) for i in range(self.reps)])  67.1 us
    pallas_call x4, Pallas kernels, per_sequence(): pl.pallas_call(kernel, grid_spec=pltpu.PrefetchScalarGridSpec(num_scalar_...  67 us
    pallas_call x1, Pallas kernels, gather_first(): pl.pallas_call(gather_first_kernel, in_specs=[anywhere] * 6, out_specs=[a...  62.4 us
    pallas_call x2, Pallas kernels, reduce_plane(): pl.pallas_call(reduce_plane_kernel, in_specs=[vmem], out_specs=[vmem, vme...  39.2 us
    pallas_call x1, Pallas kernels, scan_forward(): pl.pallas_call(scan_fwd_kernel, grid=(chunks,), in_specs=ins, out_specs=[...  36 us
    ppermute x12, waiting for transfers between devices, z(): return lax.ppermute(value, 'shard', self.planes_pairs(pairs))  31.2 us
  transfers between devices with their start and end apart: 36, of which 6 were waited for; matrix products, arithmetic and copies ran while one was open for 15% of the time, Pallas kernels for 47%

profile of v2, /device:TPU:0, one launch (start us, length us, event | category | flops | bytes accessed | tf_op | source)
XLA Modules:
  0.0 742.4 jit_solution(14476250148140837124)
XLA Ops:
  1.3 6.2 slice_in.1
  15.5 62.4 %gather_first.1 = (bf16[8,256,2048]{2,1,0:T(8,128)(2,1)}, bf16[4,512,512]{2,1,0:T(8,128)(2,1)}, bf16[4,128,384]{2,1,0:T(8,128)(2,1)}, f32[8,1,256]{2,1,0:T(1,128)}, f32[8,1,256]{2,1,0:T(1,128)}) custom-call(bf16[256,2048]{1,0:T(8,128)(2,1)} %bitcast.175, bf16[256,512]{1,0:T(8,128)(2,1)} %get-tuple-element.330.in_own, ...), custom_call_target="tpu_custom_call" | custom-call | bytes 100000000 | tf_op jit(solution)/shard_map/gather_first/pallas_call | solution.py:673
  99.4 4.5 stack.120.mask.mask_ref
  106.9 15.0 %front.1 = (bf16[8,256,2048]{2,1,0:T(8,128)(2,1)}, f32[8,256,512]{2,1,0:T(8,128)}, bf16[8,256,512]{2,1,0:T(8,128)(2,1)}, f32[8,320,128]{2,1,0:T(8,128)}) custom-call(s32[3]{0:T(128)} %pad_add_fusion.place_ref, bf16[8,256,2048]{2,1,0:T(8,128)(2,1)} %get-tuple-element.79.hid.hid_ref, f32[8,256,8]{2,1,0:T(8,128)} %stack.120.mask.mask_ref, ...), custom_call_target="tpu_custom_call" | custom-call | flops 4294967296 | bytes 40000000 | tf_op jit(solution)/shard_map/front/pallas_call | solution.py:370
  123.2 19.9 %reduce_plane.2 = (bf16[8,256,128]{2,1,0:T(8,128)(2,1)S(1)}, f32[8,64,128]{2,1,0:T(8,128)S(1)}) custom-call(f32[8,320,128]{2,1,0:T(8,128)S(1)} %copy-done.10), custom_call_target="tpu_custom_call" | custom-call | bytes 50000000 | tf_op jit(solution)/shard_map/reduce_plane/pallas_call | solution.py:730
  146.5 11.0 %collective-permute-done.3 = bf16[128,2048]{1,0:T(8,128)(2,1)S(1)} collective-permute-done((bf16[128,2048]{1,0:T(8,128)(2,1)S(1)}, bf16[128,2048]{1,0:T(8,128)(2,1)S(1)}, u32[]{:S(2)}, u32[]{:S(2)}) %collective-permute-start.3) | collective-permute-done | bytes 524320 | tf_op jit(solution)/shard_map/ppermute | solution.py:932
  160.6 3.4 pad_maximum_fusion
  175.8 36.0 %scan_forward.1 = (f32[8,256,512]{2,1,0:T(8,128)}, f32[8,16,8,512]{3,2,1,0:T(8,128)}) custom-call(bf16[8,256,128]{2,1,0:T(8,128)(2,1)S(1)} %get-tuple-element.87.dt_ref, f32[8,256,8]{2,1,0:T(8,128)S(1)} %copy-done.6, bf16[8,256,512]{2,1,0:T(8,128)(2,1)} %get-tuple-element.90.conv_ref, f32[8,32,8,32]{3,2,1,0:T(8,128)S(1)} %bitcast.172, ...), custom_call_target="tpu_custom_call" | custom-call | flops 134217728 | bytes 100000000 | tf_op jit(solution)/shard_map/scan_forward/pallas_call | solution.py:256
  214.6 3.6 collective-permute-start.10
  221.0 31.2 %collective-permute-done.10.refs_6_ = bf16[128,2048]{1,0:T(8,128)(2,1)S(1)} collective-permute-done((bf16[128,2048]{1,0:T(8,128)(2,1)S(1)}, bf16[128,2048]{1,0:T(8,128)(2,1)S(1)}, u32[]{:S(2)}, u32[]{:S(2)}) %collective-permute-start.10) | collective-permute-done | bytes 524320 | tf_op jit(solution)/shard_map/ppermute | solution.py:941
  253.2 22.1 %middle.1 = (bf16[8,256,2048]{2,1,0:T(8,128)(2,1)}, bf16[8,256,512]{2,1,0:T(8,128)(2,1)}, f32[8,256,512]{2,1,0:T(8,128)}, bf16[8,256,512]{2,1,0:T(8,128)(2,1)}, f32[8,512]{1,0:T(8,128)}) custom-call(s32[3]{0:T(128)} %pad_add_fusion.place_ref, bf16[8,256,2048]{2,1,0:T(8,128)(2,1)} %get-tuple-element.84.normed_ref, bf16[8,256,2048]{2,1,0:T(8,128)(2,1)} %copy-done.52, ...), custom_call_target="tpu_custom_call" | custom-call | flops 12884901888 | bytes 40000000 | tf_op jit(solution)/shard_map/middle/pallas_call | solution.py:370
  275.3 4.8 slice.183
  280.3 8.5 %bitcast_convert_fusion.1 = bf16[2048,512]{1,0:T(8,128)(2,1)S(1)} fusion(bf16[8,256,2048]{2,1,0:T(8,128)(2,1)} %get-tuple-element.84.normed_ref, bf16[8,256,512]{2,1,0:T(8,128)(2,1)} %get-tuple-element.101.ggate_ref), kind=kOutput, calls=%fused_computation.3 | convolution fusion | flops 4296015872 | bytes 12582912 | tf_op jit(solution)/shard_map/dot_general | solution.py:42
  290.1 11.5 %collective-permute-start.16 = (bf16[512,512]{1,0:T(8,128)(2,1)}, bf16[512,512]{1,0:T(8,128)(2,1)}, u32[]{:S(2)}, u32[]{:S(2)}) collective-permute-start(bf16[512,512]{1,0:T(8,128)(2,1)} %get-tuple-element.305), channel_id=1, source_target_pairs={{0,2},{1,3},{2,0},{3,1},{4,6},{5,7},{6,4},{7,5},{8,10},{9,11},{10,... | collective-permute-start | bytes 1572872 | tf_op jit(solution)/shard_map/ppermute | solution.py:941
  304.0 8.3 %bitcast_convert_fusion.2 = bf16[512,2048]{1,0:T(8,128)(2,1)S(1)} fusion(bf16[8,256,512]{2,1,0:T(8,128)(2,1)S(1)} %copy-done.66, bf16[8,256,2048]{2,1,0:T(8,128)(2,1)} %copy-done.52), kind=kOutput, calls=%fused_computation.4 | convolution fusion | flops 4296015872 | bytes 12582912 | tf_op jit(solution)/shard_map/dot_general | solution.py:42
  316.4 6.2 add_convert_fusion
  322.6 119.6 %scan_backward.1 = (f32[8,256,512]{2,1,0:T(8,128)}, bf16[8,256,512]{2,1,0:T(8,128)(2,1)}, f32[8,256,128]{2,1,0:T(8,128)}, f32[1,256,256]{2,1,0:T(8,128)}, f32[16,8,512]{2,1,0:T(8,128)}, /*index=5*/f32[8,512]{1,0:T(8,128)}) custom-call(bf16[8,256,128]{2,1,0:T(8,128)(2,1)} %copy-done.20, f32[8,256,8]{2,1,0:T(8,128)} %stack.120.mask.mask_ref, ...), custom_call_target="tpu_custom_call" | custom-call | flops 402653184 | bytes 300000000 | tf_op jit(solution)/shard_map/scan_backward/pallas_call | solution.py:283
  444.8 19.2 %reduce_plane.3 = (bf16[8,256,128]{2,1,0:T(8,128)(2,1)S(1)}, f32[8,64,128]{2,1,0:T(8,128)S(1)}) custom-call(f32[8,320,128]{2,1,0:T(8,128)S(1)} %pad_maximum_fusion.1.part), custom_call_target="tpu_custom_call" | custom-call | bytes 50000000 | tf_op jit(solution)/shard_map/reduce_plane/pallas_call | solution.py:730
  465.8 13.0 %back_conv.1 = (bf16[8,256,512]{2,1,0:T(8,128)(2,1)}, f32[5,8,512]{2,1,0:T(8,128)}) custom-call(s32[3]{0:T(128)} %pad_add_fusion.place_ref, f32[8,256,512]{2,1,0:T(8,128)} %get-tuple-element.107.gconv_ref, bf16[8,256,128]{2,1,0:T(8,128)(2,1)} %copy-done.8, bf16[8,32,256]{2,1,0:T(8,128)(2,1)} %convert_element_type.140.gbc_ref, ...), custom_call_target="tpu_custom_call" | custom-call | flops 268435456 | bytes 40000000 | tf_op jit(solution)/shard_map/back_conv/pallas_call | solution.py:370
  489.2 9.6 %bitcast_convert_fusion.gin = bf16[2048,512]{1,0:T(8,128)(2,1)} fusion(bf16[8,256,2048]{2,1,0:T(8,128)(2,1)} %get-tuple-element.84.normed_ref, bf16[8,256,512]{2,1,0:T(8,128)(2,1)S(1)} %copy-done.62), kind=kOutput, calls=%fused_computation.2 | convolution fusion | flops 4296015872 | bytes 12582912 | tf_op jit(solution)/shard_map/dot_general | solution.py:42
  501.4 16.9 %back_normed.1 = (bf16[8,256,2048]{2,1,0:T(8,128)(2,1)}, f32[8,2048]{1,0:T(8,128)}) custom-call(s32[3]{0:T(128)} %pad_add_fusion.place_ref, bf16[8,256,512]{2,1,0:T(8,128)(2,1)} %get-tuple-element.112.ginner_ref, bf16[8,256,512]{2,1,0:T(8,128)(2,1)} %get-tuple-element.101.ggate_ref, bf16[8,256,2048]{2,1,0:T(8,128)(2,1)} %get-tuple-element.79.hid.hid_ref, ...), custom_call_target="tpu_custom_call" | custom-call | flops 8589934592 | bytes 40000000 | tf_op jit(solution)/shard_map/back_normed/pallas_call | solution.py:370
  522.0 78.7 %finish.1 = (f32[256,2048]{1,0:T(8,128)S(1)}, bf16[2,4,256,512]{3,2,1,0:T(8,128)(2,1)S(1)}, f32[4,128,384]{2,1,0:T(8,128)S(1)}) custom-call(bf16[8,256,2048]{2,1,0:T(8,128)(2,1)} %get-tuple-element.113.part, bf16[2048,512]{1,0:T(8,128)(2,1)S(1)} %copy-done.7, f32[512,384]{1,0:T(8,128)S(1)} %pad.24.small), custom_call_target="tpu_custom_call" | custom-call | bytes 150000000 | tf_op jit(solution)/shard_map/finish/pallas_call | solution.py:884
  604.0 3.6 slice_bitcast_fusion
  623.6 8.5 %collective-permute-done.22 = bf16[128,512]{1,0:T(8,128)(2,1)} collective-permute-done((bf16[128,512]{1,0:T(8,128)(2,1)}, bf16[128,512]{1,0:T(8,128)(2,1)}, u32[]{:S(2)}, u32[]{:S(2)}) %collective-permute-start.22) | collective-permute-done | bytes 131104 | tf_op jit(solution)/shard_map/ppermute | solution.py:932
  645.7 43.2 %collective-permute-done.27 = bf16[128,512]{1,0:T(8,128)(2,1)S(1)} collective-permute-done((bf16[128,512]{1,0:T(8,128)(2,1)S(1)}, bf16[128,512]{1,0:T(8,128)(2,1)S(1)}, u32[]{:S(2)}, u32[]{:S(2)}) %collective-permute-start.27) | collective-permute-done | bytes 131104 | tf_op jit(solution)/shard_map/ppermute | solution.py:932
  694.0 3.4 copy-done
  697.4 3.4 copy-done.1
  700.8 9.8 %adam_in.2 = (f32[256,8192]{1,0:T(8,128)}, f32[256,8192]{1,0:T(8,128)}, f32[256,8192]{1,0:T(8,128)}) custom-call(s32[3]{0:T(128)S(1)} %copy-done.25, bf16[256,512]{1,0:T(8,128)(2,1)S(1)} %get-tuple-element.329.refs_0_, bf16[256,512]{1,0:T(8,128)(2,1)} %collective-permute-done.19.refs_1_, bf16[256,512]{1,0:T(8,128)(2,1)} %collective-permute-done.20.refs_2_, ...), custom_call_target="tpu_custom_call" | custom-call | flops 20971520 | bytes 27262976 | tf_op jit(solution)/shard_map/adam_in/pallas_call | solution.py:1067
  710.7 3.4 copy-done.2
  714.1 9.9 %adam_in.3 = (f32[256,8192]{1,0:T(8,128)}, f32[256,8192]{1,0:T(8,128)}, f32[256,8192]{1,0:T(8,128)}) custom-call(s32[3]{0:T(128)S(1)} %copy-done.25, bf16[256,512]{1,0:T(8,128)(2,1)S(1)} %copy-done.18, bf16[256,512]{1,0:T(8,128)(2,1)S(1)} %copy-done.17, ...), custom_call_target="tpu_custom_call", output_to_operand_aliasing={{0}: (12, {}), {1}: (13, {}), {2}: (14, {})} | custom-call | flops 20971520 | bytes 27262976 | tf_op jit(solution)/shard_map/adam_in/pallas_call | solution.py:1067
  727.3 10.0 %adam_out.1 = (f32[512,2048]{1,0:T(8,128)}, f32[512,2048]{1,0:T(8,128)}, f32[512,2048]{1,0:T(8,128)}) custom-call(s32[3]{0:T(128)S(1)} %copy-done.25, bf16[128,2048]{1,0:T(8,128)(2,1)S(1)} %add_convert_fusion.1.refs_0_, bf16[128,2048]{1,0:T(8,128)(2,1)S(1)} %collective-permute-done.31.refs_1_, bf16[128,2048]{1,0:T(8,128)(2,1)} %collective-permute-done.32.refs_2_, ...), custom_call_target="tpu_custom_call" | custom-call | flops 10485760 | bytes 27262976 | tf_op jit(solution)/shard_map/adam_out/pallas_call | solution.py:1103
  737.3 4.7 fusion.9
  (311 shorter events, 128.8 us)
Async XLA Ops:
  80.2 62.9 %collective-permute-start = (bf16[256,2048]{1,0:T(8,128)(2,1)S(1)}, bf16[256,2048]{1,0:T(8,128)(2,1)S(1)}, u32[]{:S(2)}, u32[]{:S(2)}) collective-permute-start(bf16[256,2048]{1,0:T(8,128)(2,1)S(1)} %bitcast.176), channel_id=1, source_target_pairs={{0,8},{8,0},{16,24},{24,16},{1,9},{9,1},{17,25},{25,17},{2,10},{10... | collective-permute-start | bytes 3145736 | tf_op jit(solution)/shard_map/ppermute | solution.py:932
  81.8 61.4 %collective-permute-start.1 = (bf16[256,2048]{1,0:T(8,128)(2,1)S(1)}, bf16[256,2048]{1,0:T(8,128)(2,1)}, u32[]{:S(2)}, u32[]{:S(2)}) collective-permute-start(bf16[256,2048]{1,0:T(8,128)(2,1)S(1)} %bitcast.177), channel_id=1, source_target_pairs={{0,16},{8,24},{16,0},{24,8},{1,17},{9,25},{17,1},{25,9},{2,18},{10... | collective-permute-start | bytes 3145736 | tf_op jit(solution)/shard_map/ppermute | solution.py:932
  143.2 14.3 %collective-permute-start.3 = (bf16[128,2048]{1,0:T(8,128)(2,1)S(1)}, bf16[128,2048]{1,0:T(8,128)(2,1)S(1)}, u32[]{:S(2)}, u32[]{:S(2)}) collective-permute-start(bf16[128,2048]{1,0:T(8,128)(2,1)S(1)} %slice.177), channel_id=1, source_target_pairs={{0,16},{8,24},{16,0},{24,8},{1,17},{9,25},{17,1},{25,9},{2,18},{10... | collective-permute-start | bytes 1572872 | tf_op jit(solution)/shard_map/ppermute | solution.py:932
  145.7 14.0 %collective-permute-start.2 = (bf16[128,2048]{1,0:T(8,128)(2,1)S(1)}, bf16[128,2048]{1,0:T(8,128)(2,1)S(1)}, u32[]{:S(2)}, u32[]{:S(2)}) collective-permute-start(bf16[128,2048]{1,0:T(8,128)(2,1)S(1)} %slice.176), channel_id=1, source_target_pairs={{0,8},{8,0},{16,24},{24,16},{1,9},{9,1},{17,25},{25,17},{2,10},{10... | collective-permute-start | bytes 1572872 | tf_op jit(solution)/shard_map/ppermute | solution.py:932
  164.0 54.2 %collective-permute-start.4 = (bf16[4,256,2048]{2,1,0:T(8,128)(2,1)}, bf16[4,256,2048]{2,1,0:T(8,128)(2,1)}, u32[]{:S(2)}, u32[]{:S(2)}) collective-permute-start(bf16[4,256,2048]{2,1,0:T(8,128)(2,1)} %pad_maximum_fusion), channel_id=1, source_target_pairs={{0,1},{1,0},{2,3},{3,2},{4,5},{5,4},{6,7},{7,6},{8,9},{9,8},{10,11... | collective-permute-start | bytes 12582920 | tf_op jit(solution)/shard_map/ppermute | solution.py:935
  166.9 47.7 %collective-permute-start.6 = (bf16[512,512]{1,0:T(8,128)(2,1)}, bf16[512,512]{1,0:T(8,128)(2,1)}, u32[]{:S(2)}, u32[]{:S(2)}) collective-permute-start(bf16[512,512]{1,0:T(8,128)(2,1)} %bitcast.40.refs_0_.refs_4_), channel_id=1, source_target_pairs={{0,2},{1,3},{2,0},{3,1},{4,6},{5,7},{6,4},{7,5},{8,10},{9,11},{10,... | collective-permute-start | bytes 1572872 | tf_op jit(solution)/shard_map/ppermute | solution.py:941
  168.5 52.5 %collective-permute-start.7 = (bf16[512,512]{1,0:T(8,128)(2,1)}, bf16[512,512]{1,0:T(8,128)(2,1)}, u32[]{:S(2)}, u32[]{:S(2)}) collective-permute-start(bf16[512,512]{1,0:T(8,128)(2,1)} %bitcast.40.refs_0_.refs_4_), channel_id=1, source_target_pairs={{0,4},{1,5},{2,6},{3,7},{4,0},{5,1},{6,2},{7,3},{8,12},{9,13},{10,... | collective-permute-start | bytes 1572872 | tf_op jit(solution)/shard_map/ppermute | solution.py:941
  171.1 49.9 %collective-permute-start.8 = (bf16[512,512]{1,0:T(8,128)(2,1)}, bf16[512,512]{1,0:T(8,128)(2,1)}, u32[]{:S(2)}, u32[]{:S(2)}) collective-permute-start(bf16[512,512]{1,0:T(8,128)(2,1)} %bitcast.40.refs_0_.refs_4_), channel_id=1, source_target_pairs={{0,6},{1,7},{2,4},{3,5},{4,2},{5,3},{6,0},{7,1},{8,14},{9,15},{10,... | collective-permute-start | bytes 1572872 | tf_op jit(solution)/shard_map/ppermute | solution.py:941
  175.0 46.0 %collective-permute-start.9 = (bf16[128,2048]{1,0:T(8,128)(2,1)}, bf16[128,2048]{1,0:T(8,128)(2,1)S(1)}, u32[]{:S(2)}, u32[]{:S(2)}) collective-permute-start(bf16[128,2048]{1,0:T(8,128)(2,1)} %dynamic-slice_convert_fusion.refs_4_), channel_id=1, source_target_pairs={{0,2},{1,3},{2,0},{3,1},{4,6},{5,7},{6,4},{7,5},{8,10},{9,11},{10,... | collective-permute-start | bytes 1572872 | tf_op jit(solution)/shard_map/ppermute | solution.py:941
  214.6 37.6 %collective-permute-start.10 = (bf16[128,2048]{1,0:T(8,128)(2,1)S(1)}, bf16[128,2048]{1,0:T(8,128)(2,1)S(1)}, u32[]{:S(2)}, u32[]{:S(2)}) collective-permute-start(bf16[128,2048]{1,0:T(8,128)(2,1)S(1)} %copy-done.46), channel_id=1, source_target_pairs={{0,4},{1,5},{2,6},{3,7},{4,0},{5,1},{6,2},{7,3},{8,12},{9,13},{10,... | collective-permute-start | bytes 1572872 | tf_op jit(solution)/shard_map/ppermute | solution.py:941
  218.2 34.0 %collective-permute-start.11 = (bf16[128,2048]{1,0:T(8,128)(2,1)S(1)}, bf16[128,2048]{1,0:T(8,128)(2,1)S(1)}, u32[]{:S(2)}, u32[]{:S(2)}) collective-permute-start(bf16[128,2048]{1,0:T(8,128)(2,1)S(1)} %copy-done.46), channel_id=1, source_target_pairs={{0,6},{1,7},{2,4},{3,5},{4,2},{5,3},{6,0},{7,1},{8,14},{9,15},{10,... | collective-permute-start | bytes 1572872 | tf_op jit(solution)/shard_map/ppermute | solution.py:941
  280.1 34.5 %collective-permute-start.12 = (bf16[4,256,2048]{2,1,0:T(8,128)(2,1)}, bf16[4,256,2048]{2,1,0:T(8,128)(2,1)}, u32[]{:S(2)}, u32[]{:S(2)}) collective-permute-start(bf16[4,256,2048]{2,1,0:T(8,128)(2,1)} %slice.183), channel_id=1, source_target_pairs={{0,1},{1,0},{2,3},{3,2},{4,5},{5,4},{6,7},{7,6},{8,9},{9,8},{10,11... | collective-permute-start | bytes 12582920 | tf_op jit(solution)/shard_map/ppermute | solution.py:935
  290.1 193.2 %collective-permute-start.16 = (bf16[512,512]{1,0:T(8,128)(2,1)}, bf16[512,512]{1,0:T(8,128)(2,1)}, u32[]{:S(2)}, u32[]{:S(2)}) collective-permute-start(bf16[512,512]{1,0:T(8,128)(2,1)} %get-tuple-element.305), channel_id=1, source_target_pairs={{0,2},{1,3},{2,0},{3,1},{4,6},{5,7},{6,4},{7,5},{8,10},{9,11},{10,... | collective-permute-start | bytes 1572872 | tf_op jit(solution)/shard_map/ppermute | solution.py:941
  301.6 183.2 %collective-permute-start.17 = (bf16[512,512]{1,0:T(8,128)(2,1)}, bf16[512,512]{1,0:T(8,128)(2,1)}, u32[]{:S(2)}, u32[]{:S(2)}) collective-permute-start(bf16[512,512]{1,0:T(8,128)(2,1)} %get-tuple-element.304), channel_id=1, source_target_pairs={{0,4},{1,5},{2,6},{3,7},{4,0},{5,1},{6,2},{7,3},{8,12},{9,13},{10,... | collective-permute-start | bytes 1572872 | tf_op jit(solution)/shard_map/ppermute | solution.py:941
  302.5 182.3 %collective-permute-start.18 = (bf16[512,512]{1,0:T(8,128)(2,1)}, bf16[512,512]{1,0:T(8,128)(2,1)}, u32[]{:S(2)}, u32[]{:S(2)}) collective-permute-start(bf16[512,512]{1,0:T(8,128)(2,1)} %get-tuple-element.303), channel_id=1, source_target_pairs={{0,6},{1,7},{2,4},{3,5},{4,2},{5,3},{6,0},{7,1},{8,14},{9,15},{10,... | collective-permute-start | bytes 1572872 | tf_op jit(solution)/shard_map/ppermute | solution.py:941
  313.5 294.1 %collective-permute-start.28 = (bf16[128,2048]{1,0:T(8,128)(2,1)}, bf16[128,2048]{1,0:T(8,128)(2,1)}, u32[]{:S(2)}, u32[]{:S(2)}) collective-permute-start(bf16[128,2048]{1,0:T(8,128)(2,1)} %get-tuple-element.302), channel_id=1, source_target_pairs={{0,2},{1,3},{2,0},{3,1},{4,6},{5,7},{6,4},{7,5},{8,10},{9,11},{10,... | collective-permute-start | bytes 1572872 | tf_op jit(solution)/shard_map/ppermute | solution.py:941
  314.6 293.0 %collective-permute-start.29 = (bf16[128,2048]{1,0:T(8,128)(2,1)}, bf16[128,2048]{1,0:T(8,128)(2,1)}, u32[]{:S(2)}, u32[]{:S(2)}) collective-permute-start(bf16[128,2048]{1,0:T(8,128)(2,1)} %get-tuple-element.301), channel_id=1, source_target_pairs={{0,4},{1,5},{2,6},{3,7},{4,0},{5,1},{6,2},{7,3},{8,12},{9,13},{10,... | collective-permute-start | bytes 1572872 | tf_op jit(solution)/shard_map/ppermute | solution.py:941
  483.3 124.4 %collective-permute-start.30 = (bf16[128,2048]{1,0:T(8,128)(2,1)}, bf16[128,2048]{1,0:T(8,128)(2,1)}, u32[]{:S(2)}, u32[]{:S(2)}) collective-permute-start(bf16[128,2048]{1,0:T(8,128)(2,1)} %get-tuple-element.300), channel_id=1, source_target_pairs={{0,6},{1,7},{2,4},{3,5},{4,2},{5,3},{6,0},{7,1},{8,14},{9,15},{10,... | collective-permute-start | bytes 1572872 | tf_op jit(solution)/shard_map/ppermute | solution.py:941
  487.2 127.3 %collective-permute-start.19 = (bf16[256,512]{1,0:T(8,128)(2,1)S(1)}, bf16[256,512]{1,0:T(8,128)(2,1)}, u32[]{:S(2)}, u32[]{:S(2)}) collective-permute-start(bf16[256,512]{1,0:T(8,128)(2,1)S(1)} %get-tuple-element.329.refs_0_), channel_id=1, source_target_pairs={{0,8},{8,0},{16,24},{24,16},{1,9},{9,1},{17,25},{25,17},{2,10},{10... | collective-permute-start | bytes 786440 | tf_op jit(solution)/shard_map/ppermute | solution.py:932
  488.0 131.4 %collective-permute-start.20 = (bf16[256,512]{1,0:T(8,128)(2,1)S(1)}, bf16[256,512]{1,0:T(8,128)(2,1)}, u32[]{:S(2)}, u32[]{:S(2)}) collective-permute-start(bf16[256,512]{1,0:T(8,128)(2,1)S(1)} %get-tuple-element.329.refs_0_), channel_id=1, source_target_pairs={{0,16},{8,24},{16,0},{24,8},{1,17},{9,25},{17,1},{25,9},{2,18},{10... | collective-permute-start | bytes 786440 | tf_op jit(solution)/shard_map/ppermute | solution.py:932
  609.5 32.9 %collective-permute-start.31 = (bf16[128,2048]{1,0:T(8,128)(2,1)S(1)}, bf16[128,2048]{1,0:T(8,128)(2,1)S(1)}, u32[]{:S(2)}, u32[]{:S(2)}) collective-permute-start(bf16[128,2048]{1,0:T(8,128)(2,1)S(1)} %add_convert_fusion.1.refs_0_), channel_id=1, source_target_pairs={{0,8},{8,0},{16,24},{24,16},{1,9},{9,1},{17,25},{25,17},{2,10},{10... | collective-permute-start | bytes 1572872 | tf_op jit(solution)/shard_map/ppermute | solution.py:932
  614.5 29.4 %collective-permute-start.32 = (bf16[128,2048]{1,0:T(8,128)(2,1)S(1)}, bf16[128,2048]{1,0:T(8,128)(2,1)}, u32[]{:S(2)}, u32[]{:S(2)}) collective-permute-start(bf16[128,2048]{1,0:T(8,128)(2,1)S(1)} %add_convert_fusion.1.refs_0_), channel_id=1, source_target_pairs={{0,16},{8,24},{16,0},{24,8},{1,17},{9,25},{17,1},{25,9},{2,18},{10... | collective-permute-start | bytes 1572872 | tf_op jit(solution)/shard_map/ppermute | solution.py:932
  617.4 14.8 %collective-permute-start.22 = (bf16[128,512]{1,0:T(8,128)(2,1)}, bf16[128,512]{1,0:T(8,128)(2,1)}, u32[]{:S(2)}, u32[]{:S(2)}) collective-permute-start(bf16[128,512]{1,0:T(8,128)(2,1)} %slice.218), channel_id=1, source_target_pairs={{0,16},{8,24},{16,0},{24,8},{1,17},{9,25},{17,1},{25,9},{2,18},{10... | collective-permute-start | bytes 393224 | tf_op jit(solution)/shard_map/ppermute | solution.py:932
  618.1 20.3 %collective-permute-start.24 = (bf16[256,512]{1,0:T(8,128)(2,1)}, bf16[256,512]{1,0:T(8,128)(2,1)}, u32[]{:S(2)}, u32[]{:S(2)}) collective-permute-start(bf16[256,512]{1,0:T(8,128)(2,1)} %collective-permute-done.23.refs_4_), channel_id=1, source_target_pairs={{0,8},{8,0},{16,24},{24,16},{1,9},{9,1},{17,25},{25,17},{2,10},{10... | collective-permute-start | bytes 786440 | tf_op jit(solution)/shard_map/ppermute | solution.py:932
  619.4 19.9 %collective-permute-start.25 = (bf16[256,512]{1,0:T(8,128)(2,1)}, bf16[256,512]{1,0:T(8,128)(2,1)}, u32[]{:S(2)}, u32[]{:S(2)}) collective-permute-start(bf16[256,512]{1,0:T(8,128)(2,1)} %collective-permute-done.23.refs_4_), channel_id=1, source_target_pairs={{0,16},{8,24},{16,0},{24,8},{1,17},{9,25},{17,1},{25,9},{2,18},{10... | collective-permute-start | bytes 786440 | tf_op jit(solution)/shard_map/ppermute | solution.py:932
  637.1 100.2 %collective-permute-start.13 = (bf16[256,2048]{1,0:T(8,128)(2,1)}, bf16[256,2048]{1,0:T(8,128)(2,1)S(1)}, u32[]{:S(2)}, u32[]{:S(2)}) collective-permute-start(bf16[256,2048]{1,0:T(8,128)(2,1)} %get-tuple-element.299), channel_id=1, source_target_pairs={{0,8},{8,0},{16,24},{24,16},{1,9},{9,1},{17,25},{25,17},{2,10},{10... | collective-permute-start | bytes 3145736 | tf_op jit(solution)/shard_map/ppermute | solution.py:932
  638.4 98.9 %collective-permute-start.14 = (bf16[256,2048]{1,0:T(8,128)(2,1)}, bf16[256,2048]{1,0:T(8,128)(2,1)S(1)}, u32[]{:S(2)}, u32[]{:S(2)}) collective-permute-start(bf16[256,2048]{1,0:T(8,128)(2,1)} %get-tuple-element.298), channel_id=1, source_target_pairs={{0,16},{8,24},{16,0},{24,8},{1,17},{9,25},{17,1},{25,9},{2,18},{10... | collective-permute-start | bytes 3145736 | tf_op jit(solution)/shard_map/ppermute | solution.py:932
  639.3 98.0 %collective-permute-start.15 = (bf16[256,2048]{1,0:T(8,128)(2,1)}, bf16[256,2048]{1,0:T(8,128)(2,1)}, u32[]{:S(2)}, u32[]{:S(2)}) collective-permute-start(bf16[256,2048]{1,0:T(8,128)(2,1)} %get-tuple-element.297), channel_id=1, source_target_pairs={{0,24},{8,16},{16,8},{24,0},{1,25},{9,17},{17,9},{25,1},{2,26},{10... | collective-permute-start | bytes 3145736 | tf_op jit(solution)/shard_map/ppermute | solution.py:932
  642.5 46.4 %collective-permute-start.27 = (bf16[128,512]{1,0:T(8,128)(2,1)S(1)}, bf16[128,512]{1,0:T(8,128)(2,1)S(1)}, u32[]{:S(2)}, u32[]{:S(2)}) collective-permute-start(bf16[128,512]{1,0:T(8,128)(2,1)S(1)} %slice.220), channel_id=1, source_target_pairs={{0,16},{8,24},{16,0},{24,8},{1,17},{9,25},{17,1},{25,9},{2,18},{10... | collective-permute-start | bytes 393224 | tf_op jit(solution)/shard_map/ppermute | solution.py:932
  643.9 45.6 %collective-permute-start.26 = (bf16[128,512]{1,0:T(8,128)(2,1)S(1)}, bf16[128,512]{1,0:T(8,128)(2,1)S(1)}, u32[]{:S(2)}, u32[]{:S(2)}) collective-permute-start(bf16[128,512]{1,0:T(8,128)(2,1)S(1)} %slice.219), channel_id=1, source_target_pairs={{0,8},{8,0},{16,24},{24,16},{1,9},{9,1},{17,25},{25,17},{2,10},{10... | collective-permute-start | bytes 393224 | tf_op jit(solution)/shard_map/ppermute | solution.py:932
  688.9 35.1 %collective-permute-start.34 = (bf16[64,2048]{1,0:T(8,128)(2,1)S(1)}, bf16[64,2048]{1,0:T(8,128)(2,1)}, u32[]{:S(2)}, u32[]{:S(2)}) collective-permute-start(bf16[64,2048]{1,0:T(8,128)(2,1)S(1)} %slice.224), channel_id=1, source_target_pairs={{0,16},{8,24},{16,0},{24,8},{1,17},{9,25},{17,1},{25,9},{2,18},{10... | collective-permute-start | bytes 786440 | tf_op jit(solution)/shard_map/ppermute | solution.py:932
  689.5 34.6 %collective-permute-start.33 = (bf16[64,2048]{1,0:T(8,128)(2,1)S(1)}, bf16[64,2048]{1,0:T(8,128)(2,1)}, u32[]{:S(2)}, u32[]{:S(2)}) collective-permute-start(bf16[64,2048]{1,0:T(8,128)(2,1)S(1)} %slice.223), channel_id=1, source_target_pairs={{0,8},{8,0},{16,24},{24,16},{1,9},{9,1},{17,25},{25,17},{2,10},{10... | collective-permute-start | bytes 786440 | tf_op jit(solution)/shard_map/ppermute | solution.py:932
  (73 other events, 1070.3 us)

commit v3 on v2

--- a/solution.py
+++ b/solution.py
@@ -16,6 +16,9 @@
 SUBS = 8
 CUT = 1e30
 MASKS = 8
+TOKENS = 256
+BC_ROWS = TOKENS * 2 * NSTATE // LANES
+CH = 2 * NSTATE
 FWD_UNROLL = 8
 BWD_UNROLL = 4
 LOG2E = 1.4426950408889634
@@ -30,7 +33,6 @@
 
 bf16 = jnp.bfloat16
 f32 = jnp.float32
-PARTS = bf16
 
 
 def silu_slope(values):
@@ -42,9 +44,12 @@
     return lax.dot_general(a, b, (dims, ((), ())), preferred_element_type=f32)
 
 
-def expand_inputs(bc_ref, bx, sb):
-    rows = 2 * NSTATE * SUBS
-    v = bc_ref[0, :, pl.ds(sb * SUBS, SUBS), :].reshape(rows, CHUNK)
+def expand_inputs(bc_ref, bx, sb, chunk):
+    per = LANES // CHUNK
+    packed = BC_ROWS
+    first = sb * SUBS * packed + (chunk // per) * 2 * NSTATE
+    v = jnp.concatenate([bc_ref[pl.ds(first + n, SUBS, stride=packed), :] for n in range(2 * NSTATE)], axis=0)
+    v = pltpu.roll(v, (per - chunk % per) % per * CHUNK, 1)[:, :CHUNK]
     high = v.astype(bf16)
     rest = v - high.astype(f32)
     middle = rest.astype(bf16)
@@ -55,15 +60,21 @@
         bx[t] = dot(pieces, (token == t).astype(bf16), ((1,), (0,))).reshape(2 * NSTATE, SUBS, LANES)
 
 
-def lane_sums(acc, gbc_ref, sb):
+def lane_sums(acc, out_ref, sb, chunk):
     rows = 2 * NSTATE * SUBS
-    ones = jnp.ones((SUBS, 2 * LANES), bf16)
+    per = LANES // CHUNK
+    lane = lax.broadcasted_iota(jnp.int32, (2 * LANES, LANES), 1) - chunk % per * CHUNK
+    total = jnp.zeros((rows, LANES), f32)
     for t in range(CHUNK):
         v = acc[t].reshape(rows, LANES)
         high = v.astype(bf16)
         low = (v - high.astype(f32)).astype(bf16)
-        sums = dot(ones, jnp.concatenate([high, low], axis=1), ((1,), (1,)))
-        gbc_ref[sb, pl.ds(t, 1), :] = sums[:1]
+        total = total + dot(jnp.concatenate([high, low], axis=1), (lane == t).astype(bf16), ((1,), (0,)))
+    packed = BC_ROWS + TOKENS
+    first = sb * SUBS * packed + TOKENS + (chunk // per) * 2 * NSTATE
+    for n in range(2 * NSTATE):
+        at = pl.ds(first + n, SUBS, stride=packed)
+        out_ref[at, :] = out_ref[at, :] + total[n * SUBS : (n + 1) * SUBS]
 
 
 def spread(scratch, q, values):
@@ -86,12 +97,23 @@
     return jnp.maximum(v, 0.0) + jnp.log1p(jnp.exp(-jnp.abs(v)))
 
 
-def dt_products(dt_ref, wdt_ref, chan_ref, q):
-    return dot(dt_ref[q], wdt_ref[...], ((1,), (1,))) + chan_ref[pl.ds(KCONV + NSTATE + 1, 1), :]
+def chan_row(rest_ref, column):
+    return rest_ref[pl.ds(CH + column, 1), :]
+
+
+def dt_products(dt_ref, small_ref, rest_ref, q):
+    w_dt = small_ref[:, pl.ds(RANK, RANK)]
+    return dot(dt_ref[q], w_dt, ((1,), (1,))) + chan_row(rest_ref, KCONV + NSTATE + 1)
+
+
+def put_rates(rest_ref, rate_ref):
+    for n in range(NSTATE):
+        row = -jnp.exp(chan_row(rest_ref, KCONV + n))
+        rate_ref[n] = jnp.broadcast_to(row, rate_ref.shape[1:])
 
 
 def scan_fwd_kernel(
-    dt_ref, mask_ref, conv_ref, bc_ref, rate_ref, wdt_ref, chan_ref, y_ref, starts_ref, state, bx, stepm, drive, ys
+    dt_ref, mask_ref, conv_ref, bc_ref, small_ref, rest_ref, y_ref, starts_ref, state, bx, stepm, drive, ys, rate_ref
 ):
     seqs = dt_ref.shape[0]
     width = conv_ref.shape[2]
@@ -99,14 +121,15 @@
     @pl.when(pl.program_id(0) == 0)
     def _():
         state[...] = jnp.zeros_like(state)
+        put_rates(rest_ref, rate_ref)
 
     starts_ref[0] = state[...]
     for q in range(seqs):
-        step = softplus(dt_products(dt_ref, wdt_ref, chan_ref, q))
+        step = softplus(dt_products(dt_ref, small_ref, rest_ref, q))
         spread(stepm, q, step + mask_ref[q, :, pl.ds(KCONV - 1, 1)])
         spread(drive, q, step * conv_ref[q].astype(f32))
     for sb in range(seqs // SUBS):
-        expand_inputs(bc_ref, bx, sb)
+        expand_inputs(bc_ref, bx, sb, pl.program_id(0))
         sub = pl.ds(sb * SUBS, SUBS)
 
         def group(g, carry):
@@ -139,27 +162,30 @@
 
 
 def scan_bwd_kernel(
-    dt_ref, mask_ref, conv_ref, bc_ref, rate_ref, wdt_ref, chan_ref, starts_ref, gy_ref,
-    gconv_ref, glow_ref, gdtin_ref, gbc_ref, grate_ref, gbias_ref,
-    flow, bx, stepm, step2, conv2, gy2, gs2, gc2, dec_s, pri_s, acc,
+    dt_ref, mask_ref, conv_ref, bc_ref, small_ref, rest_ref, starts_ref, gy_ref,
+    gconv_ref, glow_ref, proj_ref, grate_ref, gbias_ref,
+    flow, bx, stepm, step2, conv2, gy2, gs2, gc2, dec_s, pri_s, acc, rate_ref,
 ):
     seqs = dt_ref.shape[0]
     width = conv_ref.shape[2]
+    chunk = pl.num_programs(0) - 1 - pl.program_id(0)
 
     @pl.when(pl.program_id(0) == 0)
     def _():
         flow[...] = jnp.zeros_like(flow)
+        proj_ref[...] = jnp.zeros_like(proj_ref)
+        put_rates(rest_ref, rate_ref)
         grate_ref[...] = jnp.zeros_like(grate_ref)
         gbias_ref[...] = jnp.zeros_like(gbias_ref)
 
     for q in range(seqs):
-        step = softplus(dt_products(dt_ref, wdt_ref, chan_ref, q))
+        step = softplus(dt_products(dt_ref, small_ref, rest_ref, q))
         spread(step2, q, step)
         spread(stepm, q, step + mask_ref[q, :, pl.ds(KCONV - 1, 1)])
         spread(conv2, q, conv_ref[q].astype(f32))
         spread(gy2, q, gy_ref[q])
     for sb in range(seqs // SUBS):
-        expand_inputs(bc_ref, bx, sb)
+        expand_inputs(bc_ref, bx, sb, chunk)
         sub = pl.ds(sb * SUBS, SUBS)
         acc[...] = jnp.zeros_like(acc)
 
@@ -217,41 +243,39 @@
             return carry
 
         lax.fori_loop(0, width // LANES, group, 0)
-        lane_sums(acc, gbc_ref, sb)
-    skip = chan_ref[pl.ds(KCONV + NSTATE + 2, 1), :]
+        lane_sums(acc, proj_ref, sb, chunk)
+    skip = chan_row(rest_ref, KCONV + NSTATE + 2)
     for q in range(seqs):
         collect(gconv_ref, q, gc2)
         gconv_ref[q] += skip * gy_ref[q]
         gstep = jnp.concatenate([gs2[g, pl.ds(q * CHUNK, CHUNK), :] for g in range(width // LANES)], axis=1)
-        grad = gstep * jax.nn.sigmoid(dt_products(dt_ref, wdt_ref, chan_ref, q))
+        grad = gstep * jax.nn.sigmoid(dt_products(dt_ref, small_ref, rest_ref, q))
         gbias_ref[...] += jnp.sum(grad.reshape(CHUNK // SUBS, SUBS, width), axis=0)
         low = grad.astype(bf16)
         glow_ref[q] = low
-        gdtin_ref[q] = dot(low, wdt_ref[...], ((1,), (0,)))
+        at = pl.multiple_of(q * (TOKENS + BC_ROWS) + chunk * CHUNK, CHUNK)
+        proj_ref[pl.ds(at, CHUNK), :] = dot(low, small_ref[:, pl.ds(RANK, RANK)], ((1,), (0,)))
 
 
 def whole(shape):
     return pl.BlockSpec(shape, lambda i, *_: (0,) * len(shape))
 
 
-def scan_specs(seqs, width, chan_cols, chunk_of):
+def scan_specs(seqs, width, small, rest, chunk_of):
     def tokens(columns):
         return pl.BlockSpec((seqs, CHUNK, columns), lambda i: (0, chunk_of(i), 0))
 
-    bcs = pl.BlockSpec((1, 2 * NSTATE, seqs, CHUNK), lambda i: (chunk_of(i), 0, 0, 0))
     starts = pl.BlockSpec((1, NSTATE, seqs, width), lambda i: (chunk_of(i), 0, 0, 0))
-    sums = pl.BlockSpec((seqs // SUBS, CHUNK, 2 * NSTATE * SUBS), lambda i: (0, chunk_of(i), 0))
     ins = [
-        tokens(RANK), tokens(MASKS), tokens(width), bcs,
-        whole((NSTATE, SUBS, width)), whole((width, RANK)), whole((chan_cols, width)),
+        tokens(RANK), tokens(MASKS), tokens(width), whole((seqs * BC_ROWS, LANES)), whole(small.shape), whole(rest.shape),
     ]
-    return tokens, starts, sums, ins
-
-
-def scan_forward(dt_in, masks, conv, bc, rates, w_dt, chan):
+    return tokens, starts, ins
+
+
+def scan_forward(dt_in, masks, conv, bc, small, rest):
     seqs, length, width = conv.shape
     chunks = length // CHUNK
-    tokens, starts, _, ins = scan_specs(seqs, width, chan.shape[0], lambda i: i)
+    tokens, starts, ins = scan_specs(seqs, width, small, rest, lambda i: i)
     tall = pltpu.VMEM((width // LANES, seqs * CHUNK, LANES), f32)
     return pl.pallas_call(
         scan_fwd_kernel,
@@ -266,33 +290,34 @@
             pltpu.VMEM((NSTATE, seqs, width), f32),
             pltpu.VMEM((CHUNK, 2 * NSTATE, SUBS, LANES), f32),
             tall, tall, tall,
+            pltpu.VMEM((NSTATE, SUBS, width), f32),
         ],
         compiler_params=pltpu.CompilerParams(vmem_limit_bytes=50 * 2**20),
         cost_estimate=pl.CostEstimate(
             flops=8 * conv.size * NSTATE, bytes_accessed=100 * 10**6, transcendentals=conv.size * NSTATE
         ),
         name="scan_forward",
-    )(dt_in, masks, conv, bc, rates, w_dt, chan)
-
-
-def scan_backward(dt_in, masks, conv, bc, rates, w_dt, chan, starts, grad_y):
+    )(dt_in, masks, conv, bc, small, rest)
+
+
+def scan_backward(dt_in, masks, conv, bc, small, rest, starts, grad_y):
     seqs, length, width = conv.shape
     chunks = length // CHUNK
-    tokens, start_spec, sums, ins = scan_specs(seqs, width, chan.shape[0], lambda i: chunks - 1 - i)
+    tokens, start_spec, ins = scan_specs(seqs, width, small, rest, lambda i: chunks - 1 - i)
+    packed = (seqs * (TOKENS + BC_ROWS), LANES)
     tall = pltpu.VMEM((width // LANES, seqs * CHUNK, LANES), f32)
     return pl.pallas_call(
         scan_bwd_kernel,
         grid=(chunks,),
         in_specs=ins + [start_spec, tokens(width)],
         out_specs=[
-            tokens(width), tokens(width), tokens(RANK), sums,
+            tokens(width), tokens(width), whole(packed),
             whole((NSTATE, SUBS, width)), whole((SUBS, width)),
         ],
         out_shape=[
             jax.ShapeDtypeStruct(conv.shape, f32),
             jax.ShapeDtypeStruct(conv.shape, bf16),
-            jax.ShapeDtypeStruct((seqs, length, RANK), f32),
-            jax.ShapeDtypeStruct((seqs // SUBS, length, 2 * NSTATE * SUBS), f32),
+            jax.ShapeDtypeStruct(packed, f32),
             jax.ShapeDtypeStruct((NSTATE, SUBS, width), f32),
             jax.ShapeDtypeStruct((SUBS, width), f32),
         ],
@@ -303,13 +328,29 @@
             pltpu.VMEM((CHUNK, NSTATE, SUBS, LANES), f32),
             pltpu.VMEM((CHUNK + 1, NSTATE, SUBS, LANES), f32),
             pltpu.VMEM((CHUNK, 2 * NSTATE, SUBS, LANES), f32),
+            pltpu.VMEM((NSTATE, SUBS, width), f32),
         ],
         compiler_params=pltpu.CompilerParams(vmem_limit_bytes=56 * 2**20),
         cost_estimate=pl.CostEstimate(
             flops=24 * conv.size * NSTATE, bytes_accessed=300 * 10**6, transcendentals=conv.size * NSTATE
         ),
         name="scan_backward",
-    )(dt_in, masks, conv, bc, rates, w_dt, chan, starts, grad_y)
+    )(dt_in, masks, conv, bc, small, rest, starts, grad_y)
+
+
+def put_combined(place_ref, blocks, w_gate, w_out):
+    @pl.when(pl.program_id(0) == 0)
+    def _():
+        for k, block in enumerate(blocks):
+            at = place_ref[2] ^ k
+            rows, width = block.shape[0] // 2, block.shape[1]
+            w_gate[pl.ds(pl.multiple_of(at * rows, rows), rows), :] = block[pl.ds(0, rows), :]
+            if w_out is not None:
+                count = w_out.shape[1] // width
+                sub = rows // count
+                for i in range(count):
+                    part = block[pl.ds(rows + i * sub, sub), :]
+                    w_out[pl.ds(pl.multiple_of(at * sub, sub), sub), pl.ds(i * width, width)] = part
 
 
 def put_blocks(place_ref, blocks, out):
@@ -333,9 +374,9 @@
 
 
 def conv_sum(terms, chan_ref):
-    total = chan_ref[pl.ds(KCONV + NSTATE, 1), :]
+    total = chan_row(chan_ref, KCONV + NSTATE)
     for k, term in enumerate(terms):
-        total = total + chan_ref[pl.ds(k, 1), :] * term
+        total = total + chan_row(chan_ref, k) * term
     return total
 
 
@@ -345,27 +386,66 @@
         ref[0, pl.ds(start + i * count, count), :] = values[:, i * LANES : (i + 1) * LANES]
 
 
-def front_kernel(planes, place_ref, hid_ref, gain_ref, mask_ref, chan_ref, wx_ref, wbc_ref, *refs):
-    blocks = refs[:planes]
-    normed_ref, inner_ref, conv_ref, proj_ref, weights = refs[planes:]
+def token_masks(ids):
+    length = ids.shape[1]
+    at = lax.broadcasted_iota(jnp.int32, (SUBS, length), 1)
+    row = lax.broadcasted_iota(jnp.int32, (SUBS, length), 0)
+    every = jnp.broadcast_to(ids, (SUBS, length))
+    rows = jnp.zeros((SUBS, length), f32)
+    for k in range(KCONV):
+        offset = max(KCONV - 1 - k, 1)
+        same = (pltpu.roll(every, offset, 1) == every) & (at >= offset)
+        if k == KCONV - 1:
+            same = ~same
+        rows = jnp.where((row == k) & same, 1.0, rows)
+    unit = lax.broadcasted_iota(jnp.int32, (length, length), 0) == lax.broadcasted_iota(jnp.int32, (length, length), 1)
+    columns = dot(unit.astype(bf16), rows.astype(bf16), ((1,), (1,)))
+    column = lax.broadcasted_iota(jnp.int32, columns.shape, 1)
+    return jnp.where(column == KCONV - 1, columns * CUT, columns)
+
+
+def front_kernel(gain_parts, planes, place_ref, hid_ref, ids_ref, *refs):
+    gains, smalls, blocks = refs[:1], refs[1 : 1 + planes], refs[1 + planes : 1 + 2 * planes]
+    normed_ref, inner_ref, conv_ref, proj_ref, mask_ref, small_ref, rest_ref, gain_ref, weights = refs[1 + 2 * planes :]
     put_blocks(place_ref, blocks, weights)
+    put_blocks(place_ref, smalls, small_ref)
+
+    @pl.when(pl.program_id(0) == 0)
+    def _():
+        rest_ref[...] = small_ref[:, pl.ds(2 * RANK, LANES)].astype(f32).T
+        if gain_parts == 1:
+            gain_ref[...] = gains[0][0]
+        else:
+            for e in range(2):
+                for k in range(planes):
+                    columns = gains[0].shape[2]
+                    at = ((place_ref[2] ^ k) * 2 + (place_ref[1] ^ e)) * columns
+                    gain_ref[:, pl.ds(pl.multiple_of(at, columns), columns)] = gains[0][e * planes + k]
+
     normed = (normalised(hid_ref[0]) * gain_ref[...]).astype(bf16)
     normed_ref[0] = normed
     inner = dot(normed, weights[...], ((1,), (0,)))
     inner_ref[0] = inner
-    pre = conv_sum(earlier_rows(inner, mask_ref[0]), chan_ref)
+    masks = token_masks(ids_ref[0])
+    mask_ref[0] = masks
+    pre = conv_sum(earlier_rows(inner, masks), rest_ref)
     conv = jax.nn.silu(pre).astype(bf16)
     conv_ref[0] = conv
-    length = conv.shape[0]
-    proj_ref[0, pl.ds(0, length), :] = dot(conv, wx_ref[...], ((1,), (1,)))
-    put_columns(proj_ref, length, dot(wbc_ref[...], conv, ((1,), (1,))))
+    proj_ref[0, pl.ds(0, TOKENS), :] = dot(conv, small_ref[:, pl.ds(0, RANK)], ((1,), (0,)))
+    put_columns(proj_ref, TOKENS, dot(rest_ref[pl.ds(0, CH), :].astype(bf16), conv, ((1,), (1,))))
 
 
 def per_sequence(kernel, place, stacked, fixed, outs, scratch, flops, name):
     seqs = stacked[0].shape[0]
-
-    def block(shape):
-        return pl.BlockSpec((1,) + tuple(shape[1:]), lambda i, p: (i, 0, 0))
+    half = seqs // 2
+    index = {
+        "every": lambda i, p: ((i + half) % seqs, 0, 0),
+        "other": lambda i, p: (jnp.minimum(i, half - 1), 0, 0),
+        "own": lambda i, p: (jnp.maximum(i - half, 0), 0, 0),
+    }
+
+    def block(shape, kind="every"):
+        return pl.BlockSpec((1,) + tuple(shape[1:]), index[kind])
 
     return pl.pallas_call(
         kernel,
@@ -373,34 +453,52 @@
             num_scalar_prefetch=1,
             grid=(seqs,),
             in_specs=[block(v.shape) for v in stacked] + [whole(v.shape) for v in fixed],
-            out_specs=[block(shape) if per else whole(shape) for shape, _, per in outs],
+            out_specs=[whole(shape) if kind == "whole" else block(shape, kind) for shape, _, kind in outs],
             scratch_shapes=scratch,
         ),
-        out_shape=[jax.ShapeDtypeStruct(shape, kind) for shape, kind, _ in outs],
+        out_shape=[jax.ShapeDtypeStruct(shape, dtype) for shape, dtype, _ in outs],
         compiler_params=pltpu.CompilerParams(vmem_limit_bytes=56 * 2**20),
         cost_estimate=pl.CostEstimate(flops=flops, bytes_accessed=40 * 10**6, transcendentals=0),
         name=name,
     )(place, *stacked, *fixed)
 
 
-def front(place, hidden_all, gain, masks, chan, w_xdt, w_xbc, inner_blocks):
+def put_part(part, own_ref, other_ref):
+    half = pl.num_programs(0) // 2
+
+    @pl.when(pl.program_id(0) < half)
+    def _():
+        other_ref[0] = part.astype(bf16)
+
+    @pl.when(pl.program_id(0) >= half)
+    def _():
+        own_ref[0] = part.astype(bf16)
+
+
+def front(place, hidden_all, ids, gains, small_blocks, inner_blocks):
     seqs, length, model = hidden_all.shape
-    width = w_xbc.shape[1]
-    packed = length + 2 * NSTATE * length // LANES
-
-    def kernel(place_ref, hid, mask, gain_ref, chan_ref, wx, wbc, *refs):
-        front_kernel(len(inner_blocks), place_ref, hid, gain_ref, mask, chan_ref, wx, wbc, *refs)
-
+    planes = len(inner_blocks)
+    width = inner_blocks[0].shape[1]
+    packed = TOKENS + BC_ROWS
+
+    def kernel(*refs):
+        front_kernel(gains.shape[0], planes, *refs)
+
+    columns = small_blocks[0].shape[1]
     return per_sequence(
         kernel,
         place,
-        [hidden_all, masks],
-        [gain, chan, w_xdt, w_xbc, *inner_blocks],
+        [hidden_all, ids],
+        [gains, *small_blocks, *inner_blocks],
         [
-            ((seqs, length, model), bf16, True),
-            ((seqs, length, width), f32, True),
-            ((seqs, length, width), bf16, True),
-            ((seqs, packed, RANK), f32, True),
+            ((seqs, length, model), bf16, "every"),
+            ((seqs, length, width), f32, "every"),
+            ((seqs, length, width), bf16, "every"),
+            ((seqs, packed, RANK), f32, "every"),
+            ((seqs, length, MASKS), f32, "every"),
+            ((width, columns), bf16, "whole"),
+            ((LANES, width), f32, "whole"),
+            ((1, model), f32, "whole"),
         ],
         [pltpu.VMEM((model, width), bf16)],
         2 * seqs * length * model * width,
@@ -408,16 +506,14 @@
     )
 
 
-def middle(place, normed, upstream, scanned, conv_out, chan, gate_blocks, out_blocks):
+def middle(place, normed, upstream, scanned, conv_out, rest, blocks):
     seqs, length, model = normed.shape
     width = conv_out.shape[2]
-    planes = len(gate_blocks)
+    planes = len(blocks)
 
     def kernel(place_ref, normed_ref, up_ref, y_ref, conv_ref, chan_ref, *refs):
-        gates, outs = refs[:planes], refs[planes : 2 * planes]
-        part_ref, mixed_ref, gy_ref, ggate_ref, gskip_ref, w_gate, w_out = refs[2 * planes :]
-        put_blocks(place_ref, gates, w_gate)
-        put_blocks(place_ref, outs, w_out)
+        own_ref, other_ref, mixed_ref, gy_ref, ggate_ref, gskip_ref, w_gate, w_out = refs[planes:]
+        put_combined(place_ref, refs[:planes], w_gate, w_out)
 
         @pl.when(pl.program_id(0) == 0)
         def _():
@@ -427,10 +523,10 @@
         conv = conv_ref[0].astype(f32)
         sigma = jax.nn.sigmoid(gate)
         act = gate * sigma
-        mixer = y_ref[0] + chan_ref[pl.ds(KCONV + NSTATE + 2, 1), :] * conv
+        mixer = y_ref[0] + chan_row(chan_ref, KCONV + NSTATE + 2) * conv
         mixed = (mixer * act).astype(bf16)
         mixed_ref[0] = mixed
-        part_ref[0] = dot(mixed, w_out[...], ((1,), (0,))).astype(part_ref.dtype)
+        put_part(dot(mixed, w_out[...], ((1,), (0,))), own_ref, other_ref)
         grad_mixed = dot(up_ref[0], w_out[...], ((1,), (1,)))
         gy = grad_mixed * act
         gy_ref[0] = gy
@@ -441,13 +537,14 @@
         kernel,
         place,
         [normed, upstream, scanned, conv_out],
-        [chan, *gate_blocks, *out_blocks],
+        [rest, *blocks],
         [
-            ((seqs, length, model), PARTS, True),
-            ((seqs, length, width), bf16, True),
-            ((seqs, length, width), f32, True),
-            ((seqs, length, width), bf16, True),
-            ((SUBS, width), f32, False),
+            ((seqs // 2, length, model), bf16, "own"),
+            ((seqs // 2, length, model), bf16, "other"),
+            ((seqs, length, width), bf16, "every"),
+            ((seqs, length, width), f32, "every"),
+            ((seqs, length, width), bf16, "every"),
+            ((SUBS, width), f32, "whole"),
         ],
         [pltpu.VMEM((model, width), bf16), pltpu.VMEM((width, model), bf16)],
         6 * seqs * length * model * width,
@@ -455,66 +552,81 @@
     )
 
 
-def back_conv(place, grad_conv, gp_dt, gp_bc, inner, masks, chan, w_xdt, w_xbc):
+def back_conv(place, grad_conv, gp_dt, gp_bc, inner, conv_out, masks, small, rest):
     seqs, length, width = grad_conv.shape
 
-    def kernel(place_ref, gconv_ref, gdt_ref, gbc_ref, inner_ref, mask_ref, chan_ref, wx_ref, wbc_ref, ginner_ref, sums_ref):
+    def kernel(
+        place_ref, gconv_ref, gdt_ref, gbc_ref, inner_ref, conv_ref, mask_ref, small_ref, rest_ref,
+        ginner_ref, sums_ref, gxbc_ref,
+    ):
         @pl.when(pl.program_id(0) == 0)
         def _():
             sums_ref[...] = jnp.zeros_like(sums_ref)
+            gxbc_ref[...] = jnp.zeros_like(gxbc_ref)
 
         masks_now = mask_ref[0]
         terms = earlier_rows(inner_ref[0], masks_now)
-        pre = conv_sum(terms, chan_ref)
-        total = gconv_ref[0] + dot(gdt_ref[0], wx_ref[...], ((1,), (0,)))
-        total = total + dot(gbc_ref[0], wbc_ref[...], ((0,), (0,)))
+        pre = conv_sum(terms, rest_ref)
+        packed = gbc_ref[0].astype(bf16)
+        gbc = jnp.concatenate([packed[i * CH : (i + 1) * CH] for i in range(length // LANES)], axis=1)
+        gxbc_ref[...] += dot(gbc, conv_ref[0], ((1,), (0,)))
+        total = gconv_ref[0] + dot(gdt_ref[0], small_ref[:, pl.ds(0, RANK)], ((1,), (1,)))
+        total = total + dot(gbc, rest_ref[pl.ds(0, CH), :].astype(bf16), ((0,), (0,)))
         grad = total * silu_slope(pre)
         for k in range(KCONV):
             sums_ref[k] += jnp.sum((grad * terms[k]).reshape(length // SUBS, SUBS, width), axis=0)
         sums_ref[KCONV] += jnp.sum(grad.reshape(length // SUBS, SUBS, width), axis=0)
-        ginner = chan_ref[pl.ds(KCONV - 1, 1), :] * grad
+        ginner = chan_row(rest_ref, KCONV - 1) * grad
         for k in range(KCONV - 1):
             moved = pltpu.roll(grad * masks_now[:, k : k + 1], length - (KCONV - 1 - k), 0)
-            ginner = ginner + chan_ref[pl.ds(k, 1), :] * moved
+            ginner = ginner + chan_row(rest_ref, k) * moved
         ginner_ref[0] = ginner.astype(bf16)
 
     return per_sequence(
         kernel,
         place,
-        [grad_conv, gp_dt, gp_bc, inner, masks],
-        [chan, w_xdt, w_xbc],
-        [((seqs, length, width), bf16, True), ((KCONV + 1, SUBS, width), f32, False)],
+        [grad_conv, gp_dt, gp_bc, inner, conv_out, masks],
+        [small, rest],
+        [
+            ((seqs, length, width), bf16, "every"),
+            ((KCONV + 1, SUBS, width), f32, "whole"),
+            ((CH, width), f32, "whole"),
+        ],
         [],
         2 * seqs * length * width * RANK,
         "back_conv",
     )
 
 
-def back_normed(place, grad_inner, grad_gate, hidden_all, inner_blocks, gate_blocks):
+def back_normed(place, grad_inner, grad_gate, hidden_all, inner_blocks, blocks):
     seqs, length, width = grad_inner.shape
     model = hidden_all.shape[2]
-    planes = len(gate_blocks)
+    planes = len(blocks)
 
     def kernel(place_ref, ginner_ref, ggate_ref, hid_ref, *refs):
         inners, gates = refs[:planes], refs[planes : 2 * planes]
-        part_ref, ggain_ref, w_inner, w_gate = refs[2 * planes :]
+        own_ref, other_ref, ggain_ref, w_inner, w_gate = refs[2 * planes :]
         put_blocks(place_ref, inners, w_inner)
-        put_blocks(place_ref, gates, w_gate)
+        put_combined(place_ref, gates, w_gate, None)
 
         @pl.when(pl.program_id(0) == 0)
         def _():
             ggain_ref[...] = jnp.zeros_like(ggain_ref)
 
         part = dot(ginner_ref[0], w_inner[...], ((1,), (1,))) + dot(ggate_ref[0], w_gate[...], ((1,), (1,)))
-        part_ref[0] = part.astype(part_ref.dtype)
+        put_part(part, own_ref, other_ref)
         ggain_ref[...] += jnp.sum((part * normalised(hid_ref[0])).reshape(length // SUBS, SUBS, model), axis=0)
 
     return per_sequence(
         kernel,
         place,
         [grad_inner, grad_gate, hidden_all],
-        [*inner_blocks, *gate_blocks],
-        [((seqs, length, model), PARTS, True), ((SUBS, model), f32, False)],
+        [*inner_blocks, *blocks],
+        [
+            ((seqs // 2, length, model), bf16, "own"),
+            ((seqs // 2, length, model), bf16, "other"),
+            ((SUBS, model), f32, "whole"),
+        ],
         [pltpu.VMEM((model, width), bf16), pltpu.VMEM((model, width), bf16)],
         4 * seqs * length * model * width,
         "back_normed",
@@ -583,32 +695,32 @@
 
 
 def gather_first_kernel(
-    hid, in_own, in_other, small, gain, ids, hid_all, weights, small_all, gain_all, ids_all, send_sems, recv_sems, local_sems
+    hid, cot, in_own, in_other, small, gain, ids,
+    hid_all, cot_all, weights, gate, small_all, gain_all, ids_all, send_sems, recv_sems, local_sems,
 ):
     me = Peers()
     net = Sends(send_sems, recv_sems)
     rows = in_own.shape[0]
+    width = in_own.shape[1] // 2
     half = hid.shape[0] // 2
     low, high = pl.ds(0, half), pl.ds(half, half)
     inside = (me.z == 1) | (me.z == 2)
     outside = (me.z == 0) | (me.z == 3)
     mine = pl.ds(pl.multiple_of(me.c * rows, rows), rows)
     local = [
-        pltpu.make_async_copy(source, target, local_sems.at[i])
-        for i, (source, target) in enumerate(
-            [
-                (in_own, weights.at[0, mine]),
-                (hid, hid_all.at[0]),
-                (small, small_all.at[0]),
-                (gain, gain_all.at[0]),
-                (ids, ids_all.at[0]),
-            ]
-        )
+        pltpu.make_async_copy(hid, hid_all.at[0], local_sems.at[0]),
+        pltpu.make_async_copy(cot, cot_all.at[0], local_sems.at[1]),
     ]
     for copy in local:
         copy.start()
+    weights[0, mine, :] = in_own[:, :width]
+    gate[mine, :] = in_own[:, width:]
+    small_all[0] = small[...]
+    gain_all[0] = gain[...]
+    ids_all[0] = ids[...]
     me.greet(True)
-    net.start(0, in_other, weights.at[0, mine], me.core())
+    net.start(0, in_other.at[:, pl.ds(0, width)], weights.at[0, mine], me.core())
+    net.start(26, in_other.at[:, pl.ds(width, width)], gate.at[mine], me.core())
     for k in (1, 2, 3):
         net.start(k, ids, ids_all.at[k], me.rep(k))
         net.start(3 + k, gain, gain_all.at[k], me.plane(k))
@@ -618,20 +730,22 @@
     net.start(12, hid.at[low], hid_all.at[1, low], me.rep(1))
     net.start(13, hid.at[high], hid_all.at[2, high], me.rep(2))
     net.start(14, hid, hid_all.at[4], me.core())
-    local[0].wait()
     net.arrived(0)
     own = weights.at[0]
     net.start(15, own, weights.at[2], me.plane(2))
     net.start(16, own, weights.at[1], me.plane(1))
     across = net.make(17, own, weights.at[3], me.plane(3))
-    local[3].wait()
-    local[4].wait()
     net.arrived(1, 2, 3, 4, 5, 6)
     net.start(18, ids_all.at[pl.ds(0, 4)], ids_all.at[pl.ds(4, 4)], me.core())
     net.start(19, gain_all.at[pl.ds(0, 4)], gain_all.at[pl.ds(4, 4)], me.core())
     net.arrived(10, 11)
     net.start(20, hid_all.at[1, high], hid_all.at[3, high], me.rep(2))
     net.start(21, hid_all.at[2, low], hid_all.at[3, low], me.rep(1))
+    net.start(27, cot.at[high], cot_all.at[1, high], me.rep(1))
+    net.start(28, cot.at[low], cot_all.at[2, low], me.rep(2))
+    net.start(29, cot.at[low], cot_all.at[1, low], me.rep(1))
+    net.start(30, cot.at[high], cot_all.at[2, high], me.rep(2))
+    net.start(31, cot, cot_all.at[4], me.core())
     net.arrived(12)
     net.start(22, hid_all.at[1], hid_all.at[5], me.core())
     net.arrived(13)
@@ -656,9 +770,18 @@
     def _():
         onward.wait_recv()
 
-    net.arrived(7, 8, 9, 14, 18, 19, 22, 23, 25)
-    local[1].wait()
-    local[2].wait()
+    net.arrived(27, 28)
+    net.start(32, cot_all.at[1, high], cot_all.at[3, high], me.rep(2))
+    net.start(33, cot_all.at[2, low], cot_all.at[3, low], me.rep(1))
+    net.arrived(29)
+    net.start(34, cot_all.at[1], cot_all.at[5], me.core())
+    net.arrived(30)
+    net.start(35, cot_all.at[2], cot_all.at[6], me.core())
+    net.arrived(32, 33)
+    net.start(36, cot_all.at[3], cot_all.at[7], me.core())
+    net.arrived(7, 8, 9, 14, 18, 19, 22, 23, 25, 26, 31, 34, 35, 36)
+    for copy in local:
+        copy.wait()
     net.sent(*[slot for slot in net.made if slot not in (17, 24)])
 
     @pl.when(inside)
@@ -667,29 +790,35 @@
         onward.wait_send()
 
 
-def gather_first(hid, in_own, in_other, small, gain, ids):
+def gather_first(hid, cot, in_own, in_other, small, gain, ids):
     length, model = hid.shape
+    rows, width = in_own.shape[0], in_own.shape[1] // 2
     anywhere = pl.BlockSpec(memory_space=pl.ANY)
+    vmem = pl.BlockSpec(memory_space=pltpu.VMEM)
     return pl.pallas_call(
         gather_first_kernel,
-        in_specs=[anywhere] * 6,
-        out_specs=[anywhere] * 5,
+        in_specs=[vmem] * 7,
+        out_specs=[anywhere] * 2 + [vmem] * 5,
         out_shape=[
             jax.ShapeDtypeStruct((8, length, model), bf16),
-            jax.ShapeDtypeStruct((4, 2 * in_own.shape[0], in_own.shape[1]), bf16),
+            jax.ShapeDtypeStruct((8, length, model), bf16),
+            jax.ShapeDtypeStruct((4, 2 * rows, width), bf16),
+            jax.ShapeDtypeStruct((2 * rows, width), bf16),
             jax.ShapeDtypeStruct((4,) + small.shape, bf16),
             jax.ShapeDtypeStruct((8,) + gain.shape, f32),
             jax.ShapeDtypeStruct((8,) + ids.shape, f32),
         ],
         scratch_shapes=[
-            pltpu.SemaphoreType.DMA((26,)),
-            pltpu.SemaphoreType.DMA((26,)),
-            pltpu.SemaphoreType.DMA((5,)),
-        ],
-        compiler_params=pltpu.CompilerParams(collective_id=1, has_side_effects=True),
+            pltpu.SemaphoreType.DMA((37,)),
+            pltpu.SemaphoreType.DMA((37,)),
+            pltpu.SemaphoreType.DMA((2,)),
+        ],
+        compiler_params=pltpu.CompilerParams(
+            collective_id=1, has_side_effects=True, vmem_limit_bytes=24 * 2**20
+        ),
         cost_estimate=pl.CostEstimate(flops=0, bytes_accessed=100 * 10**6, transcendentals=0),
         name="gather_first",
-    )(hid, in_own, in_other, small, gain, ids)
+    )(hid, cot, in_own, in_other, small, gain, ids)
 
 
 def reduce_plane_kernel(part, dt_all, bc_all, near, pair, far, send_sems, recv_sems):
@@ -751,7 +880,7 @@
 
 
 def finish_kernel(
-    part, gin, small, grad_normed, pieces, small_all,
+    part, other_part, gin, small, grad_normed, pieces, small_all,
     own_part, core_part, pair, far_one, far_two, from_one, from_two,
     blocks, ends, middle_block, block_one, block_two, two_out, total, small_own, small_in, small_total,
     send_sems, recv_sems, local_sems,
@@ -770,7 +899,7 @@
         return ref.at[pl.ds(pl.multiple_of(me.flip(me.z, k) * size, size), size)]
 
     local = [
-        pltpu.make_async_copy(part.at[pl.ds(0, 4)], own_part, local_sems.at[0]),
+        pltpu.make_async_copy(part, own_part, local_sems.at[0]),
         pltpu.make_async_copy(block(gin, 0, rows), blocks.at[0], local_sems.at[1]),
         pltpu.make_async_copy(block(gin, 2, rows), blocks.at[1], local_sems.at[2]),
         pltpu.make_async_copy(block(small, 0, small_rows), small_own, local_sems.at[3]),
@@ -779,9 +908,7 @@
         copy.start()
     me.greet(True)
     for i, k in enumerate((3, 1, 2, 0)):
-        net.start(i, part.at[4 + k], core_part.at[k], me.core())
-    for k in (1, 2, 3):
-        net.start(3 + k, block(small, k, small_rows), small_in.at[k - 1], me.plane(k))
+        net.start(i, other_part.at[k], core_part.at[k], me.core())
     to_ends = net.make(7, block(gin, 3, rows), ends, me.plane(1))
     to_middle = net.make(8, block(gin, 3, rows), middle_block, me.plane(3))
 
@@ -795,13 +922,6 @@
 
     two = net.make(9, two_out, block_two, me.plane(2))
     local[2].wait()
-
-    @pl.when(outside)
-    def _():
-        two_out[...] = blocks[1]
-        two.start()
-
-    net.start(10, block(gin, 1, rows), block_one, me.plane(1))
     local[0].wait()
     for i, k in enumerate((3, 1, 2)):
         net.arrived(i)
@@ -814,18 +934,51 @@
         else:
             net.start(14, pair.at[1, high], from_two.at[high], me.rep(2))
 
+    @pl.when(outside)
+    def _():
+        to_ends.wait_send()
+        two_out[...] = blocks[1]
+        two.start()
+
+    net.start(10, block(gin, 1, rows), block_one, me.plane(1))
+
     @pl.when(inside)
     def _():
         to_ends.wait_recv()
         two_out[...] = (blocks[1].astype(f32) + ends[...].astype(f32)).astype(bf16)
         two.start()
 
+    for k in (1, 2, 3):
+        net.start(3 + k, block(small, k, small_rows), small_in.at[k - 1], me.plane(k))
     net.arrived(11)
     pair[1, low] = (pair[1, low].astype(f32) + far_one[...].astype(f32)).astype(bf16)
     net.start(15, pair.at[1, low], from_two.at[low], me.rep(2))
     net.arrived(12)
     pair[0, high] = (pair[0, high].astype(f32) + far_two[...].astype(f32)).astype(bf16)
     net.start(16, pair.at[0, high], from_one.at[high], me.rep(1))
+    local[1].wait()
+    net.arrived(10, 9)
+    summed = blocks[0].astype(f32) + block_one[...].astype(f32) + block_two[...].astype(f32)
+
+    @pl.when(inside)
+    def _():
+        to_middle.wait_recv()
+        total[...] = (summed + middle_block[...].astype(f32)).astype(bf16)
+
+    @pl.when(outside)
+    def _():
+        total[...] = summed.astype(bf16)
+
+    mine = total.at[pl.ds(pl.multiple_of(me.c * own_rows, own_rows), own_rows)]
+    other = total.at[pl.ds(pl.multiple_of((1 - me.c) * own_rows, own_rows), own_rows)]
+    net.start(20, other, pieces.at[4], me.core())
+    kept = pltpu.make_async_copy(mine, pieces.at[0], local_sems.at[5])
+    kept.start()
+    for k in (1, 2, 3):
+        net.start(20 + k, mine, pieces.at[k], me.rep(k))
+    net.arrived(20)
+    for k in (1, 2, 3):
+        net.start(23 + k, pieces.at[4], pieces.at[4 + k], me.rep(k))
     local[3].wait()
     net.arrived(4, 5, 6)
     small_total[...] = small_own[...] + small_in[0] + small_in[1] + small_in[2]
@@ -833,29 +986,6 @@
     kept_small.start()
     for k in (1, 2, 3):
         net.start(16 + k, small_total, small_all.at[k], me.rep(k))
-    local[1].wait()
-    net.arrived(10, 9)
-    summed = blocks[0].astype(f32) + block_one[...].astype(f32) + block_two[...].astype(f32)
-
-    @pl.when(inside)
-    def _():
-        to_middle.wait_recv()
-        total[...] = (summed + middle_block[...].astype(f32)).astype(bf16)
-
-    @pl.when(outside)
-    def _():
-        total[...] = summed.astype(bf16)
-
-    mine = total.at[pl.ds(pl.multiple_of(me.c * own_rows, own_rows), own_rows)]
-    other = total.at[pl.ds(pl.multiple_of((1 - me.c) * own_rows, own_rows), own_rows)]
-    net.start(20, other, pieces.at[1, 0], me.core())
-    kept = pltpu.make_async_copy(mine, pieces.at[0, 0], local_sems.at[5])
-    kept.start()
-    for k in (1, 2, 3):
-        net.start(20 + k, mine, pieces.at[0, k], me.rep(k))
-    net.arrived(20)
-    for k in (1, 2, 3):
-        net.start(23 + k, pieces.at[1, 0], pieces.at[1, k], me.rep(k))
     net.arrived(3)
     net.arrived(13, 14, 15, 16)
     grad_normed[...] = (
@@ -866,16 +996,12 @@
     kept_small.wait()
     net.sent(*[slot for slot in net.made if slot not in (7, 8)])
 
-    @pl.when(outside)
-    def _():
-        to_ends.wait_send()
-
     @pl.when(inside)
     def _():
         to_middle.wait_send()
 
 
-def finish(part, gin, small):
+def finish(part, other_part, gin, small):
     _, length, model = part.shape
     rows, width = gin.shape[0] // 4, gin.shape[1]
     small_rows, cols = small.shape[0] // 4, small.shape[1]
@@ -883,11 +1009,11 @@
     big = (length, model)
     return pl.pallas_call(
         finish_kernel,
-        in_specs=[anywhere] * 3,
+        in_specs=[anywhere] * 4,
         out_specs=[pl.BlockSpec(memory_space=pltpu.VMEM), anywhere, anywhere],
         out_shape=[
             jax.ShapeDtypeStruct(big, f32),
-            jax.ShapeDtypeStruct((2, 4, rows // 2, width), bf16),
+            jax.ShapeDtypeStruct((8, rows // 2, width), bf16),
             jax.ShapeDtypeStruct((4, small_rows, cols), f32),
         ],
         scratch_shapes=[
@@ -917,7 +1043,7 @@
         ),
         cost_estimate=pl.CostEstimate(flops=0, bytes_accessed=150 * 10**6, transcendentals=0),
         name="finish",
-    )(part, gin, small)
+    )(part, other_part, gin, small)
 
 
 class Links:
@@ -950,14 +1076,8 @@
         one, two = self.rep(value, 1), self.rep(value, 2)
         return [value, one, two, self.across(one, two, half)]
 
-    def gather_near(self, value):
-        return [value] + [self.rep(value, k) for k in ((1, 2) if self.reps == 4 else range(1, self.reps))]
-
-    def gather_far(self, near):
-        return [self.across(near[1], near[2], near[0].shape[0] // 2)] if self.reps == 4 else []
-
-    def across(self, one, two, half):
-        return jnp.concatenate([self.rep(two[:half], 1), self.rep(one[half:], 2)], axis=0)
+    def gather_rep_list(self, value):
+        return [value] + [self.rep(value, k) for k in range(1, self.reps)]
 
     def gather_plane(self, value):
         near = jnp.stack([value] + [self.rep(value, k) for k in range(1, self.reps)])
@@ -998,8 +1118,19 @@
             total = total + other.astype(f32)
         return total.astype(value.dtype)
 
+    def send_half(self, part, k):
+        return self.rep(part[k : 2 * k], k)
+
+    def sum_halves(self, part, moved):
+        k = self.reps // 2
+        while k > 1:
+            part = (part[:k].astype(f32) + moved.astype(f32)).astype(part.dtype)
+            k //= 2
+            moved = self.send_half(part, k)
+        return part[0].astype(f32) + moved[0].astype(f32)
+
     def add_pair(self, part, far):
-        return (part[: self.reps].astype(f32) + far.astype(f32)).astype(bf16)
+        return (part.astype(f32) + far.astype(f32)).astype(bf16)
 
     def pair_rows(self, own, other):
         first = jnp.where(self.c == 0, own, other)
@@ -1035,7 +1166,7 @@
     master_ref, first_ref, second_ref = refs[2 * reps : 2 * reps + 3]
     first_out, second_out, master_out = refs[-3:]
     r, c = place_ref[0], place_ref[1]
-    sub = pieces[0].shape[1]
+    sub = LANES
     for e in range(2):
         for k in range(reps):
             at = ((c ^ e) * reps + (r ^ k)) * sub
@@ -1056,8 +1187,8 @@
     sub = LANES
     block = 2 * reps * sub
     steps = columns // 2 // block
-    wide = pl.BlockSpec((rows, block), lambda i, place_ref: (0, half * steps + i))
-    thin = pl.BlockSpec((rows, sub), lambda i, place_ref: (0, i))
+    wide = pl.BlockSpec((rows, block), lambda i, p: (0, half * steps + i))
+    thin = [pl.BlockSpec((rows, sub), functools.partial(lambda at, i, p: (at, i), at)) for _, at in pieces]
     anywhere = pl.BlockSpec(memory_space=pl.ANY)
     if earlier is None:
         earlier = (master, first, second)
@@ -1069,7 +1200,7 @@
         grid_spec=pltpu.PrefetchScalarGridSpec(
             num_scalar_prefetch=1,
             grid=(steps,),
-            in_specs=[thin] * (2 * reps) + [wide] * 3 + [anywhere] * 3,
+            in_specs=thin + [wide] * 3 + [anywhere] * 3,
             out_specs=[wide] * 3,
         ),
         out_shape=[jax.ShapeDtypeStruct(master.shape, f32)] * 3,
@@ -1077,7 +1208,7 @@
         compiler_params=pltpu.CompilerParams(vmem_limit_bytes=32 * 2**20),
         cost_estimate=pl.CostEstimate(flops=10 * master.size, bytes_accessed=13 * master.size, transcendentals=master.size),
         name="adam_in",
-    )(place, *pieces, master, first, second, *earlier)
+    )(place, *[array for array, _ in pieces], master, first, second, *earlier)
 
 
 def adam_out_kernel(place_ref, *refs):
@@ -1097,14 +1228,15 @@
     rows, columns = master.shape
     reps = len(pieces)
     sub = rows // reps
-    wide = columns // 2
+    high, wide = pieces[0].shape
+    first_block = high // 2 // sub
     mine = pl.BlockSpec((sub, wide), lambda k, j, p: (p[0] ^ k, j))
-    piece = pl.BlockSpec((sub, wide), lambda k, j, p: (0, j))
+    piece = pl.BlockSpec((sub, wide), lambda k, j, p: (first_block + j, 0))
     return pl.pallas_call(
         adam_out_kernel,
         grid_spec=pltpu.PrefetchScalarGridSpec(
             num_scalar_prefetch=1,
-            grid=(reps, 2),
+            grid=(reps, columns // wide),
             in_specs=[piece] * reps + [mine] * 3,
             out_specs=[mine] * 3,
         ),
@@ -1148,26 +1280,10 @@
     return list(lax.optimization_barrier((*values, *earlier))[: len(values)])
 
 
-def unpack(values):
-    seqs, rows, _ = values.shape
-    parts = values.reshape(seqs, rows // (2 * NSTATE), 2 * NSTATE, LANES)
-    return parts.transpose(0, 2, 1, 3).reshape(seqs, 2 * NSTATE, -1)
-
-
-def pack(values):
-    seqs, count, length = values.shape
-    return values.reshape(seqs, count, length // LANES, LANES).transpose(0, 2, 1, 3).reshape(seqs, -1, LANES)
-
-
-def to_chunks(values):
-    seqs, count, length = values.shape
-    return values.reshape(seqs, count, length // CHUNK, CHUNK).transpose(2, 1, 0, 3)
-
-
-def from_sums(values):
-    groups, length, _ = values.shape
-    parts = values.reshape(groups, length, 2 * NSTATE, SUBS).transpose(0, 3, 2, 1)
-    return parts.reshape(groups * SUBS, 2 * NSTATE, length)
+def to_columns(values, width):
+    *lead, rows, columns = values.shape
+    blocks = values.reshape(*lead, rows, columns // width, width)
+    return jnp.swapaxes(blocks, -3, -2).reshape(*lead, rows * columns // width, width)
 
 
 def order(values, index):
@@ -1203,6 +1319,17 @@
     def sub_rows(value):
         return lax.dynamic_slice_in_dim(value, r * sub, sub, 0)
 
+    def own_rows(rows):
+        rows = rows.reshape(2, in_rows, width)
+        own = lax.dynamic_index_in_dim(rows, c, 0, keepdims=False)
+        return own, net.core(lax.dynamic_index_in_dim(rows, 1 - c, 0, keepdims=False))
+
+    def full_in(pieces):
+        own = net.order_reps(pieces[:reps])
+        other = net.order_reps(pieces[reps:])
+        every = net.pair_rows(own, other).reshape(2, reps, in_rows, planes, sub)
+        return every.transpose(2, 3, 0, 1, 4).reshape(in_rows, width * seqs).astype(f32)
+
     place = jnp.stack([r, c, net.plane]).astype(jnp.int32)
     own_hidden = hidden[0]
     tiled = sub % LANES == 0
@@ -1214,111 +1341,73 @@
         in_mine = lax.dynamic_index_in_dim(in_view, r, 4, keepdims=False).astype(bf16)
         in_own = lax.dynamic_index_in_dim(in_mine, c, 3, keepdims=False).reshape(in_rows, 2 * width)
         in_other = lax.dynamic_index_in_dim(in_mine, 1 - c, 3, keepdims=False).reshape(in_rows, 2 * width)
-    small = jnp.concatenate(
-        [sub_rows(x_master).astype(bf16), sub_rows(dt_master).astype(bf16), sub_rows(chan_master).astype(bf16)], axis=1
-    )
+    x_mine = sub_rows(x_master)
+    small = jnp.concatenate([x_mine[:, :RANK], sub_rows(dt_master), x_mine[:, RANK:], sub_rows(chan_master)], axis=1)
+    small = jnp.pad(small.astype(bf16), ((0, 0), (0, -small.shape[1] % LANES)))
+    out_mine = sub_rows(out_master).astype(bf16)
     own_gain = lax.reduce_precision(gain_master, 8, 7)[None]
     own_ids = segments.astype(f32)
     if fast:
-        small = jnp.pad(small, ((0, 0), (0, -small.shape[1] % LANES)))
-        hidden_all, inner_blocks, small_parts, gain_parts, ids = gather_first(
-            own_hidden, in_own[:, :width], in_other[:, :width], small, own_gain, own_ids
+        hidden_all, upstream, inner_blocks, gate_pair, small_parts, gains, ids = gather_first(
+            own_hidden, cotangent[0], in_own, in_other, small, own_gain, own_ids
         )
         inner_blocks = [inner_blocks[k] for k in range(planes)]
-        small_all = order(list(small_parts), net.plane).reshape(width, -1)
-        two = [order([gain_parts[e * planes + k] for k in range(planes)], net.plane) for e in range(2)]
-        gain = jnp.stack(order(two, c), axis=1).reshape(model)
-        ids = ids.reshape(seqs, length)
-        own_up = after(cotangent[0], hidden_all)
-        gate_pair = net.pair_rows(in_own[:, width:], net.core(in_other[:, width:])).reshape(2 * in_rows, width)
-        gate_blocks = net.gather_z_list(after(gate_pair, hidden_all))
-        out_blocks = net.gather_z_list(after(sub_rows(out_master).astype(bf16), hidden_all))
+        small_blocks = [small_parts[k] for k in range(planes)]
     else:
-        ids = net.gather_plane(own_ids).reshape(seqs, length)
+        ids = net.gather_plane(own_ids).reshape(seqs, 1, length)
         gain_pair = net.pair_rows(own_gain[0], net.core(own_gain[0])).reshape(2 * in_rows)
-        gain = net.gather_z(gain_pair)
-        small_all = net.gather_z(small)
+        gains = net.gather_z(gain_pair).reshape(1, 1, model)
+        small_blocks = net.gather_z_list(small)
         in_pair = net.pair_rows(in_own, net.core(in_other)).reshape(2 * in_rows, 2 * width)
         inner_blocks = net.gather_z_list(in_pair[:, :width])
         hidden_all = net.gather_plane(own_hidden)
-        own_up = after(cotangent[0], hidden_all)
-        gate_blocks = net.gather_z_list(in_pair[:, width:])
-        out_blocks = net.gather_z_list(sub_rows(out_master).astype(bf16))
-    up_near = net.gather_near(own_up)
-    w_xdt = small_all[:, :RANK]
-    w_xdt_t = w_xdt.T
-    w_xbc = small_all[:, RANK:xcols].T
-    w_dt = small_all[:, xcols : xcols + RANK]
-    channel = small_all[:, xcols + RANK : xcols + RANK + chan_cols].astype(f32)
-    a_log = channel[:, KCONV : KCONV + NSTATE]
-    rates = -jnp.exp(a_log)
-    rate_tiles = jnp.broadcast_to(rates.T[:, None, :], (NSTATE, SUBS, width))
-    chan = channel.T
-    same = [
-        (jnp.pad(ids, ((0, 0), (KCONV - 1 - k, 0)), constant_values=-1)[:, :length] == ids).astype(f32)
-        for k in range(KCONV - 1)
-    ]
-    cut = jnp.where(same[-1] > 0, 0.0, CUT)
-    masks = jnp.stack(same + [cut] + [jnp.zeros_like(cut)] * (MASKS - KCONV), axis=2)
-
-    normed, inner, conv_out, proj_part = front(
-        place, hidden_all, gain[None], masks, chan, w_xdt_t, w_xbc, inner_blocks
+        upstream = net.gather_plane(cotangent[0])
+        gate_pair = in_pair[:, width:]
+    blocks = net.gather_z_list(jnp.concatenate([gate_pair, to_columns(out_mine, width)]))
+    normed, inner, conv_out, proj_part, masks, small_all, rest, gain = front(
+        place, hidden_all, ids, gains, small_blocks, inner_blocks
     )
     dt_in, bc = net.sum_plane(proj_part, length, 2)
-    up_all = jnp.stack(up_near + net.gather_far(after_all(up_near, dt_in)))
-    upstream = jnp.concatenate([up_all, net.core(up_all)])
-    bc = to_chunks(unpack(bc))
-    scanned, starts = scan_forward(dt_in, masks, conv_out, bc, rate_tiles, w_dt, chan)
-    out_part, mixed, grad_y, grad_gate, grad_skip = middle(
-        place, normed, upstream, scanned, conv_out, chan, gate_blocks, out_blocks
+    bc = bc.reshape(-1, LANES)
+    scanned, starts = scan_forward(dt_in, masks, conv_out, bc, small_all, rest)
+    out_own, out_other, mixed, grad_y, grad_gate, grad_skip = middle(
+        place, normed, upstream, scanned, conv_out, rest, blocks
     )
-    out_far = net.core(out_part[reps:])
+    out_far = net.core(out_other)
     grad_out = dot(mixed.reshape(-1, width), upstream.reshape(-1, model), ((0,), (0,))).astype(bf16)
     flat_normed = normed.reshape(-1, model)
     gin_gate = dot(flat_normed, grad_gate.reshape(-1, width), ((0,), (0,))).astype(bf16)
-    pair, grad_y = lax.optimization_barrier((net.add_pair(out_part, out_far), grad_y))
-    out_moved = [net.rep(pair[k], k) for k in range(1, reps)]
-    grad_out_moved = net.send_z(grad_out)
-    gin_gate_moved = net.send_z(gin_gate)
-    grad_y = after(grad_y, grad_out, gin_gate)
-
-    grad_conv, grad_dtlow, grad_dtin, grad_bc, grad_rates, grad_dtbias = scan_backward(
-        dt_in, masks, conv_out, bc, rate_tiles, w_dt, chan, starts, grad_y
+    grad_rows = jnp.concatenate(
+        [gin_gate.reshape(planes, -1, width), to_columns(grad_out.reshape(planes, sub, model), width)], axis=1
+    ).reshape(-1, width)
+    grad_rows_moved = net.send_z(grad_rows)
+    pair = net.add_pair(out_own, out_far)
+    out_first_half = net.send_half(pair, reps // 2)
+    grad_y = after(grad_y, grad_rows, pair)
+
+    grad_conv, grad_dtlow, proj_back, grad_rates, grad_dtbias = scan_backward(
+        dt_in, masks, conv_out, bc, small_all, rest, starts, grad_y
     )
     grad_rates = jnp.sum(grad_rates, axis=1).T
+    rates = -jnp.exp(rest[CH + KCONV : CH + KCONV + NSTATE].T)
     grad_dt = dot(grad_dtlow.reshape(-1, width), dt_in.reshape(-1, RANK), ((0,), (0,)))
-    out_sum = pair[0].astype(f32)
-    for moved in after_all(out_moved, grad_dtin):
-        out_sum = out_sum + moved.astype(f32)
+    out_sum = net.sum_halves(pair, after(out_first_half, proj_back))
     layer_output = (hidden[0].astype(f32) + out_sum).astype(bf16)
-    grad_out_own = net.sum_z(grad_out, after_all(grad_out_moved, grad_dtin))
-    gin_gate_rows = net.sum_z(gin_gate, after_all(gin_gate_moved, grad_dtin))
-    proj_back = jnp.concatenate([grad_dtin, pack(from_sums(grad_bc))], axis=1)
-    gp_dt, gp_bc = net.sum_plane(proj_back, length, 3)
-    gp_bc = unpack(gp_bc).astype(bf16)
-    flat_conv = conv_out.reshape(-1, width)
-    grad_xdt = dot(flat_conv, gp_dt.reshape(-1, RANK), ((0,), (0,)))
-    grad_xbc = lax.dot_general(
-        conv_out, gp_bc, (((1,), (2,)), ((0,), (0,))), preferred_element_type=f32
-    ).sum(axis=0)
-    grad_x = jnp.concatenate([grad_xdt, grad_xbc], axis=1)
-    grad_inner, conv_sums = back_conv(place, grad_conv, gp_dt, gp_bc, inner, masks, chan, w_xdt_t, w_xbc)
+    grad_rows = net.sum_z(grad_rows, after_all(grad_rows_moved, proj_back))
+    gate_rows = own_rows(grad_rows[: 2 * in_rows])
+    pieces = jnp.concatenate([*gate_rows, grad_rows[2 * in_rows :]])
+    proj_back = after(proj_back, pieces)
+    gp_dt, gp_bc = net.sum_plane(proj_back.reshape(seqs, TOKENS + BC_ROWS, LANES), length, 3)
+    pieces = net.gather_rep_list(after(pieces, gp_dt))
+    grad_xdt = dot(conv_out.reshape(-1, width), gp_dt.reshape(-1, RANK), ((0,), (0,)))
+    grad_inner, conv_sums, grad_xbc = back_conv(
+        place, grad_conv, gp_dt, gp_bc, inner, conv_out, masks, small_all, rest
+    )
+    grad_x = jnp.concatenate([grad_xdt, grad_xbc.T], axis=1)
     gin_inner = dot(flat_normed, grad_inner.reshape(-1, width), ((0,), (0,))).astype(bf16)
-    normed_part, grad_gain = back_normed(place, grad_inner, grad_gate, hidden_all, inner_blocks, gate_blocks)
-    def pieces_in(rows):
-        rows = rows.reshape(2, in_rows, width)
-        own = lax.dynamic_index_in_dim(rows, c, 0, keepdims=False)
-        other = net.core(lax.dynamic_index_in_dim(rows, 1 - c, 0, keepdims=False))
-        return net.gather_rep(own) + net.gather_rep(other)
-
-    def full_in(pieces):
-        own = net.order_reps(pieces[:reps])
-        other = net.order_reps(pieces[reps:])
-        every = net.pair_rows(own, other).reshape(2, reps, in_rows, planes, sub)
-        return every.transpose(2, 3, 0, 1, 4).reshape(in_rows, width * seqs).astype(f32)
-
+    back_own, back_other, grad_gain = back_normed(place, grad_inner, grad_gate, hidden_all, inner_blocks, blocks)
     out_new = adam_out(
-        place, net.gather_rep(grad_out_own), out_master, out_first, out_second
+        place, pieces, out_master, out_first, out_second
     )
     grad_small = jnp.concatenate(
         [
@@ -1335,12 +1424,14 @@
     )
     if fast:
         grad_small = jnp.pad(grad_small, ((0, 0), (0, -grad_small.shape[1] % LANES)))
-        grad_normed, inner_pieces, small_sum = finish(normed_part, gin_inner, grad_small)
-        inner_pieces = [inner_pieces[e, k] for e in range(2) for k in range(reps)]
+        grad_small = after(grad_small, *pieces)
+        grad_normed, inner_pieces, small_sum = finish(back_own, back_other, gin_inner, grad_small)
+        inner_pieces = [(inner_pieces.reshape(-1, width), e * reps + k) for e in range(2) for k in range(reps)]
         small_sum = net.order_reps(list(small_sum))
     else:
-        grad_normed = net.scatter_plane(normed_part, bf16)
-        inner_pieces = pieces_in(net.sum_z(gin_inner, net.send_z(gin_inner)))
+        grad_normed = net.scatter_plane(jnp.concatenate([back_own, back_other]), bf16)
+        inner_own_rows, inner_other_rows = own_rows(net.sum_z(gin_inner, net.send_z(gin_inner)))
+        inner_pieces = net.gather_rep(inner_own_rows) + net.gather_rep(inner_other_rows)
         small_sum = net.order_reps(net.gather_rep(net.sum_z(grad_small, net.send_z(grad_small))))
     own_res = hidden[0].astype(f32)
     own_inv = lax.rsqrt(jnp.mean(own_res * own_res, axis=1, keepdims=True) + norm_eps)
@@ -1352,10 +1443,12 @@
     ).astype(bf16)
 
     if tiled:
-        in_new = adam_in(place, 1, pieces_in(gin_gate_rows), in_master, in_first, in_second, None)
+        gate_pieces = [(pieces[k], e) for e in range(2) for k in range(reps)]
+        in_new = adam_in(place, 1, gate_pieces, in_master, in_first, in_second, None)
         in_new = adam_in(place, 0, inner_pieces, in_master, in_first, in_second, in_new)
     else:
-        in_sum = jnp.concatenate([full_in(inner_pieces), full_in(pieces_in(gin_gate_rows))], axis=1)
+        gate_pieces = [pieces[k][e * in_rows : (e + 1) * in_rows] for e in range(2) for k in range(reps)]
+        in_sum = jnp.concatenate([full_in(inner_pieces), full_in(gate_pieces)], axis=1)
         in_new = adam_step(in_master, in_first, in_second, in_sum, learn_rates[0], with_decay[0])
     gain_cols = slice(xcols + RANK + chan_cols, xcols + RANK + chan_cols + reps)
     gain_two = jnp.sum(small_sum[:, :, gain_cols], axis=0).reshape(2, in_rows)

time: 754 us -> 617 us (0.82)
  waiting for transfers between devices: 98.3 us -> 0.04 us
  starting transfers between devices: 49.1 us -> 24.7 us
  local copies, waits for them, and re-layouts: 83.9 us -> 67.2 us
  Pallas kernels: 439 us -> 451 us
  other arithmetic: 40.1 us -> 29.1 us
    ppermute x19 -> x5, waiting for transfers between devices: 67.1 us -> 0.01 us  [rep(): return lax.ppermute(value, 'rep', [(i, i ^ k) for i in range(self.reps)])]
    ppermute x12 -> x6, waiting for transfers between devices: 31.2 us -> 0.02 us  [z(): return lax.ppermute(value, 'shard', self.planes_pairs(pairs))]
    ppermute x19 -> x5, starting transfers between devices: 21.2 us -> 5.61 us  [rep(): return lax.ppermute(value, 'rep', [(i, i ^ k) for i in range(self.reps)])]
    unnamed x147 -> x127, local copies, waits for them, and re-layouts: 25.1 us -> 38 us
    slice x11 -> x5, local copies, waits for them, and re-layouts: 13.6 us -> 2.7 us  [the longest x2 2.62 us: send_half(): return self.rep(part[k:2 * k], k)]
    pallas_call x4, Pallas kernels: 67 us -> 77.4 us  [per_sequence(): pl.pallas_call(kernel, grid_spec=pltpu.PrefetchScalarGridSpec(num_scalar_...]
    another operation x10 -> x2, local copies, waits for them, and re-layouts: 14 us -> 4.32 us  [the longest x1 3.46 us: to_columns(): blocks = values.reshape(*lead, rows, columns // width, width)]
    pallas_call x1, Pallas kernels: 120 us -> 110 us  [scan_backward(): pl.pallas_call(scan_bwd_kernel, grid=(chunks,), in_specs=ins + [start_spe...]
  transfers between devices with their start and end apart: 36 -> 14, of which waited for: 6 -> 0; matrix products, arithmetic and copies ran while one was open for 15% -> 14% of each run, Pallas kernels for 47% -> 56%
where the time goes in v3:
time: 617 us; the launch traced here: 606 us
  Pallas kernels  451 us (73%)
  local copies, waits for them, and re-layouts  67.2 us (11%)
  matrix products  32.8 us (5%)
  other arithmetic  29.1 us (5%)
  starting transfers between devices  24.7 us (4%)
    pallas_call x1, Pallas kernels, scan_backward(): pl.pallas_call(scan_bwd_kernel, grid=(chunks,), in_specs=ins + [start_spe...  110 us
    pallas_call x1, Pallas kernels, gather_first(): pl.pallas_call(gather_first_kernel, in_specs=[vmem] * 7, out_specs=[anywh...  77.7 us
    pallas_call x4, Pallas kernels, per_sequence(): pl.pallas_call(kernel, grid_spec=pltpu.PrefetchScalarGridSpec(num_scalar_...  77.4 us
    pallas_call x1, Pallas kernels, finish(): pl.pallas_call(finish_kernel, in_specs=[anywhere] * 4, out_specs=[pl.Bloc...  72.5 us
    pallas_call x2, Pallas kernels, reduce_plane(): pl.pallas_call(reduce_plane_kernel, in_specs=[vmem], out_specs=[vmem, vme...  39.9 us
    unnamed x127, local copies, waits for them, and re-layouts  38 us
    pallas_call x1, Pallas kernels, scan_forward(): pl.pallas_call(scan_fwd_kernel, grid=(chunks,), in_specs=ins, out_specs=[...  33.7 us
    dot_general x5, matrix products, dot(): return lax.dot_general(a, b, (dims, ((), ())), preferred_element_type=f32)  32.8 us
  transfers between devices with their start and end apart: 14, of which 0 were waited for; matrix products, arithmetic and copies ran while one was open for 14% of the time, Pallas kernels for 56%

profile of v3, /device:TPU:0, one launch (start us, length us, event | category | flops | bytes accessed | tf_op | source)
XLA Modules:
  0.0 606.1 jit_solution(7755960679251073888)
XLA Ops:
  2.2 6.2 %slice_in.1 = bf16[2,256,1024]{2,1,0:T(8,128)(2,1)} custom-call(s32[3]{0:T(128)} %pad_add_fusion.place_ref.refs_0_, f32[256,8192]{1,0:T(8,128)} %refs_8_.3, f32[256,8192]{1,0:T(8,128)} %refs_8_.3), custom_call_target="tpu_custom_call" | custom-call | tf_op jit(solution)/shard_map/slice_in/pallas_call | solution.py:1262
  13.3 77.7 %gather_first.1 = (bf16[8,256,2048]{2,1,0:T(8,128)(2,1)S(1)}, bf16[8,256,2048]{2,1,0:T(8,128)(2,1)S(1)}, bf16[4,512,512]{2,1,0:T(8,128)(2,1)S(1)}, bf16[512,512]...) custom-call(bf16[256,2048]{1,0:T(8,128)(2,1)S(1)} %bitcast.90, ...), custom_call_target="tpu_custom_call" | custom-call | bytes 100000000 | tf_op jit(solution)/shard_map/gather_first/pallas_call | solution.py:798
  91.0 3.4 copy-done.27
  94.3 3.4 copy-done.28
  99.9 2.4 collective-permute-start.2
  104.4 17.1 %front.1 = (bf16[8,256,2048]{2,1,0:T(8,128)(2,1)}, f32[8,256,512]{2,1,0:T(8,128)}, bf16[8,256,512]{2,1,0:T(8,128)(2,1)}, f32[8,320,128]{2,1,0:T(8,128)}, f32[8,2...) custom-call(s32[3]{0:T(128)} %pad_add_fusion.place_ref.refs_0_, ...), custom_call_target="tpu_custom_call" | custom-call | flops 4294967296 | bytes 40000000 | tf_op jit(solution)/shard_map/front/pallas_call | solution.py:450
  122.8 19.9 %reduce_plane.2 = (bf16[8,256,128]{2,1,0:T(8,128)(2,1)S(1)}, f32[8,64,128]{2,1,0:T(8,128)S(1)}) custom-call(f32[8,320,128]{2,1,0:T(8,128)S(1)} %copy-done.19), custom_call_target="tpu_custom_call" | custom-call | bytes 50000000 | tf_op jit(solution)/shard_map/reduce_plane/pallas_call | solution.py:859
  146.2 33.7 %scan_forward.1 = (f32[8,256,512]{2,1,0:T(8,128)}, f32[8,16,8,512]{3,2,1,0:T(8,128)}) custom-call(bf16[8,256,128]{2,1,0:T(8,128)(2,1)S(1)} %get-tuple-element.86.dt_ref, f32[8,256,8]{2,1,0:T(8,128)S(1)} %copy-done.20, bf16[8,256,512]{2,1,0:T(8,128)(2,1)} %get-tuple-element.88.conv_ref, f32[512,128]{1,0:T(8,128)S(1)} %bitcast.94, ...), custom_call_target="tpu_custom_call" | custom-call | flops 134217728 | bytes 100000000 | tf_op jit(solution)/shard_map/scan_forward/pallas_call | solution.py:280
  181.6 25.0 %middle.1 = (bf16[4,256,2048]{2,1,0:T(8,128)(2,1)}, bf16[4,256,2048]{2,1,0:T(8,128)(2,1)}, bf16[8,256,512]{2,1,0:T(8,128)(2,1)}, f32[8,256,512]{2,1,0:T(8,128)},...) custom-call(s32[3]{0:T(128)} %pad_add_fusion.place_ref.refs_0_, bf16[8,256,2048]{2,1,0:T(8,128)(2,1)} %get-tuple-element.83.normed_ref, ...), custom_call_target="tpu_custom_call" | custom-call | flops 12884901888 | bytes 40000000 | tf_op jit(solution)/shard_map/middle/pallas_call | solution.py:450
  207.1 9.9 %bitcast_convert_fusion.1 = bf16[512,2048]{1,0:T(8,128)(2,1)} fusion(bf16[8,256,512]{2,1,0:T(8,128)(2,1)} %get-tuple-element.99, bf16[8,256,2048]{2,1,0:T(8,128)(2,1)} %copy-done.28), kind=kOutput, calls=%fused_computation.3 | convolution fusion | flops 4296015872 | bytes 12582912 | tf_op jit(solution)/shard_map/dot_general | solution.py:44
  217.0 3.5 reshape_reshape.3
  222.1 8.4 %bitcast_convert_fusion.2 = bf16[2048,512]{1,0:T(8,128)(2,1)S(1)} fusion(bf16[8,256,2048]{2,1,0:T(8,128)(2,1)} %get-tuple-element.83.normed_ref, bf16[8,256,512]{2,1,0:T(8,128)(2,1)S(1)} %copy-done.60), kind=kOutput, calls=%fused_computation.4 | convolution fusion | flops 4296015872 | bytes 12582912 | tf_op jit(solution)/shard_map/dot_general | solution.py:44
  233.1 11.6 %collective-permute-start.6 = (bf16[1024,512]{1,0:T(8,128)(2,1)}, bf16[1024,512]{1,0:T(8,128)(2,1)S(1)}, u32[]{:S(2)}, u32[]{:S(2)}) collective-permute-start(bf16[1024,512]{1,0:T(8,128)(2,1)} %get-tuple-element.212), channel_id=1, source_target_pairs={{0,2},{1,3},{2,0},{3,1},{4,6},{5,7},{6,4},{7,5},{8,10},{9,11},{10,... | collective-permute-start | bytes 3145736 | tf_op jit(solution)/shard_map/ppermute | solution.py:1067
  244.8 2.4 collective-permute-start.8
  249.7 5.4 add_convert_fusion
  259.2 109.9 %scan_backward.1 = (f32[8,256,512]{2,1,0:T(8,128)}, bf16[8,256,512]{2,1,0:T(8,128)(2,1)}, f32[2560,128]{1,0:T(8,128)}, f32[16,8,512]{2,1,0:T(8,128)}, f32[8,512]{1,0:T(8,128)}) custom-call(bf16[8,256,128]{2,1,0:T(8,128)(2,1)} %copy-done.21, f32[8,256,8]{2,1,0:T(8,128)} %get-tuple-element.87.mask_ref, bf16[8,256,512]{2,1,0:T(8,128)(2,1)} %get-tuple-element.88.conv_ref, ...), custom_call_target="tpu_custom_call" | custom-call | flops 402653184 | bytes 300000000 | tf_op jit(solution)/shard_map/scan_backward/pallas_call | solution.py:309
  369.2 2.4 add_convert_fusion.2
  377.9 19.9 %reduce_plane.3 = (bf16[8,256,128]{2,1,0:T(8,128)(2,1)S(1)}, f32[8,64,128]{2,1,0:T(8,128)S(1)}) custom-call(f32[8,320,128]{2,1,0:T(8,128)S(1)} %bitcast.92), custom_call_target="tpu_custom_call" | custom-call | bytes 50000000 | tf_op jit(solution)/shard_map/reduce_plane/pallas_call | solution.py:859
  402.9 13.6 %back_conv.1 = (bf16[8,256,512]{2,1,0:T(8,128)(2,1)}, f32[5,8,512]{2,1,0:T(8,128)}, f32[32,512]{1,0:T(8,128)}) custom-call(s32[3]{0:T(128)} %pad_add_fusion.place_ref.refs_0_, f32[8,256,512]{2,1,0:T(8,128)} %get-tuple-element.103.gconv_ref, bf16[8,256,128]{2,1,0:T(8,128)(2,1)} %copy-done.16, f32[8,64,128]{2,1,0:T(8,128)} %copy-done.25, ...), custom_call_target="tpu_custom_call" | custom-call | flops 268435456 | bytes 40000000 | tf_op jit(solution)/shard_map/back_conv/pallas_call | solution.py:450
  416.5 9.9 %bitcast_convert_fusion.gin = bf16[2048,512]{1,0:T(8,128)(2,1)} fusion(bf16[8,256,2048]{2,1,0:T(8,128)(2,1)} %get-tuple-element.83.normed_ref, bf16[8,256,512]{2,1,0:T(8,128)(2,1)} %get-tuple-element.111.ginner_ref), kind=kOutput, calls=%fused_computation.2 | convolution fusion | flops 4296015872 | bytes 12582912 | tf_op jit(solution)/shard_map/dot_general | solution.py:44
  427.2 21.7 %back_normed.1 = (bf16[4,256,2048]{2,1,0:T(8,128)(2,1)}, bf16[4,256,2048]{2,1,0:T(8,128)(2,1)}, f32[8,2048]{1,0:T(8,128)}) custom-call(s32[3]{0:T(128)} %pad_add_fusion.place_ref.refs_0_, bf16[8,256,512]{2,1,0:T(8,128)(2,1)} %get-tuple-element.111.ginner_ref, bf16[8,256,512]{2,1,0:T(8,128)(2,1)} %get-tuple-element.98.ggate_ref, ...), custom_call_target="tpu_custom_call" | custom-call | flops 8589934592 | bytes 40000000 | tf_op jit(solution)/shard_map/back_normed/pallas_call | solution.py:450
  452.5 3.1 convolution_bitcast_fusion.1
  455.6 2.7 concatenate.20
  465.2 72.5 %finish.1 = (f32[256,2048]{1,0:T(8,128)S(1)}, bf16[8,256,512]{2,1,0:T(8,128)(2,1)S(1)}, f32[4,128,384]{2,1,0:T(8,128)S(1)}) custom-call(bf16[4,256,2048]{2,1,0:T(8,128)(2,1)S(1)} %copy-done.13, bf16[4,256,2048]{2,1,0:T(8,128)(2,1)} %get-tuple-element.113.other_part, bf16[2048,512]{1,0:T(8,128)(2,1)S(1)} %copy-done.17, f32[512,384]{1,0:T(8,128)S(1)} %pad.9.small), custom_call_target="tpu_custom_call" | custom-call | bytes 150000000 | tf_op jit(solution)/shard_map/finish/pallas_call | solution.py:1010
  544.6 2.6 fusion
  551.7 2.4 add_convert_fusion.1
  556.7 3.4 copy-done
  560.1 3.4 copy-done.1
  563.5 9.6 %adam_in.2 = (f32[256,8192]{1,0:T(8,128)}, f32[256,8192]{1,0:T(8,128)}, f32[256,8192]{1,0:T(8,128)}) custom-call(s32[3]{0:T(128)S(1)} %copy-done.26, bf16[1024,512]{1,0:T(8,128)(2,1)S(1)} %pad_maximum_fusion.2.refs_0_.refs_4_, bf16[1024,512]{1,0:T(8,128)(2,1)S(1)} %copy-done.5, bf16[1024,512]{1,0:T(8,128)(2,1)S(1)} %copy-done.7, ...), custom_call_target="tpu_custom_call" | custom-call | flops 20971520 | bytes 27262976 | tf_op jit(solution)/shard_map/adam_in/pallas_call | solution.py:1198
  573.2 10.0 %adam_in.3 = (f32[256,8192]{1,0:T(8,128)}, f32[256,8192]{1,0:T(8,128)}, f32[256,8192]{1,0:T(8,128)}) custom-call(s32[3]{0:T(128)S(1)} %copy-done.26, bf16[2048,512]{1,0:T(8,128)(2,1)S(1)} %bitcast.82, bf16[2048,512]{1,0:T(8,128)(2,1)S(1)} %bitcast.83, bf16[2048,512]{1,0:T(8,128)(2,1)S(1)} %bitcast.84, ...), custom_call_target="tpu_custom_call", output_to_operand_aliasing={{0}: (12, {}), {1}: (13, {}), {2}: (14, {})} | custom-call | flops 20971520 | bytes 27262976 | tf_op jit(solution)/shard_map/adam_in/pallas_call | solution.py:1198
  588.7 13.6 %adam_out.1 = (f32[512,2048]{1,0:T(8,128)}, f32[512,2048]{1,0:T(8,128)}, f32[512,2048]{1,0:T(8,128)}) custom-call(s32[3]{0:T(128)S(1)} %copy-done.26, bf16[1024,512]{1,0:T(8,128)(2,1)S(1)} %pad_maximum_fusion.2.refs_0_.refs_4_, bf16[1024,512]{1,0:T(8,128)(2,1)S(1)} %copy-done.5, bf16[1024,512]{1,0:T(8,128)(2,1)S(1)} %copy-done.7, ...), custom_call_target="tpu_custom_call" | custom-call | flops 10485760 | bytes 27262976 | tf_op jit(solution)/shard_map/adam_out/pallas_call | solution.py:1235
  602.9 2.8 add_convert_fusion.3
  (203 shorter events, 70.9 us)
Async XLA Ops:
  97.8 82.1 %collective-permute-start = (bf16[1024,512]{1,0:T(8,128)(2,1)S(1)}, bf16[1024,512]{1,0:T(8,128)(2,1)S(1)}, u32[]{:S(2)}, u32[]{:S(2)}) collective-permute-start(bf16[1024,512]{1,0:T(8,128)(2,1)S(1)} %pad_maximum_fusion.1.refs_0_.refs_4_), channel_id=1, source_target_pairs={{0,2},{1,3},{2,0},{3,1},{4,6},{5,7},{6,4},{7,5},{8,10},{9,11},{10,... | collective-permute-start | bytes 3145736 | tf_op jit(solution)/shard_map/ppermute | solution.py:1067
  98.4 81.5 %collective-permute-start.1 = (bf16[1024,512]{1,0:T(8,128)(2,1)S(1)}, bf16[1024,512]{1,0:T(8,128)(2,1)S(1)}, u32[]{:S(2)}, u32[]{:S(2)}) collective-permute-start(bf16[1024,512]{1,0:T(8,128)(2,1)S(1)} %pad_maximum_fusion.1.refs_0_.refs_4_), channel_id=1, source_target_pairs={{0,4},{1,5},{2,6},{3,7},{4,0},{5,1},{6,2},{7,3},{8,12},{9,13},{10,... | collective-permute-start | bytes 3145736 | tf_op jit(solution)/shard_map/ppermute | solution.py:1067
  99.9 80.0 %collective-permute-start.2 = (bf16[1024,512]{1,0:T(8,128)(2,1)S(1)}, bf16[1024,512]{1,0:T(8,128)(2,1)S(1)}, u32[]{:S(2)}, u32[]{:S(2)}) collective-permute-start(bf16[1024,512]{1,0:T(8,128)(2,1)S(1)} %pad_maximum_fusion.1.refs_0_.refs_4_), channel_id=1, source_target_pairs={{0,6},{1,7},{2,4},{3,5},{4,2},{5,3},{6,0},{7,1},{8,14},{9,15},{10,... | collective-permute-start | bytes 3145736 | tf_op jit(solution)/shard_map/ppermute | solution.py:1067
  142.7 37.2 %copy-start.21 = (bf16[8,256,128]{2,1,0:T(8,128)(2,1)}, bf16[8,256,128]{2,1,0:T(8,128)(2,1)S(1)}, u32[]{:S(2)}) copy-start(bf16[8,256,128]{2,1,0:T(8,128)(2,1)S(1)} %get-tuple-element.86.dt_ref) | copy-start | bytes 1572868
  142.7 37.2 %copy-start.29 = (f32[8,64,128]{2,1,0:T(8,128)}, f32[8,64,128]{2,1,0:T(8,128)S(1)}, u32[]{:S(2)}) copy-start(f32[8,64,128]{2,1,0:T(8,128)S(1)} %get-tuple-element.89) | copy-start | bytes 786436
  206.6 43.1 %collective-permute-start.3 = (bf16[4,256,2048]{2,1,0:T(8,128)(2,1)}, bf16[4,256,2048]{2,1,0:T(8,128)(2,1)}, u32[]{:S(2)}, u32[]{:S(2)}) collective-permute-start(bf16[4,256,2048]{2,1,0:T(8,128)(2,1)} %get-tuple-element.95), channel_id=1, source_target_pairs={{0,1},{1,0},{2,3},{3,2},{4,5},{5,4},{6,7},{7,6},{8,9},{9,8},{10,11... | collective-permute-start | bytes 12582920 | tf_op jit(solution)/shard_map/ppermute | solution.py:1061
  230.8 18.0 %copy-start.51 = (f32[8,512]{1,0:T(8,128)S(1)}, f32[8,512]{1,0:T(8,128)}, u32[]{:S(2)}) copy-start(f32[8,512]{1,0:T(8,128)} %get-tuple-element.119) | copy-start | bytes 49156
  233.1 136.0 %collective-permute-start.6 = (bf16[1024,512]{1,0:T(8,128)(2,1)}, bf16[1024,512]{1,0:T(8,128)(2,1)S(1)}, u32[]{:S(2)}, u32[]{:S(2)}) collective-permute-start(bf16[1024,512]{1,0:T(8,128)(2,1)} %get-tuple-element.212), channel_id=1, source_target_pairs={{0,2},{1,3},{2,0},{3,1},{4,6},{5,7},{6,4},{7,5},{8,10},{9,11},{10,... | collective-permute-start | bytes 3145736 | tf_op jit(solution)/shard_map/ppermute | solution.py:1067
  244.8 124.4 %collective-permute-start.7 = (bf16[1024,512]{1,0:T(8,128)(2,1)S(1)}, bf16[1024,512]{1,0:T(8,128)(2,1)}, u32[]{:S(2)}, u32[]{:S(2)}) collective-permute-start(bf16[1024,512]{1,0:T(8,128)(2,1)S(1)} %get-tuple-element.211), channel_id=1, source_target_pairs={{0,4},{1,5},{2,6},{3,7},{4,0},{5,1},{6,2},{7,3},{8,12},{9,13},{10,... | collective-permute-start | bytes 3145736 | tf_op jit(solution)/shard_map/ppermute | solution.py:1067
  244.8 124.4 %collective-permute-start.8 = (bf16[1024,512]{1,0:T(8,128)(2,1)S(1)}, bf16[1024,512]{1,0:T(8,128)(2,1)}, u32[]{:S(2)}, u32[]{:S(2)}) collective-permute-start(bf16[1024,512]{1,0:T(8,128)(2,1)S(1)} %get-tuple-element.210), channel_id=1, source_target_pairs={{0,6},{1,7},{2,4},{3,5},{4,2},{5,3},{6,0},{7,1},{8,14},{9,15},{10,... | collective-permute-start | bytes 3145736 | tf_op jit(solution)/shard_map/ppermute | solution.py:1067
  257.7 293.9 %collective-permute-start.4 = (bf16[2,256,2048]{2,1,0:T(8,128)(2,1)}, bf16[2,256,2048]{2,1,0:T(8,128)(2,1)}, u32[]{:S(2)}, u32[]{:S(2)}) collective-permute-start(bf16[2,256,2048]{2,1,0:T(8,128)(2,1)} %slice.97), channel_id=1, source_target_pairs={{0,16},{8,24},{16,0},{24,8},{1,17},{9,25},{17,1},{25,9},{2,18},{10... | collective-permute-start | bytes 6291464 | tf_op jit(solution)/shard_map/ppermute | solution.py:1058
  372.6 4.3 collective-permute-start.9
  399.4 60.1 %collective-permute-start.10 = (bf16[1024,512]{1,0:T(8,128)(2,1)S(1)}, bf16[1024,512]{1,0:T(8,128)(2,1)S(1)}, u32[]{:S(2)}, u32[]{:S(2)}) collective-permute-start(bf16[1024,512]{1,0:T(8,128)(2,1)S(1)} %pad_maximum_fusion.2.refs_0_.refs_4_), channel_id=1, source_target_pairs={{0,8},{8,0},{16,24},{24,16},{1,9},{9,1},{17,25},{25,17},{2,10},{10... | collective-permute-start | bytes 3145736 | tf_op jit(solution)/shard_map/ppermute | solution.py:1058
  400.0 60.5 %collective-permute-start.11 = (bf16[1024,512]{1,0:T(8,128)(2,1)S(1)}, bf16[1024,512]{1,0:T(8,128)(2,1)S(1)}, u32[]{:S(2)}, u32[]{:S(2)}) collective-permute-start(bf16[1024,512]{1,0:T(8,128)(2,1)S(1)} %pad_maximum_fusion.2.refs_0_.refs_4_), channel_id=1, source_target_pairs={{0,16},{8,24},{16,0},{24,8},{1,17},{9,25},{17,1},{25,9},{2,18},{10... | collective-permute-start | bytes 3145736 | tf_op jit(solution)/shard_map/ppermute | solution.py:1058
  401.4 60.0 %collective-permute-start.12 = (bf16[1024,512]{1,0:T(8,128)(2,1)S(1)}, bf16[1024,512]{1,0:T(8,128)(2,1)}, u32[]{:S(2)}, u32[]{:S(2)}) collective-permute-start(bf16[1024,512]{1,0:T(8,128)(2,1)S(1)} %pad_maximum_fusion.2.refs_0_.refs_4_), channel_id=1, source_target_pairs={{0,24},{8,16},{16,8},{24,0},{1,25},{9,17},{17,9},{25,1},{2,26},{10... | collective-permute-start | bytes 3145736 | tf_op jit(solution)/shard_map/ppermute | solution.py:1058
  416.5 9.9 %copy-start.46 = (f32[32,512]{1,0:T(8,128)S(1)}, f32[32,512]{1,0:T(8,128)}, u32[]{:S(2)}) copy-start(f32[32,512]{1,0:T(8,128)} %get-tuple-element.114) | copy-start | bytes 196612
  427.2 21.7 %copy-start.45 = (f32[5,8,512]{2,1,0:T(8,128)S(1)}, f32[5,8,512]{2,1,0:T(8,128)}, u32[]{:S(2)}) copy-start(f32[5,8,512]{2,1,0:T(8,128)} %get-tuple-element.116) | copy-start | bytes 245764
  537.8 6.7 %copy-start.50 = (f32[1,2048]{1,0:T(1,128)S(1)}, f32[1,2048]{1,0:T(1,128)}, u32[]{:S(2)}) copy-start(f32[1,2048]{1,0:T(1,128)} %get-tuple-element.124) | copy-start | bytes 24580
  544.5 57.8 %collective-permute-start.13 = (f32[256]{0:T(256)S(1)}, f32[256]{0:T(256)S(1)}, u32[]{:S(2)}, u32[]{:S(2)}) collective-permute-start(f32[256]{0:T(256)S(1)} %bitcast.115), channel_id=1, source_target_pairs={{0,1},{1,0},{2,3},{3,2},{4,5},{5,4},{6,7},{7,6},{8,9},{9,8},{10,11... | collective-permute-start | bytes 3080 | tf_op jit(solution)/shard_map/ppermute | solution.py:1061
  544.6 7.1 %copy-start.33 = (bf16[4,256,2048]{2,1,0:T(8,128)(2,1)S(1)}, bf16[4,256,2048]{2,1,0:T(8,128)(2,1)}, u32[]{:S(2)}) copy-start(bf16[4,256,2048]{2,1,0:T(8,128)(2,1)} %copy-done.32) | copy-start | bytes 12582916
  555.1 47.8 %collective-permute-start.5 = (bf16[1,256,2048]{2,1,0:T(8,128)(2,1)}, bf16[1,256,2048]{2,1,0:T(8,128)(2,1)}, u32[]{:S(2)}, u32[]{:S(2)}) collective-permute-start(bf16[1,256,2048]{2,1,0:T(8,128)(2,1)} %slice.99), channel_id=1, source_target_pairs={{0,8},{8,0},{16,24},{24,16},{1,9},{9,1},{17,25},{25,17},{2,10},{10... | collective-permute-start | bytes 3145736 | tf_op jit(solution)/shard_map/ppermute | solution.py:1058
  573.2 10.1 %copy-start.44 = (f32[512,23]{0,1:T(8,128)S(1)}, f32[512,23]{0,1:T(8,128)}, u32[]{:S(2)}) copy-start(f32[512,23]{0,1:T(8,128)} %copy.147) | copy-start | bytes 141316
  573.2 10.1 %copy-start.47 = (f32[512,23]{0,1:T(8,128)S(1)}, f32[512,23]{0,1:T(8,128)}, u32[]{:S(2)}) copy-start(f32[512,23]{0,1:T(8,128)} %param.36) | copy-start | bytes 141316
  573.2 10.1 %copy-start.48 = (f32[512,23]{0,1:T(8,128)S(1)}, f32[512,23]{0,1:T(8,128)}, u32[]{:S(2)}) copy-start(f32[512,23]{0,1:T(8,128)} %param.38) | copy-start | bytes 141316
  573.2 10.1 %copy-start.49 = (f32[512,23]{0,1:T(8,128)S(1)}, f32[512,23]{0,1:T(8,128)}, u32[]{:S(2)}) copy-start(f32[512,23]{0,1:T(8,128)} %param.37) | copy-start | bytes 141316
  573.2 10.7 %copy-start.3 = (bf16[1,256,2048]{2,1,0:T(8,128)(2,1)S(1)}, bf16[1,256,2048]{2,1,0:T(8,128)(2,1)}, u32[]{:S(2)}) copy-start(bf16[1,256,2048]{2,1,0:T(8,128)(2,1)} %param.21) | copy-start | bytes 3145732
  573.2 10.7 %copy-start.9 = (f32[256,2048]{1,0:T(8,128)S(1)}, f32[256,2048]{1,0:T(8,128)}, u32[]{:S(2)}) copy-start(f32[256,2048]{1,0:T(8,128)} %copy-done.8) | copy-start | bytes 6291460
  573.2 10.7 %copy-start.15 = (bf16[1,256,2048]{2,1,0:T(8,128)(2,1)S(1)}, bf16[1,256,2048]{2,1,0:T(8,128)(2,1)}, u32[]{:S(2)}) copy-start(bf16[1,256,2048]{2,1,0:T(8,128)(2,1)} %param.23) | copy-start | bytes 3145732
  573.2 12.4 %copy-start.11 = (f32[512,2048]{1,0:T(8,128)S(1)}, f32[512,2048]{1,0:T(8,128)}, u32[]{:S(2)}) copy-start(f32[512,2048]{1,0:T(8,128)} %refs_5_.1) | copy-start | bytes 12582916
  588.7 13.6 %copy-start.55 = (f32[256]{0:T(256)S(1)}, f32[256]{0:T(256)}, u32[]{:S(2)}) copy-start(f32[256]{0:T(256)} %param.41) | copy-start | bytes 3076
  588.7 13.6 %copy-start.56 = (f32[256]{0:T(256)S(1)}, f32[256]{0:T(256)}, u32[]{:S(2)}) copy-start(f32[256]{0:T(256)} %param.40) | copy-start | bytes 3076
  588.7 14.2 %copy-start.36 = (bf16[2,256,2048]{2,1,0:T(8,128)(2,1)S(1)}, bf16[2,256,2048]{2,1,0:T(8,128)(2,1)}, u32[]{:S(2)}) copy-start(bf16[2,256,2048]{2,1,0:T(8,128)(2,1)} %copy-done.35) | copy-start | bytes 6291460
  (43 other events, 112.4 us)

commit v4 on v3

--- a/solution.py
+++ b/solution.py
@@ -16,6 +16,7 @@
 SUBS = 8
 CUT = 1e30
 MASKS = 8
+MOST = 58 * 2**20
 TOKENS = 256
 BC_ROWS = TOKENS * 2 * NSTATE // LANES
 CH = 2 * NSTATE
@@ -405,8 +406,9 @@
 
 
 def front_kernel(gain_parts, planes, place_ref, hid_ref, ids_ref, *refs):
-    gains, smalls, blocks = refs[:1], refs[1 : 1 + planes], refs[1 + planes : 1 + 2 * planes]
-    normed_ref, inner_ref, conv_ref, proj_ref, mask_ref, small_ref, rest_ref, gain_ref, weights = refs[1 + 2 * planes :]
+    gains = refs[:1]
+    smalls, blocks = ([ref.at[k] for k in range(planes)] for ref in refs[1:3])
+    normed_ref, inner_ref, conv_ref, proj_ref, mask_ref, small_ref, rest_ref, gain_ref, weights = refs[3:]
     put_blocks(place_ref, blocks, weights)
     put_blocks(place_ref, smalls, small_ref)
 
@@ -477,19 +479,18 @@
 
 def front(place, hidden_all, ids, gains, small_blocks, inner_blocks):
     seqs, length, model = hidden_all.shape
-    planes = len(inner_blocks)
-    width = inner_blocks[0].shape[1]
+    planes, _, width = inner_blocks.shape
     packed = TOKENS + BC_ROWS
 
     def kernel(*refs):
         front_kernel(gains.shape[0], planes, *refs)
 
-    columns = small_blocks[0].shape[1]
+    columns = small_blocks.shape[2]
     return per_sequence(
         kernel,
         place,
         [hidden_all, ids],
-        [gains, *small_blocks, *inner_blocks],
+        [gains, small_blocks, inner_blocks],
         [
             ((seqs, length, model), bf16, "every"),
             ((seqs, length, width), f32, "every"),
@@ -604,8 +605,8 @@
     planes = len(blocks)
 
     def kernel(place_ref, ginner_ref, ggate_ref, hid_ref, *refs):
-        inners, gates = refs[:planes], refs[planes : 2 * planes]
-        own_ref, other_ref, ggain_ref, w_inner, w_gate = refs[2 * planes :]
+        inners, gates = [refs[0].at[k] for k in range(planes)], refs[1 : 1 + planes]
+        own_ref, other_ref, ggain_ref, w_inner, w_gate = refs[1 + planes :]
         put_blocks(place_ref, inners, w_inner)
         put_combined(place_ref, gates, w_gate, None)
 
@@ -621,7 +622,7 @@
         kernel,
         place,
         [grad_inner, grad_gate, hidden_all],
-        [*inner_blocks, *blocks],
+        [inner_blocks, *blocks],
         [
             ((seqs // 2, length, model), bf16, "own"),
             ((seqs // 2, length, model), bf16, "other"),
@@ -814,7 +815,7 @@
             pltpu.SemaphoreType.DMA((2,)),
         ],
         compiler_params=pltpu.CompilerParams(
-            collective_id=1, has_side_effects=True, vmem_limit_bytes=24 * 2**20
+            collective_id=1, has_side_effects=True, vmem_limit_bytes=MOST
         ),
         cost_estimate=pl.CostEstimate(flops=0, bytes_accessed=100 * 10**6, transcendentals=0),
         name="gather_first",
@@ -1039,7 +1040,7 @@
             pltpu.SemaphoreType.DMA((6,)),
         ],
         compiler_params=pltpu.CompilerParams(
-            collective_id=4, has_side_effects=True, vmem_limit_bytes=40 * 2**20
+            collective_id=4, has_side_effects=True, vmem_limit_bytes=MOST
         ),
         cost_estimate=pl.CostEstimate(flops=0, bytes_accessed=150 * 10**6, transcendentals=0),
         name="finish",
@@ -1160,8 +1161,7 @@
     return (first_new, second_new, master - rate * update)
 
 
-def adam_in_kernel(place_ref, *refs):
-    reps = (len(refs) - 9) // 2
+def adam_in_kernel(reps, place_ref, *refs):
     pieces = refs[: 2 * reps]
     master_ref, first_ref, second_ref = refs[2 * reps : 2 * reps + 3]
     first_out, second_out, master_out = refs[-3:]
@@ -1190,22 +1190,18 @@
     wide = pl.BlockSpec((rows, block), lambda i, p: (0, half * steps + i))
     thin = [pl.BlockSpec((rows, sub), functools.partial(lambda at, i, p: (at, i), at)) for _, at in pieces]
     anywhere = pl.BlockSpec(memory_space=pl.ANY)
-    if earlier is None:
-        earlier = (master, first, second)
-        aliases = {}
-    else:
-        aliases = {1 + 2 * reps + 3 + i: i for i in range(3)}
+    aliases = {1 + 2 * reps + 3 + i: i for i in range(len(earlier))}
     return pl.pallas_call(
-        adam_in_kernel,
+        functools.partial(adam_in_kernel, reps),
         grid_spec=pltpu.PrefetchScalarGridSpec(
             num_scalar_prefetch=1,
             grid=(steps,),
-            in_specs=thin + [wide] * 3 + [anywhere] * 3,
+            in_specs=thin + [wide] * 3 + [anywhere] * len(earlier),
             out_specs=[wide] * 3,
         ),
         out_shape=[jax.ShapeDtypeStruct(master.shape, f32)] * 3,
         input_output_aliases=aliases,
-        compiler_params=pltpu.CompilerParams(vmem_limit_bytes=32 * 2**20),
+        compiler_params=pltpu.CompilerParams(vmem_limit_bytes=MOST),
         cost_estimate=pl.CostEstimate(flops=10 * master.size, bytes_accessed=13 * master.size, transcendentals=master.size),
         name="adam_in",
     )(place, *[array for array, _ in pieces], master, first, second, *earlier)
@@ -1214,34 +1210,35 @@
 def adam_out_kernel(place_ref, *refs):
     reps = len(refs) - 6
     master_ref, first_ref, second_ref, first_out, second_out, master_out = refs[reps:]
+    sub, wide = master_ref.shape[0], refs[0].shape[1]
     for k in range(reps):
 
         @pl.when(pl.program_id(0) == k)
         def _():
-            first_out[...], second_out[...], master_out[...] = adam_step(
-                master_ref[...], first_ref[...], second_ref[...], refs[k][...].astype(f32),
-                learn_rates[3], with_decay[3],
-            )
+            for j in range(master_ref.shape[1] // wide):
+                lanes = pl.ds(j * wide, wide)
+                first_out[:, lanes], second_out[:, lanes], master_out[:, lanes] = adam_step(
+                    master_ref[:, lanes], first_ref[:, lanes], second_ref[:, lanes],
+                    refs[k][pl.ds(j * sub, sub), :].astype(f32), learn_rates[3], with_decay[3],
+                )
 
 
 def adam_out(place, pieces, master, first, second):
     rows, columns = master.shape
     reps = len(pieces)
-    sub = rows // reps
     high, wide = pieces[0].shape
-    first_block = high // 2 // sub
-    mine = pl.BlockSpec((sub, wide), lambda k, j, p: (p[0] ^ k, j))
-    piece = pl.BlockSpec((sub, wide), lambda k, j, p: (first_block + j, 0))
+    mine = pl.BlockSpec((rows // reps, columns), lambda k, p: (p[0] ^ k, 0))
+    piece = pl.BlockSpec((high // 2, wide), lambda k, p: (1, 0))
     return pl.pallas_call(
         adam_out_kernel,
         grid_spec=pltpu.PrefetchScalarGridSpec(
             num_scalar_prefetch=1,
-            grid=(reps, columns // wide),
+            grid=(reps,),
             in_specs=[piece] * reps + [mine] * 3,
             out_specs=[mine] * 3,
         ),
         out_shape=[jax.ShapeDtypeStruct(master.shape, f32)] * 3,
-        compiler_params=pltpu.CompilerParams(vmem_limit_bytes=32 * 2**20),
+        compiler_params=pltpu.CompilerParams(vmem_limit_bytes=MOST),
         cost_estimate=pl.CostEstimate(flops=10 * master.size, bytes_accessed=26 * master.size, transcendentals=master.size),
         name="adam_out",
     )(place, *pieces, master, first, second)
@@ -1348,18 +1345,16 @@
     own_gain = lax.reduce_precision(gain_master, 8, 7)[None]
     own_ids = segments.astype(f32)
     if fast:
-        hidden_all, upstream, inner_blocks, gate_pair, small_parts, gains, ids = gather_first(
+        hidden_all, upstream, inner_blocks, gate_pair, small_blocks, gains, ids = gather_first(
             own_hidden, cotangent[0], in_own, in_other, small, own_gain, own_ids
         )
-        inner_blocks = [inner_blocks[k] for k in range(planes)]
-        small_blocks = [small_parts[k] for k in range(planes)]
     else:
         ids = net.gather_plane(own_ids).reshape(seqs, 1, length)
         gain_pair = net.pair_rows(own_gain[0], net.core(own_gain[0])).reshape(2 * in_rows)
         gains = net.gather_z(gain_pair).reshape(1, 1, model)
-        small_blocks = net.gather_z_list(small)
+        small_blocks = jnp.stack(net.gather_z_list(small))
         in_pair = net.pair_rows(in_own, net.core(in_other)).reshape(2 * in_rows, 2 * width)
-        inner_blocks = net.gather_z_list(in_pair[:, :width])
+        inner_blocks = jnp.stack(net.gather_z_list(in_pair[:, :width]))
         hidden_all = net.gather_plane(own_hidden)
         upstream = net.gather_plane(cotangent[0])
         gate_pair = in_pair[:, width:]
@@ -1444,7 +1439,7 @@
 
     if tiled:
         gate_pieces = [(pieces[k], e) for e in range(2) for k in range(reps)]
-        in_new = adam_in(place, 1, gate_pieces, in_master, in_first, in_second, None)
+        in_new = adam_in(place, 1, gate_pieces, in_master, in_first, in_second, ())
         in_new = adam_in(place, 0, inner_pieces, in_master, in_first, in_second, in_new)
     else:
         gate_pieces = [pieces[k][e * in_rows : (e + 1) * in_rows] for e in range(2) for k in range(reps)]

time: 617 us -> 603 us (0.977)
  local copies, waits for them, and re-layouts: 67.2 us -> 40.9 us
  Pallas kernels: 451 us -> 459 us
    unnamed x127 -> x89, local copies, waits for them, and re-layouts: 38 us -> 14.8 us
  transfers between devices with their start and end apart: 14 -> 14, of which waited for: 0 -> 0; matrix products, arithmetic and copies ran while one was open for 14% -> 14% of each run, Pallas kernels for 56% -> 58%
where the time goes in v4:
time: 603 us; the launch traced here: 593 us
  Pallas kernels  459 us (76%)
  local copies, waits for them, and re-layouts  40.9 us (7%)
  matrix products  32.7 us (5%)
  other arithmetic  32.6 us (5%)
  starting transfers between devices  26.7 us (4%)
    pallas_call x1, Pallas kernels, scan_backward(): pl.pallas_call(scan_bwd_kernel, grid=(chunks,), in_specs=ins + [start_spe...  110 us
    pallas_call x1, Pallas kernels, gather_first(): pl.pallas_call(gather_first_kernel, in_specs=[vmem] * 7, out_specs=[anywh...  81.5 us
    pallas_call x4, Pallas kernels, per_sequence(): pl.pallas_call(kernel, grid_spec=pltpu.PrefetchScalarGridSpec(num_scalar_...  77.3 us
    pallas_call x1, Pallas kernels, finish(): pl.pallas_call(finish_kernel, in_specs=[anywhere] * 4, out_specs=[pl.Bloc...  73.1 us
    pallas_call x2, Pallas kernels, reduce_plane(): pl.pallas_call(reduce_plane_kernel, in_specs=[vmem], out_specs=[vmem, vme...  39.9 us
    pallas_call x1, Pallas kernels, scan_forward(): pl.pallas_call(scan_fwd_kernel, grid=(chunks,), in_specs=ins, out_specs=[...  33.7 us
    dot_general x5, matrix products, dot(): return lax.dot_general(a, b, (dims, ((), ())), preferred_element_type=f32)  32.7 us
    pallas_call x2, Pallas kernels, adam_in(): pl.pallas_call(functools.partial(adam_in_kernel, reps), grid_spec=pltpu.P...  24 us
  transfers between devices with their start and end apart: 14, of which 0 were waited for; matrix products, arithmetic and copies ran while one was open for 14% of the time, Pallas kernels for 58%

profile of v4, /device:TPU:0, one launch (start us, length us, event | category | flops | bytes accessed | tf_op | source)
XLA Modules:
  0.0 593.2 jit_solution(12801725194066478820)
XLA Ops:
  2.2 6.2 %slice_in.1 = bf16[2,256,1024]{2,1,0:T(8,128)(2,1)} custom-call(s32[3]{0:T(128)} %pad_add_fusion.place_ref.refs_0_, f32[256,8192]{1,0:T(8,128)} %refs_8_.3, f32[256,8192]{1,0:T(8,128)} %refs_8_.3), custom_call_target="tpu_custom_call" | custom-call | tf_op jit(solution)/shard_map/slice_in/pallas_call | solution.py:1259
  8.4 2.3 slice_bitcast_fusion
  15.8 81.5 %gather_first.1 = (bf16[8,256,2048]{2,1,0:T(8,128)(2,1)}, bf16[8,256,2048]{2,1,0:T(8,128)(2,1)}, bf16[4,512,512]{2,1,0:T(8,128)(2,1)}, bf16[512,512]{1,0:T(8,128...) custom-call(bf16[256,2048]{1,0:T(8,128)(2,1)} %bitcast.79, ...), custom_call_target="tpu_custom_call" | custom-call | bytes 100000000 | tf_op jit(solution)/shard_map/gather_first/pallas_call | solution.py:799
  100.5 2.4 collective-permute-start.2
  102.9 17.0 %front.1 = (bf16[8,256,2048]{2,1,0:T(8,128)(2,1)}, f32[8,256,512]{2,1,0:T(8,128)}, bf16[8,256,512]{2,1,0:T(8,128)(2,1)}, f32[8,320,128]{2,1,0:T(8,128)}, f32[8,2...) custom-call(s32[3]{0:T(128)} %pad_add_fusion.place_ref.refs_0_, ...), custom_call_target="tpu_custom_call" | custom-call | flops 4294967296 | bytes 40000000 | tf_op jit(solution)/shard_map/front/pallas_call | solution.py:452
  121.2 20.0 %reduce_plane.2 = (bf16[8,256,128]{2,1,0:T(8,128)(2,1)S(1)}, f32[8,64,128]{2,1,0:T(8,128)S(1)}) custom-call(f32[8,320,128]{2,1,0:T(8,128)S(1)} %copy-done.3), custom_call_target="tpu_custom_call" | custom-call | bytes 50000000 | tf_op jit(solution)/shard_map/reduce_plane/pallas_call | solution.py:860
  144.7 33.7 %scan_forward.1 = (f32[8,256,512]{2,1,0:T(8,128)}, f32[8,16,8,512]{3,2,1,0:T(8,128)}) custom-call(bf16[8,256,128]{2,1,0:T(8,128)(2,1)S(1)} %get-tuple-element.86.dt_ref, f32[8,256,8]{2,1,0:T(8,128)S(1)} %copy-done.4, bf16[8,256,512]{2,1,0:T(8,128)(2,1)} %get-tuple-element.88.conv_ref, f32[512,128]{1,0:T(8,128)S(1)} %bitcast.67, ...), custom_call_target="tpu_custom_call" | custom-call | flops 134217728 | bytes 100000000 | tf_op jit(solution)/shard_map/scan_forward/pallas_call | solution.py:281
  180.1 25.0 %middle.1 = (bf16[4,256,2048]{2,1,0:T(8,128)(2,1)}, bf16[4,256,2048]{2,1,0:T(8,128)(2,1)}, bf16[8,256,512]{2,1,0:T(8,128)(2,1)}, f32[8,256,512]{2,1,0:T(8,128)},...) custom-call(s32[3]{0:T(128)} %pad_add_fusion.place_ref.refs_0_, bf16[8,256,2048]{2,1,0:T(8,128)(2,1)} %get-tuple-element.83.normed_ref, ...), custom_call_target="tpu_custom_call" | custom-call | flops 12884901888 | bytes 40000000 | tf_op jit(solution)/shard_map/middle/pallas_call | solution.py:452
  205.5 9.9 %bitcast_convert_fusion.1 = bf16[512,2048]{1,0:T(8,128)(2,1)} fusion(bf16[8,256,512]{2,1,0:T(8,128)(2,1)} %get-tuple-element.99, bf16[8,256,2048]{2,1,0:T(8,128)(2,1)} %get-tuple-element.84.up_ref), kind=kOutput, calls=%fused_computation.3 | convolution fusion | flops 4296015872 | bytes 12582912 | tf_op jit(solution)/shard_map/dot_general | solution.py:45
  215.4 3.5 reshape_reshape.3
  220.5 8.4 %bitcast_convert_fusion.2 = bf16[2048,512]{1,0:T(8,128)(2,1)S(1)} fusion(bf16[8,256,2048]{2,1,0:T(8,128)(2,1)} %get-tuple-element.83.normed_ref, bf16[8,256,512]{2,1,0:T(8,128)(2,1)S(1)} %copy-done.41), kind=kOutput, calls=%fused_computation.4 | convolution fusion | flops 4296015872 | bytes 12582912 | tf_op jit(solution)/shard_map/dot_general | solution.py:45
  231.6 13.8 %collective-permute-start.6 = (bf16[1024,512]{1,0:T(8,128)(2,1)}, bf16[1024,512]{1,0:T(8,128)(2,1)S(1)}, u32[]{:S(2)}, u32[]{:S(2)}) collective-permute-start(bf16[1024,512]{1,0:T(8,128)(2,1)} %get-tuple-element.212), channel_id=1, source_target_pairs={{0,2},{1,3},{2,0},{3,1},{4,6},{5,7},{6,4},{7,5},{8,10},{9,11},{10,... | collective-permute-start | bytes 3145736 | tf_op jit(solution)/shard_map/ppermute | solution.py:1068
  245.5 2.4 collective-permute-start.8
  250.4 5.4 add_convert_fusion
  259.9 110.2 %scan_backward.1 = (f32[8,256,512]{2,1,0:T(8,128)}, bf16[8,256,512]{2,1,0:T(8,128)(2,1)}, f32[2560,128]{1,0:T(8,128)}, f32[16,8,512]{2,1,0:T(8,128)}, f32[8,512]{1,0:T(8,128)}) custom-call(bf16[8,256,128]{2,1,0:T(8,128)(2,1)} %copy-done.5, f32[8,256,8]{2,1,0:T(8,128)} %get-tuple-element.87.mask_ref, bf16[8,256,512]{2,1,0:T(8,128)(2,1)} %get-tuple-element.88.conv_ref, ...), custom_call_target="tpu_custom_call" | custom-call | flops 402653184 | bytes 300000000 | tf_op jit(solution)/shard_map/scan_backward/pallas_call | solution.py:310
  370.1 2.4 add_convert_fusion.2
  378.8 19.9 %reduce_plane.3 = (bf16[8,256,128]{2,1,0:T(8,128)(2,1)S(1)}, f32[8,64,128]{2,1,0:T(8,128)S(1)}) custom-call(f32[8,320,128]{2,1,0:T(8,128)S(1)} %bitcast.66), custom_call_target="tpu_custom_call" | custom-call | bytes 50000000 | tf_op jit(solution)/shard_map/reduce_plane/pallas_call | solution.py:860
  403.8 13.6 %back_conv.1 = (bf16[8,256,512]{2,1,0:T(8,128)(2,1)}, f32[5,8,512]{2,1,0:T(8,128)}, f32[32,512]{1,0:T(8,128)}) custom-call(s32[3]{0:T(128)} %pad_add_fusion.place_ref.refs_0_, f32[8,256,512]{2,1,0:T(8,128)} %get-tuple-element.103.gconv_ref, bf16[8,256,128]{2,1,0:T(8,128)(2,1)} %copy-done, f32[8,64,128]{2,1,0:T(8,128)} %copy-done.9, ...), custom_call_target="tpu_custom_call" | custom-call | flops 268435456 | bytes 40000000 | tf_op jit(solution)/shard_map/back_conv/pallas_call | solution.py:452
  417.4 9.9 %bitcast_convert_fusion.gin = bf16[2048,512]{1,0:T(8,128)(2,1)} fusion(bf16[8,256,2048]{2,1,0:T(8,128)(2,1)} %get-tuple-element.83.normed_ref, bf16[8,256,512]{2,1,0:T(8,128)(2,1)} %get-tuple-element.111.ginner_ref), kind=kOutput, calls=%fused_computation.2 | convolution fusion | flops 4296015872 | bytes 12582912 | tf_op jit(solution)/shard_map/dot_general | solution.py:45
  427.4 21.7 %back_normed.1 = (bf16[4,256,2048]{2,1,0:T(8,128)(2,1)}, bf16[4,256,2048]{2,1,0:T(8,128)(2,1)}, f32[8,2048]{1,0:T(8,128)}) custom-call(s32[3]{0:T(128)} %pad_add_fusion.place_ref.refs_0_, bf16[8,256,512]{2,1,0:T(8,128)(2,1)} %get-tuple-element.111.ginner_ref, bf16[8,256,512]{2,1,0:T(8,128)(2,1)} %get-tuple-element.98.ggate_ref, ...), custom_call_target="tpu_custom_call" | custom-call | flops 8589934592 | bytes 40000000 | tf_op jit(solution)/shard_map/back_normed/pallas_call | solution.py:452
  452.7 3.0 convolution_bitcast_fusion.1
  455.8 2.1 concatenate.20
  458.8 73.1 %finish.1 = (f32[256,2048]{1,0:T(8,128)}, bf16[8,256,512]{2,1,0:T(8,128)(2,1)}, f32[4,128,384]{2,1,0:T(8,128)}) custom-call(bf16[4,256,2048]{2,1,0:T(8,128)(2,1)} %get-tuple-element.112.part, bf16[4,256,2048]{2,1,0:T(8,128)(2,1)} %get-tuple-element.113.other_part, bf16[2048,512]{1,0:T(8,128)(2,1)} %bitcast_convert_fusion.gin, f32[512,384]{1,0:T(8,128)} %pad.9.small), custom_call_target="tpu_custom_call" | custom-call | bytes 150000000 | tf_op jit(solution)/shard_map/finish/pallas_call | solution.py:1011
  536.5 1.7 copy.147
  540.3 2.7 multiply_subtract_fusion.1
  543.1 2.2 multiply_subtract_fusion
  545.2 2.4 add_convert_fusion.1
  549.3 12.0 %adam_in.2 = (f32[256,8192]{1,0:T(8,128)}, f32[256,8192]{1,0:T(8,128)}, f32[256,8192]{1,0:T(8,128)}) custom-call(s32[3]{0:T(128)} %pad_add_fusion.place_ref.refs_0_, bf16[1024,512]{1,0:T(8,128)(2,1)} %copy-done.13, bf16[1024,512]{1,0:T(8,128)(2,1)} %copy-done.16, bf16[1024,512]{1,0:T(8,128)(2,1)} %collective-permute-done.11.refs_2_.refs_6_, ...), custom_call_target="tpu_custom_call" | custom-call | flops 20971520 | bytes 27262976 | tf_op jit(solution)/shard_map/adam_in/pallas_call | solution.py:1194
  561.3 12.1 %adam_in.3 = (f32[256,8192]{1,0:T(8,128)}, f32[256,8192]{1,0:T(8,128)}, f32[256,8192]{1,0:T(8,128)}) custom-call(s32[3]{0:T(128)} %pad_add_fusion.place_ref.refs_0_, bf16[2048,512]{1,0:T(8,128)(2,1)} %bitcast.69, bf16[2048,512]{1,0:T(8,128)(2,1)} %bitcast.70, ...), custom_call_target="tpu_custom_call", output_to_operand_aliasing={{0}: (12, {}), {1}: (13, {}), {2}: (14, {})} | custom-call | flops 20971520 | bytes 27262976 | tf_op jit(solution)/shard_map/adam_in/pallas_call | solution.py:1194
  574.1 2.9 fusion.6
  577.0 12.7 %adam_out.1 = (f32[512,2048]{1,0:T(8,128)}, f32[512,2048]{1,0:T(8,128)}, f32[512,2048]{1,0:T(8,128)}) custom-call(s32[3]{0:T(128)} %pad_add_fusion.place_ref.refs_0_, bf16[1024,512]{1,0:T(8,128)(2,1)} %copy-done.13, bf16[1024,512]{1,0:T(8,128)(2,1)} %copy-done.16, bf16[1024,512]{1,0:T(8,128)(2,1)} %collective-permute-done.11.refs_2_.refs_6_, ...), custom_call_target="tpu_custom_call" | custom-call | flops 10485760 | bytes 27262976 | tf_op jit(solution)/shard_map/adam_out/pallas_call | solution.py:1232
  590.3 2.7 add_convert_fusion.3
  (163 shorter events, 52.9 us)
Async XLA Ops:
  98.4 21.5 %copy-start.20 = (bf16[1024,512]{1,0:T(8,128)(2,1)}, bf16[1024,512]{1,0:T(8,128)(2,1)S(1)}, u32[]{:S(2)}) copy-start(bf16[1024,512]{1,0:T(8,128)(2,1)S(1)} %pad_maximum_fusion.1.refs_0_.refs_1_) | copy-start | bytes 3145732
  98.4 80.0 %collective-permute-start = (bf16[1024,512]{1,0:T(8,128)(2,1)S(1)}, bf16[1024,512]{1,0:T(8,128)(2,1)S(1)}, u32[]{:S(2)}, u32[]{:S(2)}) collective-permute-start(bf16[1024,512]{1,0:T(8,128)(2,1)S(1)} %pad_maximum_fusion.1.refs_0_.refs_1_), channel_id=1, source_target_pairs={{0,2},{1,3},{2,0},{3,1},{4,6},{5,7},{6,4},{7,5},{8,10},{9,11},{10,... | collective-permute-start | bytes 3145736 | tf_op jit(solution)/shard_map/ppermute | solution.py:1068
  99.1 79.4 %collective-permute-start.1 = (bf16[1024,512]{1,0:T(8,128)(2,1)S(1)}, bf16[1024,512]{1,0:T(8,128)(2,1)S(1)}, u32[]{:S(2)}, u32[]{:S(2)}) collective-permute-start(bf16[1024,512]{1,0:T(8,128)(2,1)S(1)} %pad_maximum_fusion.1.refs_0_.refs_1_), channel_id=1, source_target_pairs={{0,4},{1,5},{2,6},{3,7},{4,0},{5,1},{6,2},{7,3},{8,12},{9,13},{10,... | collective-permute-start | bytes 3145736 | tf_op jit(solution)/shard_map/ppermute | solution.py:1068
  100.5 77.9 %collective-permute-start.2 = (bf16[1024,512]{1,0:T(8,128)(2,1)S(1)}, bf16[1024,512]{1,0:T(8,128)(2,1)S(1)}, u32[]{:S(2)}, u32[]{:S(2)}) collective-permute-start(bf16[1024,512]{1,0:T(8,128)(2,1)S(1)} %pad_maximum_fusion.1.refs_0_.refs_1_), channel_id=1, source_target_pairs={{0,6},{1,7},{2,4},{3,5},{4,2},{5,3},{6,0},{7,1},{8,14},{9,15},{10,... | collective-permute-start | bytes 3145736 | tf_op jit(solution)/shard_map/ppermute | solution.py:1068
  141.2 37.2 %copy-start.5 = (bf16[8,256,128]{2,1,0:T(8,128)(2,1)}, bf16[8,256,128]{2,1,0:T(8,128)(2,1)S(1)}, u32[]{:S(2)}) copy-start(bf16[8,256,128]{2,1,0:T(8,128)(2,1)S(1)} %get-tuple-element.86.dt_ref) | copy-start | bytes 1572868
  141.2 37.2 %copy-start.10 = (f32[8,64,128]{2,1,0:T(8,128)}, f32[8,64,128]{2,1,0:T(8,128)S(1)}, u32[]{:S(2)}) copy-start(f32[8,64,128]{2,1,0:T(8,128)S(1)} %get-tuple-element.89) | copy-start | bytes 786436
  205.1 45.3 %collective-permute-start.3 = (bf16[4,256,2048]{2,1,0:T(8,128)(2,1)}, bf16[4,256,2048]{2,1,0:T(8,128)(2,1)}, u32[]{:S(2)}, u32[]{:S(2)}) collective-permute-start(bf16[4,256,2048]{2,1,0:T(8,128)(2,1)} %get-tuple-element.95), channel_id=1, source_target_pairs={{0,1},{1,0},{2,3},{3,2},{4,5},{5,4},{6,7},{7,6},{8,9},{9,8},{10,11... | collective-permute-start | bytes 12582920 | tf_op jit(solution)/shard_map/ppermute | solution.py:1062
  229.3 20.2 %copy-start.32 = (f32[8,512]{1,0:T(8,128)S(1)}, f32[8,512]{1,0:T(8,128)}, u32[]{:S(2)}) copy-start(f32[8,512]{1,0:T(8,128)} %get-tuple-element.119) | copy-start | bytes 49156
  231.6 138.4 %collective-permute-start.6 = (bf16[1024,512]{1,0:T(8,128)(2,1)}, bf16[1024,512]{1,0:T(8,128)(2,1)S(1)}, u32[]{:S(2)}, u32[]{:S(2)}) collective-permute-start(bf16[1024,512]{1,0:T(8,128)(2,1)} %get-tuple-element.212), channel_id=1, source_target_pairs={{0,2},{1,3},{2,0},{3,1},{4,6},{5,7},{6,4},{7,5},{8,10},{9,11},{10,... | collective-permute-start | bytes 3145736 | tf_op jit(solution)/shard_map/ppermute | solution.py:1068
  245.5 124.6 %collective-permute-start.7 = (bf16[1024,512]{1,0:T(8,128)(2,1)S(1)}, bf16[1024,512]{1,0:T(8,128)(2,1)}, u32[]{:S(2)}, u32[]{:S(2)}) collective-permute-start(bf16[1024,512]{1,0:T(8,128)(2,1)S(1)} %get-tuple-element.211), channel_id=1, source_target_pairs={{0,4},{1,5},{2,6},{3,7},{4,0},{5,1},{6,2},{7,3},{8,12},{9,13},{10,... | collective-permute-start | bytes 3145736 | tf_op jit(solution)/shard_map/ppermute | solution.py:1068
  245.5 124.6 %collective-permute-start.8 = (bf16[1024,512]{1,0:T(8,128)(2,1)S(1)}, bf16[1024,512]{1,0:T(8,128)(2,1)}, u32[]{:S(2)}, u32[]{:S(2)}) collective-permute-start(bf16[1024,512]{1,0:T(8,128)(2,1)S(1)} %get-tuple-element.210), channel_id=1, source_target_pairs={{0,6},{1,7},{2,4},{3,5},{4,2},{5,3},{6,0},{7,1},{8,14},{9,15},{10,... | collective-permute-start | bytes 3145736 | tf_op jit(solution)/shard_map/ppermute | solution.py:1068
  258.4 286.8 %collective-permute-start.4 = (bf16[2,256,2048]{2,1,0:T(8,128)(2,1)}, bf16[2,256,2048]{2,1,0:T(8,128)(2,1)}, u32[]{:S(2)}, u32[]{:S(2)}) collective-permute-start(bf16[2,256,2048]{2,1,0:T(8,128)(2,1)} %slice.65), channel_id=1, source_target_pairs={{0,16},{8,24},{16,0},{24,8},{1,17},{9,25},{17,1},{25,9},{2,18},{10... | collective-permute-start | bytes 6291464 | tf_op jit(solution)/shard_map/ppermute | solution.py:1059
  373.5 4.3 collective-permute-start.9
  378.8 38.6 %copy-start.13 = (bf16[1024,512]{1,0:T(8,128)(2,1)}, bf16[1024,512]{1,0:T(8,128)(2,1)S(1)}, u32[]{:S(2)}) copy-start(bf16[1024,512]{1,0:T(8,128)(2,1)S(1)} %pad_maximum_fusion.2.refs_0_.refs_4_) | copy-start | bytes 3145732
  400.3 58.5 %collective-permute-start.10 = (bf16[1024,512]{1,0:T(8,128)(2,1)S(1)}, bf16[1024,512]{1,0:T(8,128)(2,1)S(1)}, u32[]{:S(2)}, u32[]{:S(2)}) collective-permute-start(bf16[1024,512]{1,0:T(8,128)(2,1)S(1)} %pad_maximum_fusion.2.refs_0_.refs_4_), channel_id=1, source_target_pairs={{0,8},{8,0},{16,24},{24,16},{1,9},{9,1},{17,25},{25,17},{2,10},{10... | collective-permute-start | bytes 3145736 | tf_op jit(solution)/shard_map/ppermute | solution.py:1059
  400.9 57.9 %collective-permute-start.11 = (bf16[1024,512]{1,0:T(8,128)(2,1)S(1)}, bf16[1024,512]{1,0:T(8,128)(2,1)}, u32[]{:S(2)}, u32[]{:S(2)}) collective-permute-start(bf16[1024,512]{1,0:T(8,128)(2,1)S(1)} %pad_maximum_fusion.2.refs_0_.refs_4_), channel_id=1, source_target_pairs={{0,16},{8,24},{16,0},{24,8},{1,17},{9,25},{17,1},{25,9},{2,18},{10... | collective-permute-start | bytes 3145736 | tf_op jit(solution)/shard_map/ppermute | solution.py:1059
  402.3 56.5 %collective-permute-start.12 = (bf16[1024,512]{1,0:T(8,128)(2,1)S(1)}, bf16[1024,512]{1,0:T(8,128)(2,1)}, u32[]{:S(2)}, u32[]{:S(2)}) collective-permute-start(bf16[1024,512]{1,0:T(8,128)(2,1)S(1)} %pad_maximum_fusion.2.refs_0_.refs_4_), channel_id=1, source_target_pairs={{0,24},{8,16},{16,8},{24,0},{1,25},{9,17},{17,9},{25,1},{2,26},{10... | collective-permute-start | bytes 3145736 | tf_op jit(solution)/shard_map/ppermute | solution.py:1059
  417.4 9.9 %copy-start.27 = (f32[32,512]{1,0:T(8,128)S(1)}, f32[32,512]{1,0:T(8,128)}, u32[]{:S(2)}) copy-start(f32[32,512]{1,0:T(8,128)} %get-tuple-element.114) | copy-start | bytes 196612
  427.4 21.7 %copy-start.26 = (f32[5,8,512]{2,1,0:T(8,128)S(1)}, f32[5,8,512]{2,1,0:T(8,128)}, u32[]{:S(2)}) copy-start(f32[5,8,512]{2,1,0:T(8,128)} %get-tuple-element.116) | copy-start | bytes 245764
  427.4 25.3 %copy-start.1 = (bf16[8,256,128]{2,1,0:T(8,128)(2,1)S(1)}, bf16[8,256,128]{2,1,0:T(8,128)(2,1)}, u32[]{:S(2)}) copy-start(bf16[8,256,128]{2,1,0:T(8,128)(2,1)} %copy-done) | copy-start | bytes 1572868
  458.8 73.1 %copy-start.16 = (bf16[1024,512]{1,0:T(8,128)(2,1)}, bf16[1024,512]{1,0:T(8,128)(2,1)S(1)}, u32[]{:S(2)}) copy-start(bf16[1024,512]{1,0:T(8,128)(2,1)S(1)} %collective-permute-done.10.refs_1_.refs_5_) | copy-start | bytes 3145732
  533.3 6.2 %copy-start.15 = (bf16[1,256,2048]{2,1,0:T(8,128)(2,1)S(1)}, bf16[1,256,2048]{2,1,0:T(8,128)(2,1)}, u32[]{:S(2)}) copy-start(bf16[1,256,2048]{2,1,0:T(8,128)(2,1)} %param.21) | copy-start | bytes 3145732
  533.3 6.2 %copy-start.17 = (f32[256,2048]{1,0:T(8,128)S(1)}, f32[256,2048]{1,0:T(8,128)}, u32[]{:S(2)}) copy-start(f32[256,2048]{1,0:T(8,128)} %get-tuple-element.123) | copy-start | bytes 6291460
  533.3 6.2 %copy-start.31 = (f32[1,2048]{1,0:T(1,128)S(1)}, f32[1,2048]{1,0:T(1,128)}, u32[]{:S(2)}) copy-start(f32[1,2048]{1,0:T(1,128)} %get-tuple-element.124) | copy-start | bytes 24580
  539.4 50.2 %collective-permute-start.13 = (f32[256]{0:T(256)S(1)}, f32[256]{0:T(256)S(1)}, u32[]{:S(2)}, u32[]{:S(2)}) collective-permute-start(f32[256]{0:T(256)S(1)} %bitcast.99), channel_id=1, source_target_pairs={{0,1},{1,0},{2,3},{3,2},{4,5},{5,4},{6,7},{7,6},{8,9},{9,8},{10,11... | collective-permute-start | bytes 3080 | tf_op jit(solution)/shard_map/ppermute | solution.py:1062
  548.7 41.6 %collective-permute-start.5 = (bf16[1,256,2048]{2,1,0:T(8,128)(2,1)}, bf16[1,256,2048]{2,1,0:T(8,128)(2,1)}, u32[]{:S(2)}, u32[]{:S(2)}) collective-permute-start(bf16[1,256,2048]{2,1,0:T(8,128)(2,1)} %slice.67), channel_id=1, source_target_pairs={{0,8},{8,0},{16,24},{24,16},{1,9},{9,1},{17,25},{25,17},{2,10},{10... | collective-permute-start | bytes 3145736 | tf_op jit(solution)/shard_map/ppermute | solution.py:1059
  561.2 12.1 %copy-start.25 = (f32[512,23]{0,1:T(8,128)S(1)}, f32[512,23]{0,1:T(8,128)}, u32[]{:S(2)}) copy-start(f32[512,23]{0,1:T(8,128)} %copy.147) | copy-start | bytes 141316
  561.3 12.1 %copy-start.28 = (f32[512,23]{0,1:T(8,128)S(1)}, f32[512,23]{0,1:T(8,128)}, u32[]{:S(2)}) copy-start(f32[512,23]{0,1:T(8,128)} %param.36) | copy-start | bytes 141316
  561.3 12.1 %copy-start.29 = (f32[512,23]{0,1:T(8,128)S(1)}, f32[512,23]{0,1:T(8,128)}, u32[]{:S(2)}) copy-start(f32[512,23]{0,1:T(8,128)} %param.38) | copy-start | bytes 141316
  561.3 12.1 %copy-start.30 = (f32[512,23]{0,1:T(8,128)S(1)}, f32[512,23]{0,1:T(8,128)}, u32[]{:S(2)}) copy-start(f32[512,23]{0,1:T(8,128)} %param.37) | copy-start | bytes 141316
  577.0 12.7 %copy-start.36 = (f32[256]{0:T(256)S(1)}, f32[256]{0:T(256)}, u32[]{:S(2)}) copy-start(f32[256]{0:T(256)} %param.41) | copy-start | bytes 3076
  577.0 12.7 %copy-start.37 = (f32[256]{0:T(256)S(1)}, f32[256]{0:T(256)}, u32[]{:S(2)}) copy-start(f32[256]{0:T(256)} %param.40) | copy-start | bytes 3076
  (24 other events, 52.4 us)

commit v5 on v4

--- a/solution.py
+++ b/solution.py
@@ -982,7 +982,7 @@
         net.start(23 + k, pieces.at[4], pieces.at[4 + k], me.rep(k))
     local[3].wait()
     net.arrived(4, 5, 6)
-    small_total[...] = small_own[...] + small_in[0] + small_in[1] + small_in[2]
+    small_total[...] = small_own[...].astype(f32) + sum(small_in[k].astype(f32) for k in range(3))
     kept_small = pltpu.make_async_copy(small_total, small_all.at[0], local_sems.at[4])
     kept_small.start()
     for k in (1, 2, 3):
@@ -1032,8 +1032,8 @@
             pltpu.VMEM((rows, width), bf16),
             pltpu.VMEM((rows, width), bf16),
             pltpu.VMEM((rows, width), bf16),
-            pltpu.VMEM((small_rows, cols), f32),
-            pltpu.VMEM((3, small_rows, cols), f32),
+            pltpu.VMEM((small_rows, cols), bf16),
+            pltpu.VMEM((3, small_rows, cols), bf16),
             pltpu.VMEM((small_rows, cols), f32),
             pltpu.SemaphoreType.DMA((27,)),
             pltpu.SemaphoreType.DMA((27,)),
@@ -1244,9 +1244,9 @@
     )(place, *pieces, master, first, second)
 
 
-def slice_in_kernel(place_ref, own_ref, other_ref, out_ref):
-    out_ref[0] = own_ref[...].astype(bf16)
-    out_ref[1] = other_ref[...].astype(bf16)
+def slice_in_kernel(place_ref, own_ref, other_ref, own_out, other_out):
+    own_out[...] = own_ref[...].astype(bf16)
+    other_out[...] = other_ref[...].astype(bf16)
 
 
 def slice_in(place, master, reps):
@@ -1262,9 +1262,9 @@
             num_scalar_prefetch=1,
             grid=(blocks,),
             in_specs=[of_core(0), of_core(1)],
-            out_specs=pl.BlockSpec((2, rows, LANES), lambda b, p: (0, 0, b)),
+            out_specs=[pl.BlockSpec((rows, LANES), lambda b, p: (0, b))] * 2,
         ),
-        out_shape=jax.ShapeDtypeStruct((2, rows, blocks * LANES), bf16),
+        out_shape=[jax.ShapeDtypeStruct((rows, blocks * LANES), bf16)] * 2,
         name="slice_in",
     )(place, master, master)
 
@@ -1419,7 +1419,7 @@
     )
     if fast:
         grad_small = jnp.pad(grad_small, ((0, 0), (0, -grad_small.shape[1] % LANES)))
-        grad_small = after(grad_small, *pieces)
+        grad_small = after(grad_small.astype(bf16), *pieces)
         grad_normed, inner_pieces, small_sum = finish(back_own, back_other, gin_inner, grad_small)
         inner_pieces = [(inner_pieces.reshape(-1, width), e * reps + k) for e in range(2) for k in range(reps)]
         small_sum = net.order_reps(list(small_sum))

time: 603 us -> 597 us (0.990)
  local copies, waits for them, and re-layouts: 40.9 us -> 34.2 us
    unnamed x89 -> x87, local copies, waits for them, and re-layouts: 14.8 us -> 17 us
  transfers between devices with their start and end apart: 14 -> 14, of which waited for: 0 -> 0; matrix products, arithmetic and copies ran while one was open for 14% -> 13% of each run, Pallas kernels for 58% -> 59%
where the time goes in v5:
time: 597 us; the launch traced here: 587 us
  Pallas kernels  458 us (77%)
  local copies, waits for them, and re-layouts  34.2 us (6%)
  other arithmetic  33 us (6%)
  matrix products  32.8 us (5%)
  starting transfers between devices  27 us (5%)
    pallas_call x1, Pallas kernels, scan_backward(): pl.pallas_call(scan_bwd_kernel, grid=(chunks,), in_specs=ins + [start_spe...  110 us
    pallas_call x1, Pallas kernels, gather_first(): pl.pallas_call(gather_first_kernel, in_specs=[vmem] * 7, out_specs=[anywh...  81.5 us
    pallas_call x4, Pallas kernels, per_sequence(): pl.pallas_call(kernel, grid_spec=pltpu.PrefetchScalarGridSpec(num_scalar_...  77.3 us
    pallas_call x1, Pallas kernels, finish(): pl.pallas_call(finish_kernel, in_specs=[anywhere] * 4, out_specs=[pl.Bloc...  73.1 us
    pallas_call x2, Pallas kernels, reduce_plane(): pl.pallas_call(reduce_plane_kernel, in_specs=[vmem], out_specs=[vmem, vme...  39.4 us
    pallas_call x1, Pallas kernels, scan_forward(): pl.pallas_call(scan_fwd_kernel, grid=(chunks,), in_specs=ins, out_specs=[...  33.7 us
    dot_general x5, matrix products, dot(): return lax.dot_general(a, b, (dims, ((), ())), preferred_element_type=f32)  32.8 us
    pallas_call x2, Pallas kernels, adam_in(): pl.pallas_call(functools.partial(adam_in_kernel, reps), grid_spec=pltpu.P...  24 us
  transfers between devices with their start and end apart: 14, of which 0 were waited for; matrix products, arithmetic and copies ran while one was open for 13% of the time, Pallas kernels for 59%

profile of v5, /device:TPU:0, one launch (start us, length us, event | category | flops | bytes accessed | tf_op | source)
XLA Modules:
  0.0 586.9 jit_solution(10378446004215343503)
XLA Ops:
  8.0 6.2 %slice_in.1 = (bf16[256,1024]{1,0:T(8,128)(2,1)}, bf16[256,1024]{1,0:T(8,128)(2,1)}) custom-call(s32[3]{0:T(128)} %pad_add_fusion.place_ref.refs_0_, f32[256,8192]{1,0:T(8,128)} %refs_8_.3, f32[256,8192]{1,0:T(8,128)} %refs_8_.3), custom_call_target="tpu_custom_call" | custom-call | tf_op jit(solution)/shard_map/slice_in/pallas_call | solution.py:1259
  14.9 81.5 %gather_first.1 = (bf16[8,256,2048]{2,1,0:T(8,128)(2,1)}, bf16[8,256,2048]{2,1,0:T(8,128)(2,1)}, bf16[4,512,512]{2,1,0:T(8,128)(2,1)}, bf16[512,512]{1,0:T(8,128...) custom-call(bf16[256,2048]{1,0:T(8,128)(2,1)} %bitcast.76, ...), custom_call_target="tpu_custom_call" | custom-call | bytes 100000000 | tf_op jit(solution)/shard_map/gather_first/pallas_call | solution.py:799
  99.7 2.4 collective-permute-start.2
  102.0 17.0 %front.1 = (bf16[8,256,2048]{2,1,0:T(8,128)(2,1)}, f32[8,256,512]{2,1,0:T(8,128)}, bf16[8,256,512]{2,1,0:T(8,128)(2,1)}, f32[8,320,128]{2,1,0:T(8,128)}, f32[8,2...) custom-call(s32[3]{0:T(128)} %pad_add_fusion.place_ref.refs_0_, ...), custom_call_target="tpu_custom_call" | custom-call | flops 4294967296 | bytes 40000000 | tf_op jit(solution)/shard_map/front/pallas_call | solution.py:452
  120.4 20.0 %reduce_plane.2 = (bf16[8,256,128]{2,1,0:T(8,128)(2,1)S(1)}, f32[8,64,128]{2,1,0:T(8,128)S(1)}) custom-call(f32[8,320,128]{2,1,0:T(8,128)S(1)} %copy-done.3), custom_call_target="tpu_custom_call" | custom-call | bytes 50000000 | tf_op jit(solution)/shard_map/reduce_plane/pallas_call | solution.py:860
  143.8 33.7 %scan_forward.1 = (f32[8,256,512]{2,1,0:T(8,128)}, f32[8,16,8,512]{3,2,1,0:T(8,128)}) custom-call(bf16[8,256,128]{2,1,0:T(8,128)(2,1)S(1)} %get-tuple-element.90.dt_ref, f32[8,256,8]{2,1,0:T(8,128)S(1)} %copy-done.4, bf16[8,256,512]{2,1,0:T(8,128)(2,1)} %get-tuple-element.92.conv_ref, f32[512,128]{1,0:T(8,128)S(1)} %bitcast.64, ...), custom_call_target="tpu_custom_call" | custom-call | flops 134217728 | bytes 100000000 | tf_op jit(solution)/shard_map/scan_forward/pallas_call | solution.py:281
  179.2 25.0 %middle.1 = (bf16[4,256,2048]{2,1,0:T(8,128)(2,1)}, bf16[4,256,2048]{2,1,0:T(8,128)(2,1)}, bf16[8,256,512]{2,1,0:T(8,128)(2,1)}, f32[8,256,512]{2,1,0:T(8,128)},...) custom-call(s32[3]{0:T(128)} %pad_add_fusion.place_ref.refs_0_, bf16[8,256,2048]{2,1,0:T(8,128)(2,1)} %get-tuple-element.87.normed_ref, ...), custom_call_target="tpu_custom_call" | custom-call | flops 12884901888 | bytes 40000000 | tf_op jit(solution)/shard_map/middle/pallas_call | solution.py:452
  204.6 9.9 %bitcast_convert_fusion.1 = bf16[512,2048]{1,0:T(8,128)(2,1)} fusion(bf16[8,256,512]{2,1,0:T(8,128)(2,1)} %get-tuple-element.103, bf16[8,256,2048]{2,1,0:T(8,128)(2,1)} %get-tuple-element.88.up_ref), kind=kOutput, calls=%fused_computation.3 | convolution fusion | flops 4296015872 | bytes 12582912 | tf_op jit(solution)/shard_map/dot_general | solution.py:45
  214.5 3.3 reshape_reshape.3
  219.4 8.6 %bitcast_convert_fusion.2 = bf16[2048,512]{1,0:T(8,128)(2,1)S(1)} fusion(bf16[8,256,2048]{2,1,0:T(8,128)(2,1)} %get-tuple-element.87.normed_ref, bf16[8,256,512]{2,1,0:T(8,128)(2,1)S(1)} %copy-done.40), kind=kOutput, calls=%fused_computation.4 | convolution fusion | flops 4296015872 | bytes 12582912 | tf_op jit(solution)/shard_map/dot_general | solution.py:45
  230.8 13.8 %collective-permute-start.6 = (bf16[1024,512]{1,0:T(8,128)(2,1)}, bf16[1024,512]{1,0:T(8,128)(2,1)S(1)}, u32[]{:S(2)}, u32[]{:S(2)}) collective-permute-start(bf16[1024,512]{1,0:T(8,128)(2,1)} %get-tuple-element.216), channel_id=1, source_target_pairs={{0,2},{1,3},{2,0},{3,1},{4,6},{5,7},{6,4},{7,5},{8,10},{9,11},{10,... | collective-permute-start | bytes 3145736 | tf_op jit(solution)/shard_map/ppermute | solution.py:1068
  244.6 2.4 collective-permute-start.8
  248.1 5.4 add_convert_fusion
  253.5 1.6 slice.65
  257.6 110.1 %scan_backward.1 = (f32[8,256,512]{2,1,0:T(8,128)}, bf16[8,256,512]{2,1,0:T(8,128)(2,1)}, f32[2560,128]{1,0:T(8,128)}, f32[16,8,512]{2,1,0:T(8,128)}, f32[8,512]{1,0:T(8,128)}) custom-call(bf16[8,256,128]{2,1,0:T(8,128)(2,1)} %copy-done.5, f32[8,256,8]{2,1,0:T(8,128)} %get-tuple-element.91.mask_ref, bf16[8,256,512]{2,1,0:T(8,128)(2,1)} %get-tuple-element.92.conv_ref, ...), custom_call_target="tpu_custom_call" | custom-call | flops 402653184 | bytes 300000000 | tf_op jit(solution)/shard_map/scan_backward/pallas_call | solution.py:310
  367.8 2.4 add_convert_fusion.2
  375.6 19.5 %reduce_plane.3 = (bf16[8,256,128]{2,1,0:T(8,128)(2,1)S(1)}, f32[8,64,128]{2,1,0:T(8,128)S(1)}) custom-call(f32[8,320,128]{2,1,0:T(8,128)S(1)} %bitcast.63), custom_call_target="tpu_custom_call" | custom-call | bytes 50000000 | tf_op jit(solution)/shard_map/reduce_plane/pallas_call | solution.py:860
  400.1 13.6 %back_conv.1 = (bf16[8,256,512]{2,1,0:T(8,128)(2,1)}, f32[5,8,512]{2,1,0:T(8,128)}, f32[32,512]{1,0:T(8,128)}) custom-call(s32[3]{0:T(128)} %pad_add_fusion.place_ref.refs_0_, f32[8,256,512]{2,1,0:T(8,128)} %get-tuple-element.107.gconv_ref, bf16[8,256,128]{2,1,0:T(8,128)(2,1)} %copy-done, f32[8,64,128]{2,1,0:T(8,128)} %copy-done.9, ...), custom_call_target="tpu_custom_call" | custom-call | flops 268435456 | bytes 40000000 | tf_op jit(solution)/shard_map/back_conv/pallas_call | solution.py:452
  413.7 9.9 %bitcast_convert_fusion.gin = bf16[2048,512]{1,0:T(8,128)(2,1)} fusion(bf16[8,256,2048]{2,1,0:T(8,128)(2,1)} %get-tuple-element.87.normed_ref, bf16[8,256,512]{2,1,0:T(8,128)(2,1)} %get-tuple-element.115.ginner_ref), kind=kOutput, calls=%fused_computation.2 | convolution fusion | flops 4296015872 | bytes 12582912 | tf_op jit(solution)/shard_map/dot_general | solution.py:45
  423.5 21.7 %back_normed.1 = (bf16[4,256,2048]{2,1,0:T(8,128)(2,1)}, bf16[4,256,2048]{2,1,0:T(8,128)(2,1)}, f32[8,2048]{1,0:T(8,128)}) custom-call(s32[3]{0:T(128)} %pad_add_fusion.place_ref.refs_0_, bf16[8,256,512]{2,1,0:T(8,128)(2,1)} %get-tuple-element.115.ginner_ref, bf16[8,256,512]{2,1,0:T(8,128)(2,1)} %get-tuple-element.102.ggate_ref, ...), custom_call_target="tpu_custom_call" | custom-call | flops 8589934592 | bytes 40000000 | tf_op jit(solution)/shard_map/back_normed/pallas_call | solution.py:452
  446.9 3.0 fusion.6
  449.9 1.6 concatenate.21
  452.3 73.1 %finish.1 = (f32[256,2048]{1,0:T(8,128)}, bf16[8,256,512]{2,1,0:T(8,128)(2,1)}, f32[4,128,384]{2,1,0:T(8,128)}) custom-call(bf16[4,256,2048]{2,1,0:T(8,128)(2,1)} %get-tuple-element.116.part, bf16[4,256,2048]{2,1,0:T(8,128)(2,1)} %get-tuple-element.117.other_part, bf16[2048,512]{1,0:T(8,128)(2,1)} %bitcast_convert_fusion.gin, bf16[512,384]{1,0:T(8,128)(2,1)} %pad.10.small), custom_call_target="tpu_custom_call" | custom-call | bytes 150000000 | tf_op jit(solution)/shard_map/finish/pallas_call | solution.py:1011
  529.9 1.7 copy.147
  533.8 2.7 multiply_subtract_fusion.1
  536.5 2.2 multiply_subtract_fusion
  538.7 2.4 add_convert_fusion.1
  543.0 12.0 %adam_in.2 = (f32[256,8192]{1,0:T(8,128)}, f32[256,8192]{1,0:T(8,128)}, f32[256,8192]{1,0:T(8,128)}) custom-call(s32[3]{0:T(128)} %pad_add_fusion.place_ref.refs_0_, bf16[1024,512]{1,0:T(8,128)(2,1)} %copy-done.13, bf16[1024,512]{1,0:T(8,128)(2,1)} %copy-done.16, bf16[1024,512]{1,0:T(8,128)(2,1)} %collective-permute-done.11.refs_2_.refs_6_, ...), custom_call_target="tpu_custom_call" | custom-call | flops 20971520 | bytes 27262976 | tf_op jit(solution)/shard_map/adam_in/pallas_call | solution.py:1194
  555.0 12.1 %adam_in.3 = (f32[256,8192]{1,0:T(8,128)}, f32[256,8192]{1,0:T(8,128)}, f32[256,8192]{1,0:T(8,128)}) custom-call(s32[3]{0:T(128)} %pad_add_fusion.place_ref.refs_0_, bf16[2048,512]{1,0:T(8,128)(2,1)} %bitcast.66, bf16[2048,512]{1,0:T(8,128)(2,1)} %bitcast.67, ...), custom_call_target="tpu_custom_call", output_to_operand_aliasing={{0}: (12, {}), {1}: (13, {}), {2}: (14, {})} | custom-call | flops 20971520 | bytes 27262976 | tf_op jit(solution)/shard_map/adam_in/pallas_call | solution.py:1194
  567.8 2.9 fusion.8
  570.6 12.7 %adam_out.1 = (f32[512,2048]{1,0:T(8,128)}, f32[512,2048]{1,0:T(8,128)}, f32[512,2048]{1,0:T(8,128)}) custom-call(s32[3]{0:T(128)} %pad_add_fusion.place_ref.refs_0_, bf16[1024,512]{1,0:T(8,128)(2,1)} %copy-done.13, bf16[1024,512]{1,0:T(8,128)(2,1)} %copy-done.16, bf16[1024,512]{1,0:T(8,128)(2,1)} %collective-permute-done.11.refs_2_.refs_6_, ...), custom_call_target="tpu_custom_call" | custom-call | flops 10485760 | bytes 27262976 | tf_op jit(solution)/shard_map/adam_out/pallas_call | solution.py:1232
  583.9 2.7 add_convert_fusion.3
  (161 shorter events, 48.3 us)
Async XLA Ops:
  97.6 21.5 %copy-start.20 = (bf16[1024,512]{1,0:T(8,128)(2,1)}, bf16[1024,512]{1,0:T(8,128)(2,1)S(1)}, u32[]{:S(2)}) copy-start(bf16[1024,512]{1,0:T(8,128)(2,1)S(1)} %pad_maximum_fusion.1.refs_0_.refs_1_) | copy-start | bytes 3145732
  97.6 80.0 %collective-permute-start = (bf16[1024,512]{1,0:T(8,128)(2,1)S(1)}, bf16[1024,512]{1,0:T(8,128)(2,1)S(1)}, u32[]{:S(2)}, u32[]{:S(2)}) collective-permute-start(bf16[1024,512]{1,0:T(8,128)(2,1)S(1)} %pad_maximum_fusion.1.refs_0_.refs_1_), channel_id=1, source_target_pairs={{0,2},{1,3},{2,0},{3,1},{4,6},{5,7},{6,4},{7,5},{8,10},{9,11},{10,... | collective-permute-start | bytes 3145736 | tf_op jit(solution)/shard_map/ppermute | solution.py:1068
  98.2 79.4 %collective-permute-start.1 = (bf16[1024,512]{1,0:T(8,128)(2,1)S(1)}, bf16[1024,512]{1,0:T(8,128)(2,1)S(1)}, u32[]{:S(2)}, u32[]{:S(2)}) collective-permute-start(bf16[1024,512]{1,0:T(8,128)(2,1)S(1)} %pad_maximum_fusion.1.refs_0_.refs_1_), channel_id=1, source_target_pairs={{0,4},{1,5},{2,6},{3,7},{4,0},{5,1},{6,2},{7,3},{8,12},{9,13},{10,... | collective-permute-start | bytes 3145736 | tf_op jit(solution)/shard_map/ppermute | solution.py:1068
  99.7 77.9 %collective-permute-start.2 = (bf16[1024,512]{1,0:T(8,128)(2,1)S(1)}, bf16[1024,512]{1,0:T(8,128)(2,1)S(1)}, u32[]{:S(2)}, u32[]{:S(2)}) collective-permute-start(bf16[1024,512]{1,0:T(8,128)(2,1)S(1)} %pad_maximum_fusion.1.refs_0_.refs_1_), channel_id=1, source_target_pairs={{0,6},{1,7},{2,4},{3,5},{4,2},{5,3},{6,0},{7,1},{8,14},{9,15},{10,... | collective-permute-start | bytes 3145736 | tf_op jit(solution)/shard_map/ppermute | solution.py:1068
  140.3 37.2 %copy-start.5 = (bf16[8,256,128]{2,1,0:T(8,128)(2,1)}, bf16[8,256,128]{2,1,0:T(8,128)(2,1)S(1)}, u32[]{:S(2)}) copy-start(bf16[8,256,128]{2,1,0:T(8,128)(2,1)S(1)} %get-tuple-element.90.dt_ref) | copy-start | bytes 1572868
  140.4 37.2 %copy-start.10 = (f32[8,64,128]{2,1,0:T(8,128)}, f32[8,64,128]{2,1,0:T(8,128)S(1)}, u32[]{:S(2)}) copy-start(f32[8,64,128]{2,1,0:T(8,128)S(1)} %get-tuple-element.93) | copy-start | bytes 786436
  204.2 43.9 %collective-permute-start.3 = (bf16[4,256,2048]{2,1,0:T(8,128)(2,1)}, bf16[4,256,2048]{2,1,0:T(8,128)(2,1)}, u32[]{:S(2)}, u32[]{:S(2)}) collective-permute-start(bf16[4,256,2048]{2,1,0:T(8,128)(2,1)} %get-tuple-element.99), channel_id=1, source_target_pairs={{0,1},{1,0},{2,3},{3,2},{4,5},{5,4},{6,7},{7,6},{8,9},{9,8},{10,11... | collective-permute-start | bytes 12582920 | tf_op jit(solution)/shard_map/ppermute | solution.py:1062
  228.4 19.5 %copy-start.32 = (f32[8,512]{1,0:T(8,128)S(1)}, f32[8,512]{1,0:T(8,128)}, u32[]{:S(2)}) copy-start(f32[8,512]{1,0:T(8,128)} %get-tuple-element.123) | copy-start | bytes 49156
  230.8 137.0 %collective-permute-start.6 = (bf16[1024,512]{1,0:T(8,128)(2,1)}, bf16[1024,512]{1,0:T(8,128)(2,1)S(1)}, u32[]{:S(2)}, u32[]{:S(2)}) collective-permute-start(bf16[1024,512]{1,0:T(8,128)(2,1)} %get-tuple-element.216), channel_id=1, source_target_pairs={{0,2},{1,3},{2,0},{3,1},{4,6},{5,7},{6,4},{7,5},{8,10},{9,11},{10,... | collective-permute-start | bytes 3145736 | tf_op jit(solution)/shard_map/ppermute | solution.py:1068
  244.6 123.2 %collective-permute-start.7 = (bf16[1024,512]{1,0:T(8,128)(2,1)S(1)}, bf16[1024,512]{1,0:T(8,128)(2,1)}, u32[]{:S(2)}, u32[]{:S(2)}) collective-permute-start(bf16[1024,512]{1,0:T(8,128)(2,1)S(1)} %get-tuple-element.215), channel_id=1, source_target_pairs={{0,4},{1,5},{2,6},{3,7},{4,0},{5,1},{6,2},{7,3},{8,12},{9,13},{10,... | collective-permute-start | bytes 3145736 | tf_op jit(solution)/shard_map/ppermute | solution.py:1068
  244.6 123.2 %collective-permute-start.8 = (bf16[1024,512]{1,0:T(8,128)(2,1)S(1)}, bf16[1024,512]{1,0:T(8,128)(2,1)}, u32[]{:S(2)}, u32[]{:S(2)}) collective-permute-start(bf16[1024,512]{1,0:T(8,128)(2,1)S(1)} %get-tuple-element.214), channel_id=1, source_target_pairs={{0,6},{1,7},{2,4},{3,5},{4,2},{5,3},{6,0},{7,1},{8,14},{9,15},{10,... | collective-permute-start | bytes 3145736 | tf_op jit(solution)/shard_map/ppermute | solution.py:1068
  256.2 282.5 %collective-permute-start.4 = (bf16[2,256,2048]{2,1,0:T(8,128)(2,1)}, bf16[2,256,2048]{2,1,0:T(8,128)(2,1)}, u32[]{:S(2)}, u32[]{:S(2)}) collective-permute-start(bf16[2,256,2048]{2,1,0:T(8,128)(2,1)} %slice.65), channel_id=1, source_target_pairs={{0,16},{8,24},{16,0},{24,8},{1,17},{9,25},{17,1},{25,9},{2,18},{10... | collective-permute-start | bytes 6291464 | tf_op jit(solution)/shard_map/ppermute | solution.py:1059
  370.4 3.4 collective-permute-start.9
  375.6 38.1 %copy-start.13 = (bf16[1024,512]{1,0:T(8,128)(2,1)}, bf16[1024,512]{1,0:T(8,128)(2,1)S(1)}, u32[]{:S(2)}) copy-start(bf16[1024,512]{1,0:T(8,128)(2,1)S(1)} %pad_maximum_fusion.2.refs_0_.refs_4_) | copy-start | bytes 3145732
  396.6 55.7 %collective-permute-start.10 = (bf16[1024,512]{1,0:T(8,128)(2,1)S(1)}, bf16[1024,512]{1,0:T(8,128)(2,1)S(1)}, u32[]{:S(2)}, u32[]{:S(2)}) collective-permute-start(bf16[1024,512]{1,0:T(8,128)(2,1)S(1)} %pad_maximum_fusion.2.refs_0_.refs_4_), channel_id=1, source_target_pairs={{0,8},{8,0},{16,24},{24,16},{1,9},{9,1},{17,25},{25,17},{2,10},{10... | collective-permute-start | bytes 3145736 | tf_op jit(solution)/shard_map/ppermute | solution.py:1059
  397.4 54.9 %collective-permute-start.11 = (bf16[1024,512]{1,0:T(8,128)(2,1)S(1)}, bf16[1024,512]{1,0:T(8,128)(2,1)}, u32[]{:S(2)}, u32[]{:S(2)}) collective-permute-start(bf16[1024,512]{1,0:T(8,128)(2,1)S(1)} %pad_maximum_fusion.2.refs_0_.refs_4_), channel_id=1, source_target_pairs={{0,16},{8,24},{16,0},{24,8},{1,17},{9,25},{17,1},{25,9},{2,18},{10... | collective-permute-start | bytes 3145736 | tf_op jit(solution)/shard_map/ppermute | solution.py:1059
  398.6 53.6 %collective-permute-start.12 = (bf16[1024,512]{1,0:T(8,128)(2,1)S(1)}, bf16[1024,512]{1,0:T(8,128)(2,1)}, u32[]{:S(2)}, u32[]{:S(2)}) collective-permute-start(bf16[1024,512]{1,0:T(8,128)(2,1)S(1)} %pad_maximum_fusion.2.refs_0_.refs_4_), channel_id=1, source_target_pairs={{0,24},{8,16},{16,8},{24,0},{1,25},{9,17},{17,9},{25,1},{2,26},{10... | collective-permute-start | bytes 3145736 | tf_op jit(solution)/shard_map/ppermute | solution.py:1059
  423.5 21.7 %copy-start.26 = (f32[5,8,512]{2,1,0:T(8,128)S(1)}, f32[5,8,512]{2,1,0:T(8,128)}, u32[]{:S(2)}) copy-start(f32[5,8,512]{2,1,0:T(8,128)} %get-tuple-element.120) | copy-start | bytes 245764
  423.5 21.7 %copy-start.27 = (f32[32,512]{1,0:T(8,128)S(1)}, f32[32,512]{1,0:T(8,128)}, u32[]{:S(2)}) copy-start(f32[32,512]{1,0:T(8,128)} %get-tuple-element.118) | copy-start | bytes 196612
  423.5 23.4 %copy-start.1 = (bf16[8,256,128]{2,1,0:T(8,128)(2,1)S(1)}, bf16[8,256,128]{2,1,0:T(8,128)(2,1)}, u32[]{:S(2)}) copy-start(bf16[8,256,128]{2,1,0:T(8,128)(2,1)} %copy-done) | copy-start | bytes 1572868
  452.3 73.2 %copy-start.16 = (bf16[1024,512]{1,0:T(8,128)(2,1)}, bf16[1024,512]{1,0:T(8,128)(2,1)S(1)}, u32[]{:S(2)}) copy-start(bf16[1024,512]{1,0:T(8,128)(2,1)S(1)} %collective-permute-done.10.refs_1_.refs_5_) | copy-start | bytes 3145732
  526.7 6.2 %copy-start.15 = (bf16[1,256,2048]{2,1,0:T(8,128)(2,1)S(1)}, bf16[1,256,2048]{2,1,0:T(8,128)(2,1)}, u32[]{:S(2)}) copy-start(bf16[1,256,2048]{2,1,0:T(8,128)(2,1)} %param.21) | copy-start | bytes 3145732
  526.8 6.2 %copy-start.17 = (f32[256,2048]{1,0:T(8,128)S(1)}, f32[256,2048]{1,0:T(8,128)}, u32[]{:S(2)}) copy-start(f32[256,2048]{1,0:T(8,128)} %get-tuple-element.127) | copy-start | bytes 6291460
  532.9 50.4 %collective-permute-start.13 = (f32[256]{0:T(256)S(1)}, f32[256]{0:T(256)S(1)}, u32[]{:S(2)}, u32[]{:S(2)}) collective-permute-start(f32[256]{0:T(256)S(1)} %bitcast.93), channel_id=1, source_target_pairs={{0,1},{1,0},{2,3},{3,2},{4,5},{5,4},{6,7},{7,6},{8,9},{9,8},{10,11... | collective-permute-start | bytes 3080 | tf_op jit(solution)/shard_map/ppermute | solution.py:1062
  542.2 41.8 %collective-permute-start.5 = (bf16[1,256,2048]{2,1,0:T(8,128)(2,1)}, bf16[1,256,2048]{2,1,0:T(8,128)(2,1)}, u32[]{:S(2)}, u32[]{:S(2)}) collective-permute-start(bf16[1,256,2048]{2,1,0:T(8,128)(2,1)} %slice.67), channel_id=1, source_target_pairs={{0,8},{8,0},{16,24},{24,16},{1,9},{9,1},{17,25},{25,17},{2,10},{10... | collective-permute-start | bytes 3145736 | tf_op jit(solution)/shard_map/ppermute | solution.py:1059
  554.9 12.1 %copy-start.25 = (f32[512,23]{0,1:T(8,128)S(1)}, f32[512,23]{0,1:T(8,128)}, u32[]{:S(2)}) copy-start(f32[512,23]{0,1:T(8,128)} %copy.147) | copy-start | bytes 141316
  554.9 12.1 %copy-start.28 = (f32[512,23]{0,1:T(8,128)S(1)}, f32[512,23]{0,1:T(8,128)}, u32[]{:S(2)}) copy-start(f32[512,23]{0,1:T(8,128)} %param.36) | copy-start | bytes 141316
  554.9 12.1 %copy-start.29 = (f32[512,23]{0,1:T(8,128)S(1)}, f32[512,23]{0,1:T(8,128)}, u32[]{:S(2)}) copy-start(f32[512,23]{0,1:T(8,128)} %param.38) | copy-start | bytes 141316
  554.9 12.1 %copy-start.30 = (f32[512,23]{0,1:T(8,128)S(1)}, f32[512,23]{0,1:T(8,128)}, u32[]{:S(2)}) copy-start(f32[512,23]{0,1:T(8,128)} %param.37) | copy-start | bytes 141316
  570.6 12.7 %copy-start.34 = (f32[256]{0:T(256)S(1)}, f32[256]{0:T(256)}, u32[]{:S(2)}) copy-start(f32[256]{0:T(256)} %param.39) | copy-start | bytes 3076
  570.6 12.7 %copy-start.35 = (f32[256]{0:T(256)S(1)}, f32[256]{0:T(256)}, u32[]{:S(2)}) copy-start(f32[256]{0:T(256)} %param.41) | copy-start | bytes 3076
  570.6 12.7 %copy-start.36 = (f32[256]{0:T(256)S(1)}, f32[256]{0:T(256)}, u32[]{:S(2)}) copy-start(f32[256]{0:T(256)} %param.40) | copy-start | bytes 3076
  (23 other events, 46.2 us)
